TPU v7x, 256 devices: a whole 4x4x8 slice. The times are simulated.
256 devices in a mesh: dp: 16 (over x, y), vocab: 16 (over z, core).
Axes of the slice: x: 4, y: 4, z: 8, core: 2. Of those that a mesh axis runs over, the one named last changes fastest.
Arguments:
- hidden: bfloat16 [16, 32, 3584], P('dp', None, 'vocab'), may hold values from -6 to 6
- kl_hidden: bfloat16 [16, 32, 3584], P('dp', None, 'vocab'), may hold values from -6 to 6
- head_weight: bfloat16 [256000, 3584], P(('dp', 'vocab')), may hold values from -0.3125 to 0.3125
- labels: int32 [16, 32], P('dp'), may hold values from 0 to 255999
- token_mask: int32 [16, 32], P('dp'), may hold values 0 or 1
- kl_pair: int32 [16], P('dp'), may hold values from 0 to 15, as said below
- desirable: int32 [16], P('dp'), may hold values 0 or 1
- ref_logps: float32 [16, 64], P('dp', 'vocab'), may hold values from -23 to -11
Outputs:
- token_logps: float32 [16, 64], P('dp', 'vocab')
- seq_losses: float32 [16], P('dp')
- loss: float32 [], replicated
Inputs may be any that keep to these rules, and one draw needn't show every extreme that they name: kl_pair is a permutation of the 16 sequences with kl_pair[s] != s.
All inputs are finite; a program needn't handle non-finite values. No bound on the sum of `token_mask` or of `desirable` on one device may be relied on, other than what follows from the above.
Results may differ from a plain program's by a relative error of at most 0.0003.
Values may be sent and summed in bfloat16 or wider, within the bound.
No kernel may reach another device: no remote copies, remote signals or barrier semaphores. Data moves between devices by JAX's collectives and lax.ppermute only.
A program may use at most 64 MiB of HBM per device.

v0:
```python
import functools

import jax
import jax.numpy as jnp
from jax import lax
from jax.sharding import Mesh
from jax.sharding import PartitionSpec as P

VOCAB = ("vocab_0", "vocab_1")
DP = ("dp_0", "dp_1")
DP_VOCAB = ("dp_0", "dp_1", "vocab_0", "vocab_1")


kto_beta = 0.1
desirable_weight = 1.0
undesirable_weight = 1.33


def laid_out(parts, dim):
    shape = list(parts.shape[1:])
    shape[dim] *= parts.shape[0]
    return jnp.moveaxis(parts, 0, dim).reshape(shape)


def work_in_pieces(array, axis, dim, apply, out_dim):
    size, rows = (lax.axis_size(axis), array.shape[dim])
    count = 2 if rows % 2 == 0 else 1
    finished, length = ([], rows // count)
    for k in range(count):
        share = lax.slice_in_dim(array, k * length, (k + 1) * length, axis=dim)
        starts = jnp.arange(size) * rows + k * length
        finished.append(jax.vmap(apply)(lax.all_gather(share, axis), starts))
    return laid_out(jnp.concatenate(finished, axis=out_dim + 1), out_dim)


def over_axes(array, axes):
    return functools.reduce(lax.psum, axes, array)


def label_terms(logits, targets, first_row):
    shifted = targets - first_row
    inside = (shifted >= 0) & (shifted < logits.shape[1])
    clipped = jnp.clip(shifted, 0, logits.shape[1] - 1)
    picked = jnp.take_along_axis(logits, clipped[:, None], axis=1)[:, 0]
    return (jnp.sum(jnp.exp(logits), axis=1), jnp.where(inside, picked, 0.0))


def kto_losses(logratio, kl_total, seq_total, desirable):
    kl_estimate = kl_total / seq_total
    wanted = desirable_weight * (1.0 - jax.nn.sigmoid(kto_beta * (logratio - kl_estimate)))
    unwanted = undesirable_weight * (1.0 - jax.nn.sigmoid(kto_beta * (kl_estimate - logratio)))
    return jnp.where(desirable == 1, wanted, unwanted)


def on_device(hidden, kl_hidden, head_weight, labels, token_mask, kl_pair, desirable, ref_logps):
    sub_seq = hidden.shape[0]
    length = hidden.shape[1]
    vocab_rows = head_weight.shape[0]
    model_width = head_weight.shape[1]
    groups = lax.axis_size(VOCAB)
    vocab_index = lax.axis_index(VOCAB)
    data_index = lax.axis_index(DP)
    first_row = (data_index * groups + vocab_index) * vocab_rows
    all_labels, all_masks, all_pairs, all_desirable = (
        lax.all_gather(labels, DP, axis=0, tiled=True),
        lax.all_gather(token_mask, DP, axis=0, tiled=True),
        lax.all_gather(kl_pair, DP, axis=0, tiled=True),
        lax.all_gather(desirable, DP, axis=0, tiled=True),
    )
    targets = jnp.concatenate([all_labels, all_labels[all_pairs]], axis=1)
    weights_mask = jnp.concatenate([all_masks, all_masks[all_pairs]], axis=1).astype(jnp.float32)
    seq_total = targets.shape[0]
    columns = targets.shape[1]
    combined = jnp.concatenate([hidden, kl_hidden], axis=1)
    whole_rows = lax.all_gather(combined, VOCAB, axis=2, tiled=True)

    def portion_stats(portion, offset):
        number = portion.shape[0]
        logits = lax.dot_general(
            portion.reshape(number * columns, model_width),
            head_weight,
            (((1,), (1,)), ((), ())),
            preferred_element_type=jnp.float32,
        )
        portion_targets = lax.dynamic_slice_in_dim(targets, offset, number, 0).reshape(-1)
        part_sum, part_pick = label_terms(logits, portion_targets, first_row)
        return jnp.stack(
            [part_sum.reshape(number, columns), part_pick.reshape(number, columns)], axis=1
        )

    token_stats = work_in_pieces(whole_rows, DP, 0, portion_stats, 0)
    partition = token_stats[:, 0]
    picked = token_stats[:, 1]
    own_cols = columns // groups
    row_start = data_index * sub_seq
    col_start = vocab_index * own_cols
    ref_full = lax.dynamic_update_slice(
        jnp.zeros((seq_total, columns), jnp.float32), ref_logps, (row_start, col_start)
    )
    partition, picked, ref_all = (
        over_axes(partition, DP_VOCAB),
        over_axes(picked, DP_VOCAB),
        over_axes(ref_full, DP_VOCAB),
    )
    token_logps = picked - jnp.log(partition)
    differences = weights_mask * (token_logps - ref_all)
    logratio = jnp.sum(differences[:, :length], axis=1)
    kl_terms = jnp.sum(differences[:, length:], axis=1)
    losses = kto_losses(logratio, jnp.sum(kl_terms), seq_total, all_desirable)
    own_logps = lax.dynamic_slice(token_logps, (row_start, col_start), (sub_seq, own_cols))
    own_losses = lax.dynamic_slice_in_dim(losses, row_start, sub_seq, 0)
    return (own_logps, own_losses, jnp.mean(losses))


def solution(mesh):
    split = Mesh(mesh.devices.reshape(4, 4, 8, 2), ("dp_0", "dp_1", "vocab_0", "vocab_1"))
    in_specs = (
        P(DP, None, VOCAB),
        P(DP, None, VOCAB),
        P(DP_VOCAB, None),
        P(DP, None),
        P(DP, None),
        P(DP),
        P(DP),
        P(DP, VOCAB),
    )
    out_specs = (P(DP, VOCAB), P(DP), P())
    return jax.shard_map(
        on_device, mesh=split, in_specs=in_specs, out_specs=out_specs, check_vma=False
    )
```

profile of v0, /device:TPU:1, one launch (start us, length us, event | category | flops | bytes accessed | tf_op | source)
XLA Modules:
  0.0 216.1 jit_solution(3481418981377307972)
XLA Ops:
  7.2 0.0 all-gather.5.cloned.1.call-start
  7.2 0.7 pad_maximum_fusion
  8.0 0.1 copy.18
  8.1 26.5 %all_gather.21 = bf16[1,64,3584]{1,0,2:T(2,128)(2,1)S(1)} all-gather(bf16[1,64,224]{1,0,2:T(2,128)(2,1)S(1)} %copy.18), channel_id=1, replica_groups=mesh['dp_0'=4,'dp_1'=4,'vocab_0'=8,'vocab_1'=2] {'vocab_0','vocab_1'}, dimensions={2}, use_global_device_ids=true | all-gather | bytes 487424 | tf_op jit(solution)/shard_map/all_gather | solution.py:75
  34.6 3.1 %copy.19 = bf16[1,64,3584]{2,1,0:T(8,128)(2,1)} copy(bf16[1,64,3584]{1,0,2:T(2,128)(2,1)S(1)} %all_gather.21) | data formatting | bytes 917504 | tf_op jit(solution)/shard_map/all_gather | solution.py:75
  37.7 0.0 all-gather.5.cloned.1.call-update
  39.0 1.3 dynamic-slice
  40.2 0.8 dynamic-update-slice
  41.0 0.8 dynamic-update-slice.1
  41.8 13.2 %all-reduce.2 = (s32[16]{0:T(128)S(1)}, s32[16]{0:T(128)S(1)}) all-reduce(s32[16]{0:T(128)S(1)} %dynamic-update-slice, s32[16]{0:T(128)S(1)} %dynamic-update-slice.1), channel_id=1, replica_groups=mesh['dp_0'=4,'dp_1'=4,'vocab_0'=8,'vocab_1'=2] {'dp_0','dp_1'}, use_global_device_ids=true, to_apply=%add | all-reduce | flops 32 | bytes 256
  55.0 14.7 %all-gather.1 = s32[16,1,32]{2,1,0:T(1,128)S(1)} all-gather(s32[1,1,32]{2,1,0:T(1,128)} %bitcast.35), channel_id=1, replica_groups=mesh['dp_0'=4,'dp_1'=4,'vocab_0'=8,'vocab_1'=2] {'dp_0','dp_1'}, dimensions={0}, use_global_device_ids=true | all-gather | bytes 2176 | tf_op jit(solution)/shard_map/all_gather | solution.py:65
  69.7 0.6 gather_fusion
  70.2 0.1 pad_add_fusion
  70.3 0.6 gather_fusion.1
  71.0 0.1 reshape.163
  71.0 16.4 %all-gather.2 = s32[16,1,32]{2,1,0:T(1,128)S(1)} all-gather(s32[1,1,32]{2,1,0:T(1,128)} %bitcast.36), channel_id=1, replica_groups=mesh['dp_0'=4,'dp_1'=4,'vocab_0'=8,'vocab_1'=2] {'dp_0','dp_1'}, dimensions={0}, use_global_device_ids=true | all-gather | bytes 2176 | tf_op jit(solution)/shard_map/all_gather | solution.py:66
  87.4 0.6 gather_fusion.2
  88.0 0.9 dynamic_update_slice.3
  88.9 17.8 %all-gather.5.cloned.1.call-done = bf16[16,64,3584]{2,1,0:T(8,128)(2,1)} async-done(((bf16[1,64,3584]{2,1,0:T(8,128)(2,1)}), bf16[16,64,3584]{2,1,0:T(8,128)(2,1)}) %all-gather.5.cloned.1.call-update) | async-done | bytes 7340048 | tf_op jit(solution)/shard_map/all_gather | solution.py:32
  106.7 13.5 %exponential_reduce_fusion = (f32[16,64]{1,0:T(8,128)S(1)}, f32[16,64,1000]{2,1,0:T(8,128)}) fusion(bf16[16,64,3584]{2,1,0:T(8,128)(2,1)} %all-gather.5.cloned.1.call-done, bf16[1000,3584]{1,0:T(8,128)(2,1)} %param.10), kind=kOutput, calls=%fused_computation.6 | convolution fusion | flops 7341054976 | bytes 18608128 | tf_op jit(solution)/shard_map/vmap()/dot_general | solution.py:79
  120.2 17.9 %gather_fusion.3 = f32[1024]{0:T(1024)S(1)} fusion(f32[16,64,1000]{2,1,0:T(8,128)} %get-tuple-element.26, s32[1024]{0:T(1024)S(1)} %reshape.163), kind=kCustom, calls=%fused_computation.3 | custom fusion | bytes 20480 | tf_op jit(solution)/shard_map/vmap(jit(take_along_axis))/gather | solution.py:44
  138.1 0.1 gather.18
  138.2 11.8 %all-reduce.5 = (f32[16,64]{1,0:T(8,128)S(1)}, f32[16,64]{1,0:T(8,128)S(1)}, f32[16,64]{1,0:T(8,128)S(1)}) all-reduce(f32[16,64]{1,0:T(8,128)S(1)} %get-tuple-element.24, f32[16,64]{1,0:T(8,128)S(1)} %get-tuple-element.23, f32[16,64]{1,0:T(8,128)S(1)} %dynamic_update_slice.3), channel_id=1, replica_groups=mesh['dp_0'=4,'dp_1'=4,'vocab_0'=8,'vocab_1'=2] {'dp_0'}, use_global_device_ids=true, to_apply=%region_1.2 | all-reduce | flops 3072 | bytes 24576 | tf_op jit(solution)/shard_map/psum | solution.py:37
  150.0 12.2 %all-reduce.4 = (f32[16,64]{1,0:T(8,128)S(1)}, f32[16,64]{1,0:T(8,128)S(1)}, f32[16,64]{1,0:T(8,128)S(1)}) all-reduce(f32[16,64]{1,0:T(8,128)S(1)} %get-tuple-element.13, f32[16,64]{1,0:T(8,128)S(1)} %get-tuple-element.14, f32[16,64]{1,0:T(8,128)S(1)} %get-tuple-element.15), channel_id=1, replica_groups=mesh['dp_0'=4,'dp_1'=4,'vocab_0'=8,'vocab_1'=2] {'dp_1'}, use_global_device_ids=true, to_apply=%region_2.3 | all-reduce | flops 3072 | bytes 24576 | tf_op jit(solution)/shard_map/psum | solution.py:37
  162.2 23.4 %all-reduce.3 = (f32[16,64]{1,0:T(8,128)S(1)}, f32[16,64]{1,0:T(8,128)S(1)}, f32[16,64]{1,0:T(8,128)S(1)}) all-reduce(f32[16,64]{1,0:T(8,128)S(1)} %get-tuple-element.10, f32[16,64]{1,0:T(8,128)S(1)} %get-tuple-element.11, f32[16,64]{1,0:T(8,128)S(1)} %get-tuple-element.12), channel_id=1, replica_groups=mesh['dp_0'=4,'dp_1'=4,'vocab_0'=8,'vocab_1'=2] {'vocab_0'}, use_global_device_ids=true, to_apply=%region_3.4 | all-reduce | flops 3072 | bytes 24576 | tf_op jit(solution)/shard_map/psum | solution.py:37
  185.6 18.7 %all-reduce.6 = (f32[16,64]{1,0:T(8,128)S(1)}, f32[16,64]{1,0:T(8,128)S(1)}, f32[16,64]{1,0:T(8,128)S(1)}) all-reduce(f32[16,64]{1,0:T(8,128)S(1)} %get-tuple-element.7, f32[16,64]{1,0:T(8,128)S(1)} %get-tuple-element.8, f32[16,64]{1,0:T(8,128)S(1)} %get-tuple-element.9), channel_id=1, replica_groups=mesh['dp_0'=4,'dp_1'=4,'vocab_0'=8,'vocab_1'=2] {'vocab_1'}, use_global_device_ids=true, to_apply=%region_4.5 | all-reduce | flops 3072 | bytes 24576 | tf_op jit(solution)/shard_map/psum | solution.py:37
  204.3 0.1 fusion.7
  204.4 0.7 slice_reduce_fusion
  205.7 0.6 fusion.8
  207.0 0.6 dynamic_slice.7
  207.6 0.6 dynamic_slice.6
  (14 shorter events, 0.1 us)
Async XLA Ops:
  7.2 99.5 %all-gather.5.cloned.1.call-start = ((), (), s32[]{:S(2)}) async-start(), calls=%async_computation | async-start | bytes 7798784 | tf_op jit(solution)/shard_map/all_gather | solution.py:32
Sparse Core Ops, SparseCore 0:
  37.8 68.8 all-gather.4
where the time goes:
time: 217 us; the launch traced here: 216 us
  blocking collectives  137 us (63%)
  local copies, waits for them, and re-layouts  27.8 us (13%)
  waiting for transfers between devices  17.9 us (8%)
  between operations  17.9 us (8%)
  matrix products  13.5 us (6%)
  other arithmetic  2.25 us (1%)
    psum x4, blocking collectives, over_axes(): return functools.reduce(lax.psum, axes, array)  66.1 us
    all_gather x1, blocking collectives, on_device(): whole_rows = lax.all_gather(combined, VOCAB, axis=2, tiled=True)  26.5 us
    gather x3, local copies, waits for them, and re-layouts, label_terms(): picked = jnp.take_along_axis(logits, clipped[:, None], axis=1)[:, 0]  18 us
    all_gather x1, waiting for transfers between devices, work_in_pieces(): finished.append(jax.vmap(apply)(lax.all_gather(share, axis), starts))  17.8 us
    all_gather x1, blocking collectives, on_device(): lax.all_gather(token_mask, DP, axis=0, tiled=True)  16.4 us
    all_gather x1, blocking collectives, on_device(): lax.all_gather(labels, DP, axis=0, tiled=True)  14.7 us
    dot_general x1, matrix products, portion_stats(): lax.dot_general(portion.reshape(number * columns, model_width), head_weig...  13.5 us
    unnamed x1, blocking collectives  13.2 us
  transfers between devices with their start and end apart: 1, of which 1 were waited for; matrix products, arithmetic and copies ran while one was open for 3% of the time, Pallas kernels for 0%

commit v1 on v0

v1 whole, which is shorter than its diff:
```python
import itertools

import jax
import jax.numpy as jnp
from jax import lax
from jax.experimental import pallas as pl
from jax.experimental.pallas import tpu as pltpu
from jax.sharding import Mesh
from jax.sharding import PartitionSpec as P

NX, NY, NZ, NC = 4, 4, 8, 2
DP = ("x", "y")
VOCAB = ("z", "c")
LEN = 32
SEQS = NX * NY
ROWS = SEQS * LEN
D = 3584
PIECE = D // NZ
META = 128
VOCAB_ROWS = 1000
TILE = 256
MIB = 1024 * 1024

kto_beta = 0.1
desirable_weight = 1.0
undesirable_weight = 1.33


def swap_cores(array):
    return lax.ppermute(array, "c", [(0, 1), (1, 0)])


def xor_along(array, axis, k):
    return lax.ppermute(array, axis, [(i, i ^ k) for i in range(lax.axis_size(axis))])


def split_pairs(k, first):
    pairs = []
    for x, y, c in itertools.product(range(NX), range(NY), range(NC)):
        along_x = (c == 0) == first
        u, v = (x ^ k, y) if along_x else (x, y ^ k)
        pairs.append(((x * NY + y) * NC + c, (u * NY + v) * NC + c))
    return pairs


def split_xor(array, k, first):
    return lax.ppermute(array, ("x", "y", "c"), split_pairs(k, first))


def assemble_kernel(place, own4, far4, meta, out):
    z = place[2]
    for pair in range(NZ // 2):
        halves = []
        for p in (2 * pair, 2 * pair + 1):
            k = jnp.bitwise_xor(z, p)
            near = own4[jnp.bitwise_and(k, 3)]
            far = far4[jnp.bitwise_and(k, 3)]
            halves.append(jnp.where(k < 4, near, far))
        out[:, pair * 2 * PIECE : (pair + 1) * 2 * PIECE] = jnp.concatenate(halves, axis=1)
    out[:, D:] = meta[...]


def logits_kernel(place, q0, q1, q2, q3, ref, wa, wb, out, stat, rows, target):
    step = pl.program_id(0)

    @pl.when(step == 0)
    def _():
        x, y, c = place[0], place[1], place[3]
        for j, q in enumerate((q0, q1, q2, q3)):
            for k in range(4):
                u = jnp.where(c == 0, jnp.bitwise_xor(x, k), jnp.bitwise_xor(x, j))
                v = jnp.where(c == 0, jnp.bitwise_xor(y, j), jnp.bitwise_xor(y, k))
                start = pl.multiple_of((u * NY + v) * LEN, LEN)
                rows[pl.ds(start, LEN), :] = q[k]
        meta = rows[:, D:]
        partner = meta[:, 4:5].astype(jnp.float32).astype(jnp.int32)
        left = lax.broadcasted_iota(jnp.int32, (ROWS, ROWS), 0)
        right = lax.broadcasted_iota(jnp.int32, (ROWS, ROWS), 1)
        same = (partner == right // LEN) & (left % LEN == right % LEN)
        moved = lax.dot_general(
            meta,
            same.astype(jnp.float32).astype(jnp.bfloat16),
            (((0,), (1,)), ((), ())),
            preferred_element_type=jnp.float32,
        )
        target[...] = (moved[0:1] + 256.0 * moved[1:2] + 65536.0 * moved[2:3]).astype(jnp.int32)
        stat[0:1] = moved[3:4]
        stat[1:2] = moved[5:6]
        out[0:1] = jnp.zeros((1, ROWS), jnp.float32)
        out[1:2] = -ref[...]

    vocab = step * TILE + lax.broadcasted_iota(jnp.int32, (TILE, ROWS), 0)
    valid = vocab < VOCAB_ROWS
    for weight, base in ((wa, place[4]), (wb, place[5])):
        logits = lax.dot_general(
            weight[...],
            rows[:, :D],
            (((1,), (1,)), ((), ())),
            preferred_element_type=jnp.float32,
        )
        out[0:1] += jnp.sum(jnp.where(valid, jnp.exp(logits), 0.0), axis=0, keepdims=True)
        hit = valid & (vocab + base == target[...])
        out[1:2] += jnp.sum(jnp.where(hit, logits, 0.0), axis=0, keepdims=True)


def losses_kernel(place, own, other, own_stat, other_stat, ref, logps, own_loss, loss):
    x, y, z, c = place[0], place[1], place[2], place[3]
    first = c == 0
    lane = lax.broadcasted_iota(jnp.int32, (SEQS, ROWS), 1)
    row = lax.broadcasted_iota(jnp.int32, (SEQS, ROWS), 0)
    inside = lane // LEN == row
    picked = []
    sums = []
    for a, b, sa, sb in (
        (own, other, own_stat, other_stat),
        (other, own, other_stat, own_stat),
    ):
        partition = jnp.where(first, a[0:1], b[0:1])
        chosen = jnp.where(first, a[1:2], b[1:2])
        weight = jnp.where(first, sa[0:1], sb[0:1])
        value = chosen - jnp.log(partition)
        picked.append(value)
        sums.append(jnp.sum(jnp.where(inside, weight * value, 0.0), axis=1, keepdims=True))
    wanted_row = jnp.where(first, own_stat[1:2], other_stat[1:2])
    desirable = jnp.sum(
        jnp.where(inside & (lane % LEN == 0), wanted_row, 0.0), axis=1, keepdims=True
    )
    logratio, kl_terms = sums
    kl_estimate = jnp.sum(kl_terms, axis=0, keepdims=True) / SEQS
    wanted = desirable_weight * (1.0 - jax.nn.sigmoid(kto_beta * (logratio - kl_estimate)))
    unwanted = undesirable_weight * (1.0 - jax.nn.sigmoid(kto_beta * (kl_estimate - logratio)))
    losses = jnp.where(desirable > 0.5, wanted, unwanted)
    seq = x * NY + y
    here = lax.broadcasted_iota(jnp.int32, (SEQS, 1), 0) == seq
    own_loss[...] = jnp.sum(jnp.where(here, losses, 0.0), axis=0, keepdims=True)
    loss[...] = jnp.sum(losses, axis=0, keepdims=True) / SEQS
    half = jnp.where(z < NZ // 2, picked[0], picked[1])
    start = seq * LEN + (z % (NZ // 2)) * 8 + c * 4
    hit = lax.broadcasted_iota(jnp.int32, (8, ROWS), 1) == (
        start + lax.broadcasted_iota(jnp.int32, (8, ROWS), 0)
    )
    column = jnp.sum(jnp.where(hit, half, 0.0), axis=1, keepdims=True)
    square = lax.broadcasted_iota(jnp.int32, (8, 128), 0) == lax.broadcasted_iota(
        jnp.int32, (8, 128), 1
    )
    line = jnp.sum(jnp.where(square, column, 0.0), axis=0, keepdims=True)
    logps[...] = line[:, :4] + ref[...]


def smem():
    return pl.BlockSpec(memory_space=pltpu.SMEM)


def vmem():
    return pl.BlockSpec(memory_space=pltpu.VMEM)


def add4(array, parts):
    one, two, three = parts
    return (array + one) + (two + three)


def on_device(hidden, kl_hidden, head_weight, labels, token_mask, kl_pair, desirable, ref_logps):
    x, y, z, c = (lax.axis_index(a) for a in ("x", "y", "z", "c"))
    first = c == 0
    shard = ((x * NY + y) * NZ + z) * NC
    place = jnp.stack(
        [x, y, z, c, (shard + c) * VOCAB_ROWS, (shard + 1 - c) * VOCAB_ROWS]
    ).astype(jnp.int32)

    keep = jnp.where(first, hidden[0], kl_hidden[0])
    give = jnp.where(first, kl_hidden[0], hidden[0])
    came = swap_cores(give)
    ref_came = swap_cores(ref_logps)
    head_weight, came, ref_came = lax.optimization_barrier((head_weight, came, ref_came))
    other_weight = swap_cores(head_weight)
    piece = jnp.concatenate(
        [jnp.where(first, keep, came), jnp.where(first, came, keep)], axis=1
    )

    seq = x * NY + y
    label = labels[0]
    partner = jnp.where(first, seq, kl_pair[0])
    fields = jnp.stack(
        [
            label % 256,
            (label // 256) % 256,
            label // 65536,
            token_mask[0],
            jnp.broadcast_to(partner, (LEN,)),
            jnp.broadcast_to(desirable[0], (LEN,)),
        ],
        axis=1,
    )
    meta = jnp.pad(fields, ((0, 0), (0, META - fields.shape[1]))).astype(jnp.bfloat16)

    pair_ref = jnp.concatenate(
        [jnp.where(first, ref_logps, ref_came), jnp.where(first, ref_came, ref_logps)], axis=1
    )
    mine = (z // (NZ // 2)) == c
    ref_rows = lax.dynamic_update_slice(
        jnp.zeros((1, ROWS), jnp.float32),
        jnp.where(mine, pair_ref, 0.0),
        (0, seq * LEN + (z % (NZ // 2)) * 8),
    )

    own4 = jnp.stack([piece] + [xor_along(piece, "z", k) for k in (1, 2, 3)])
    far4 = xor_along(own4, "z", 4)
    whole = pl.pallas_call(
        assemble_kernel,
        out_shape=jax.ShapeDtypeStruct((LEN, D + META), jnp.bfloat16),
        in_specs=[smem(), vmem(), vmem(), vmem()],
        out_specs=vmem(),
        name="assemble",
    )(place, own4, far4, meta)

    near = jnp.stack([whole] + [split_xor(whole, k, True) for k in (1, 2, 3)])
    blocks = [near] + [split_xor(near, k, False) for k in (1, 2, 3)]

    fixed = pl.BlockSpec((4, LEN, D + META), lambda i: (0, 0, 0))
    line = pl.BlockSpec((1, ROWS), lambda i: (0, 0))
    two = pl.BlockSpec((2, ROWS), lambda i: (0, 0))
    tile = pl.BlockSpec((TILE, D), lambda i: (i, 0))
    sums, stat = pl.pallas_call(
        logits_kernel,
        grid=(pl.cdiv(VOCAB_ROWS, TILE),),
        out_shape=[jax.ShapeDtypeStruct((2, ROWS), jnp.float32)] * 2,
        in_specs=[smem(), fixed, fixed, fixed, fixed, line, tile, tile],
        out_specs=[two, two],
        scratch_shapes=[
            pltpu.VMEM((ROWS, D + META), jnp.bfloat16),
            pltpu.VMEM((1, ROWS), jnp.int32),
        ],
        compiler_params=pltpu.CompilerParams(vmem_limit_bytes=40 * MIB),
        cost_estimate=pl.CostEstimate(
            flops=4 * ROWS * VOCAB_ROWS * D,
            bytes_accessed=2 * (2 * VOCAB_ROWS + ROWS) * D,
            transcendentals=2 * ROWS * VOCAB_ROWS,
        ),
        name="logits",
    )(place, *blocks, ref_rows, head_weight, other_weight)

    other_stat = swap_cores(stat)
    sums = add4(sums, [xor_along(sums, "x", k) for k in (1, 2, 3)])
    sums = add4(sums, [xor_along(sums, "y", k) for k in (1, 2, 3)])
    sums = add4(sums, [xor_along(sums, "z", k) for k in (1, 2, 3)])
    sums = sums + xor_along(sums, "z", 4)
    other_sums = swap_cores(sums)
    logps, own_loss, loss = pl.pallas_call(
        losses_kernel,
        out_shape=[
            jax.ShapeDtypeStruct((1, 4), jnp.float32),
            jax.ShapeDtypeStruct((1, 1), jnp.float32),
            jax.ShapeDtypeStruct((1, 1), jnp.float32),
        ],
        in_specs=[smem()] + [vmem()] * 5,
        out_specs=[vmem()] * 3,
        name="losses",
    )(place, sums, other_sums, stat, other_stat, ref_logps)
    return (logps, own_loss.reshape(1), loss.reshape(()))


def solution(mesh):
    split = Mesh(mesh.devices.reshape(NX, NY, NZ, NC), DP + VOCAB)
    in_specs = (
        P(DP, None, VOCAB),
        P(DP, None, VOCAB),
        P(DP + VOCAB, None),
        P(DP, None),
        P(DP, None),
        P(DP),
        P(DP),
        P(DP, VOCAB),
    )
    out_specs = (P(DP, VOCAB), P(DP), P())
    return jax.shard_map(
        on_device, mesh=split, in_specs=in_specs, out_specs=out_specs, check_vma=False
    )
```

time: 217 us -> 116 us (0.53)
  blocking collectives: 137 us -> 0 us
  starting transfers between devices: 0.04 us -> 47.6 us
  waiting for transfers between devices: 17.9 us -> 40.3 us
  local copies, waits for them, and re-layouts: 27.8 us -> 6.37 us
  between operations: 17.9 us -> 2.08 us
  Pallas kernels: 0 us -> 14.6 us
  matrix products: 13.5 us -> 0 us
  other arithmetic: 2.25 us -> 4.74 us
    psum x4 -> x0, blocking collectives: 66.1 us -> none  [over_axes(): return functools.reduce(lax.psum, axes, array)]
    all_gather x3 -> x0, blocking collectives: 57.5 us -> none  [the longest x1 26.5 us: on_device(): whole_rows = lax.all_gather(combined, VOCAB, axis=2, tiled=True)]
    ppermute x0 -> x25, starting transfers between devices: none -> 47.6 us  [the longest x14 23.8 us: xor_along(): lax.ppermute(array, axis, [(i, i ^ k) for i in range(lax.axis_size(axis))])]
    ppermute x0 -> x25, waiting for transfers between devices: none -> 40.3 us  [the longest x6 27.5 us: split_xor(): return lax.ppermute(array, ('x', 'y', 'c'), split_pairs(k, first))]
    gather x6 -> x0, local copies, waits for them, and re-layouts: 19.7 us -> none  [the longest x3 18 us: label_terms(): picked = jnp.take_along_axis(logits, clipped[:, None], axis=1)[:, 0]]
    all_gather x1 -> x0, waiting for transfers between devices: 17.8 us -> none  [work_in_pieces(): finished.append(jax.vmap(apply)(lax.all_gather(share, axis), starts))]
    pallas_call x0 -> x3, Pallas kernels: none -> 14.6 us  [the longest x1 11.3 us: on_device(): pl.pallas_call(logits_kernel, grid=(pl.cdiv(VOCAB_ROWS, TILE),), out_shap...]
    dot_general x1 -> x0, matrix products: 13.5 us -> none  [portion_stats(): lax.dot_general(portion.reshape(number * columns, model_width), head_weig...]
  transfers between devices with their start and end apart: 1 -> 25, of which waited for: 1 -> 16; matrix products, arithmetic and copies ran while one was open for 3% -> 5% of each run, Pallas kernels for 0% -> 2%
where the time goes in v1:
time: 116 us
  starting transfers between devices  47.6 us (41%)
  waiting for transfers between devices  40.3 us (35%)
  Pallas kernels  14.6 us (13%)
  local copies, waits for them, and re-layouts  6.37 us (5%)
  other arithmetic  4.74 us (4%)
  between operations  2.08 us (2%)
    ppermute x6, waiting for transfers between devices, split_xor(): return lax.ppermute(array, ('x', 'y', 'c'), split_pairs(k, first))  27.5 us
    ppermute x14, starting transfers between devices, xor_along(): lax.ppermute(array, axis, [(i, i ^ k) for i in range(lax.axis_size(axis))])  23.8 us
    ppermute x5, starting transfers between devices, swap_cores(): return lax.ppermute(array, 'c', [(0, 1), (1, 0)])  17.1 us
    pallas_call x1, Pallas kernels, on_device(): pl.pallas_call(logits_kernel, grid=(pl.cdiv(VOCAB_ROWS, TILE),), out_shap...  11.3 us
    ppermute x14, waiting for transfers between devices, xor_along(): lax.ppermute(array, axis, [(i, i ^ k) for i in range(lax.axis_size(axis))])  10.8 us
    ppermute x6, starting transfers between devices, split_xor(): return lax.ppermute(array, ('x', 'y', 'c'), split_pairs(k, first))  6.67 us
    unnamed x16, local copies, waits for them, and re-layouts  4.89 us
  transfers between devices with their start and end apart: 25, of which 16 were waited for; matrix products, arithmetic and copies ran while one was open for 5% of the time, Pallas kernels for 2%

profile of v1, /device:TPU:1, one launch (start us, length us, event | category | flops | bytes accessed | tf_op | source)
XLA Modules:
  0.0 115.6 jit_solution(1185966759735154953)
XLA Ops:
  0.6 0.7 select_bitcast_fusion
  1.4 3.2 %collective-permute-start = (bf16[32,224]{1,0:T(8,128)(2,1)S(1)}, bf16[32,224]{1,0:T(8,128)(2,1)S(1)}, u32[]{:S(2)}, u32[]{:S(2)}) collective-permute-start(bf16[32,224]{1,0:T(8,128)(2,1)S(1)} %select_bitcast_fusion), channel_id=1, source_target_pairs={{0,1},{1,0},{2,3},{3,2},{4,5},{5,4},{6,7},{7,6},{8,9},{9,8},{10,11... | collective-permute-start | bytes 43016 | tf_op jit(solution)/shard_map/ppermute | solution.py:30
  4.6 0.1 collective-permute-start.1
  4.7 1.2 %collective-permute-done.1 = f32[1,4]{1,0:T(1,128)S(1)} collective-permute-done((f32[1,4]{1,0:T(1,128)}, f32[1,4]{1,0:T(1,128)S(1)}, u32[]{:S(2)}, u32[]{:S(2)}) %collective-permute-start.1) | collective-permute-done | bytes 48 | tf_op jit(solution)/shard_map/ppermute | solution.py:30
  5.9 0.0 collective-permute-done
  5.9 0.2 collective-permute-start.12
  6.1 0.7 bitcast_select_fusion.1
  6.8 0.1 fusion.4
  6.9 1.3 %collective-permute-start.3 = (bf16[32,448]{1,0:T(8,128)(2,1)S(1)}, bf16[32,448]{1,0:T(8,128)(2,1)S(1)}, u32[]{:S(2)}, u32[]{:S(2)}) collective-permute-start(bf16[32,448]{1,0:T(8,128)(2,1)S(1)} %get-tuple-element.22), channel_id=1, source_target_pairs={{0,4},{2,6},{4,0},{6,2},{8,12},{10,14},{12,8},{14,10},{1,5},{3,7},... | collective-permute-start | bytes 86024 | tf_op jit(solution)/shard_map/ppermute | solution.py:34
  8.2 1.6 %collective-permute-start.2 = (bf16[32,448]{1,0:T(8,128)(2,1)S(1)}, bf16[32,448]{1,0:T(8,128)(2,1)S(1)}, u32[]{:S(2)}, u32[]{:S(2)}) collective-permute-start(bf16[32,448]{1,0:T(8,128)(2,1)S(1)} %get-tuple-element.22), channel_id=1, source_target_pairs={{0,2},{2,0},{4,6},{6,4},{8,10},{10,8},{12,14},{14,12},{1,3},{3,1},... | collective-permute-start | bytes 86024 | tf_op jit(solution)/shard_map/ppermute | solution.py:34
  9.8 0.7 collective-permute-start.4
  10.5 0.7 fusion.3
  12.5 0.0 collective-permute-done.3
  12.5 0.0 collective-permute-done.2
  12.5 1.9 %collective-permute-done.4 = bf16[32,448]{1,0:T(8,128)(2,1)S(1)} collective-permute-done((bf16[32,448]{1,0:T(8,128)(2,1)S(1)}, bf16[32,448]{1,0:T(8,128)(2,1)S(1)}, u32[]{:S(2)}, u32[]{:S(2)}) %collective-permute-start.4) | collective-permute-done | bytes 28704 | tf_op jit(solution)/shard_map/ppermute | solution.py:34
  14.4 4.4 %collective-permute-start.5 = (bf16[4,32,448]{2,1,0:T(8,128)(2,1)S(1)}, bf16[4,32,448]{2,1,0:T(8,128)(2,1)S(1)}, u32[]{:S(2)}, u32[]{:S(2)}) collective-permute-start(bf16[4,32,448]{2,1,0:T(8,128)(2,1)S(1)} %pad_maximum_fusion.1.own4), channel_id=1, source_target_pairs={{0,8},{2,10},{4,12},{6,14},{8,0},{10,2},{12,4},{14,6},{1,9},{3,11}... | collective-permute-start | bytes 344072 | tf_op jit(solution)/shard_map/ppermute | solution.py:34
  18.8 0.7 convert_bitcast_fusion
  19.5 0.1 copy.16
  19.6 0.6 pad.5.meta
  20.2 0.6 stack.64.place
  20.8 1.5 %collective-permute-done.5.far4 = bf16[4,32,448]{2,1,0:T(8,128)(2,1)S(1)} collective-permute-done((bf16[4,32,448]{2,1,0:T(8,128)(2,1)S(1)}, bf16[4,32,448]{2,1,0:T(8,128)(2,1)S(1)}, u32[]{:S(2)}, u32[]{:S(2)}) %collective-permute-start.5) | collective-permute-done | bytes 114720 | tf_op jit(solution)/shard_map/ppermute | solution.py:34
  22.3 0.6 copy-done.4
  23.0 1.8 %assemble.1 = bf16[32,3712]{1,0:T(8,128)(2,1)} custom-call(s32[6]{0:T(128)} %stack.64.place, bf16[4,32,448]{2,1,0:T(8,128)(2,1)} %copy-done.3, bf16[4,32,448]{2,1,0:T(8,128)(2,1)} %copy-done.4, bf16[32,128]{1,0:T(8,128)(2,1)} %pad.5.meta), custom_call_target="tpu_custom_call" | custom-call | tf_op jit(solution)/shard_map/assemble/pallas_call | solution.py:209
  24.8 2.7 %collective-permute-start.8 = (bf16[32,3712]{1,0:T(8,128)(2,1)}, bf16[32,3712]{1,0:T(8,128)(2,1)S(1)}, u32[]{:S(2)}, u32[]{:S(2)}) collective-permute-start(bf16[32,3712]{1,0:T(8,128)(2,1)} %assemble.1), channel_id=1, source_target_pairs={{0,192},{1,49},{16,208},{17,33},{32,224},{33,17},{48,240},{49,1},{... | collective-permute-start | bytes 712712 | tf_op jit(solution)/shard_map/ppermute | solution.py:47
  27.5 0.3 collective-permute-start.7
  27.9 0.2 collective-permute-start.6
  28.1 5.3 %collective-permute-done.8 = bf16[32,3712]{1,0:T(8,128)(2,1)S(1)} collective-permute-done((bf16[32,3712]{1,0:T(8,128)(2,1)}, bf16[32,3712]{1,0:T(8,128)(2,1)S(1)}, u32[]{:S(2)}, u32[]{:S(2)}) %collective-permute-start.8) | collective-permute-done | bytes 237600 | tf_op jit(solution)/shard_map/ppermute | solution.py:47
  33.4 0.8 collective-permute-done.7
  34.2 0.5 collective-permute-done.6
  34.7 1.1 pad_maximum_fusion.q0
  35.8 2.6 %collective-permute-start.11 = (bf16[4,32,3712]{2,1,0:T(8,128)(2,1)S(1)}, bf16[4,32,3712]{2,1,0:T(8,128)(2,1)S(1)}, u32[]{:S(2)}, u32[]{:S(2)}) collective-permute-start(bf16[4,32,3712]{2,1,0:T(8,128)(2,1)S(1)} %pad_maximum_fusion.q0), channel_id=1, source_target_pairs={{0,48},{1,193},{16,32},{17,209},{32,16},{33,225},{48,0},{49,241},{... | collective-permute-start | bytes 2850824 | tf_op jit(solution)/shard_map/ppermute | solution.py:47
  38.3 0.5 collective-permute-start.10
  38.9 0.3 collective-permute-start.9
  39.1 0.7 broadcast_select_fusion.2
  39.8 0.1 broadcast_select_fusion.3
  39.8 0.1 dynamic_update_slice.3.ref
  40.0 20.2 %collective-permute-done.11.q3 = bf16[4,32,3712]{2,1,0:T(8,128)(2,1)S(1)} collective-permute-done((bf16[4,32,3712]{2,1,0:T(8,128)(2,1)S(1)}, bf16[4,32,3712]{2,1,0:T(8,128)(2,1)S(1)}, u32[]{:S(2)}, u32[]{:S(2)}) %collective-permute-start.11) | collective-permute-done | bytes 950304 | tf_op jit(solution)/shard_map/ppermute | solution.py:47
  60.1 0.0 collective-permute-done.10.q2
  60.1 0.7 collective-permute-done.9.q1
  60.9 0.0 collective-permute-done.12.wb
  60.9 0.6 copy-done
  61.5 3.0 %copy-done.2 = bf16[1000,3584]{1,0:T(8,128)(2,1)S(1)} copy-done((bf16[1000,3584]{1,0:T(8,128)(2,1)S(1)}, bf16[1000,3584]{1,0:T(8,128)(2,1)}, u32[]{:S(2)}) %copy-start.2) | copy-done | bytes 7168024
  64.5 11.3 %logits.1 = (f32[2,512]{1,0:T(2,128)S(1)}, f32[2,512]{1,0:T(2,128)S(1)}) custom-call(s32[6]{0:T(128)S(1)} %copy-done, bf16[4,32,3712]{2,1,0:T(8,128)(2,1)S(1)} %pad_maximum_fusion.q0, bf16[4,32,3712]{2,1,0:T(8,128)(2,1)} %collective-permute-done.9.q1, bf16[4,32,3712]{2,1,0:T(8,128)(2,1)S(1)} %collective-permute-done.10.q2, ...), custom_call_target="tpu_custom_call" | custom-call | flops 7340032000 | bytes 18006016 | tf_op jit(solution)/shard_map/logits/pallas_call | solution.py:224
  75.9 2.6 %collective-permute-start.15 = (f32[2,512]{1,0:T(2,128)S(1)}, f32[2,512]{1,0:T(2,128)S(1)}, u32[]{:S(2)}, u32[]{:S(2)}) collective-permute-start(f32[2,512]{1,0:T(2,128)S(1)} %get-tuple-element.14), channel_id=1, source_target_pairs={{0,192},{64,128},{128,64},{192,0},{1,193},{65,129},{129,65},{193,1... | collective-permute-start | bytes 12296 | tf_op jit(solution)/shard_map/ppermute | solution.py:34
  78.4 0.5 collective-permute-start.14
  78.9 0.3 collective-permute-start.13
  79.2 0.4 collective-permute-done.15
  79.6 2.8 %collective-permute-done.14 = f32[2,512]{1,0:T(2,128)S(1)} collective-permute-done((f32[2,512]{1,0:T(2,128)S(1)}, f32[2,512]{1,0:T(2,128)S(1)}, u32[]{:S(2)}, u32[]{:S(2)}) %collective-permute-start.14) | collective-permute-done | bytes 4128 | tf_op jit(solution)/shard_map/ppermute | solution.py:34
  82.4 2.9 %collective-permute-start.18 = (f32[2,512]{1,0:T(2,128)S(1)}, f32[2,512]{1,0:T(2,128)S(1)}, u32[]{:S(2)}, u32[]{:S(2)}) collective-permute-start(f32[2,512]{1,0:T(2,128)S(1)} %add_add_fusion.2), channel_id=1, source_target_pairs={{0,48},{16,32},{32,16},{48,0},{1,49},{17,33},{33,17},{49,1},{2,50}... | collective-permute-start | bytes 12296 | tf_op jit(solution)/shard_map/ppermute | solution.py:34
  85.3 0.4 collective-permute-start.17
  85.7 0.3 collective-permute-start.16
  86.0 0.4 collective-permute-done.18
  86.3 2.9 %collective-permute-done.17 = f32[2,512]{1,0:T(2,128)S(1)} collective-permute-done((f32[2,512]{1,0:T(2,128)S(1)}, f32[2,512]{1,0:T(2,128)S(1)}, u32[]{:S(2)}, u32[]{:S(2)}) %collective-permute-start.17) | collective-permute-done | bytes 4128 | tf_op jit(solution)/shard_map/ppermute | solution.py:34
  89.3 1.1 collective-permute-start.21
  90.4 2.5 %collective-permute-start.19 = (f32[2,512]{1,0:T(2,128)S(1)}, f32[2,512]{1,0:T(2,128)S(1)}, u32[]{:S(2)}, u32[]{:S(2)}) collective-permute-start(f32[2,512]{1,0:T(2,128)S(1)} %add_add_fusion.1), channel_id=1, source_target_pairs={{0,2},{2,0},{4,6},{6,4},{8,10},{10,8},{12,14},{14,12},{1,3},{3,1},... | collective-permute-start | bytes 12296 | tf_op jit(solution)/shard_map/ppermute | solution.py:34
  92.9 0.7 collective-permute-done.21
  93.6 0.1 collective-permute-done.20
  93.8 0.1 collective-permute-done.19
  93.9 5.3 %collective-permute-start.22 = (f32[2,512]{1,0:T(2,128)S(1)}, f32[2,512]{1,0:T(2,128)S(1)}, u32[]{:S(2)}, u32[]{:S(2)}) collective-permute-start(f32[2,512]{1,0:T(2,128)S(1)} %add_add_fusion), channel_id=1, source_target_pairs={{0,8},{2,10},{4,12},{6,14},{8,0},{10,2},{12,4},{14,6},{1,9},{3,11}... | collective-permute-start | bytes 12296 | tf_op jit(solution)/shard_map/ppermute | solution.py:34
  99.2 10.5 %collective-permute-start.24 = (f32[2,512]{1,0:T(2,128)S(1)}, f32[2,512]{1,0:T(2,128)S(1)}, u32[]{:S(2)}, u32[]{:S(2)}) collective-permute-start(f32[2,512]{1,0:T(2,128)S(1)} %get-tuple-element.15.own_stat), channel_id=1, source_target_pairs={{0,1},{1,0},{2,3},{3,2},{4,5},{5,4},{6,7},{7,6},{8,9},{9,8},{10,11... | collective-permute-start | bytes 12296 | tf_op jit(solution)/shard_map/ppermute | solution.py:30
  109.7 3.1 %collective-permute-start.23 = (f32[2,512]{1,0:T(2,128)S(1)}, f32[2,512]{1,0:T(2,128)S(1)}, u32[]{:S(2)}, u32[]{:S(2)}) collective-permute-start(f32[2,512]{1,0:T(2,128)S(1)} %add.114.own), channel_id=1, source_target_pairs={{0,1},{1,0},{2,3},{3,2},{4,5},{5,4},{6,7},{7,6},{8,9},{9,8},{10,11... | collective-permute-start | bytes 12296 | tf_op jit(solution)/shard_map/ppermute | solution.py:30
  112.8 0.8 collective-permute-done.23.other
  113.6 0.6 copy-done.7
  114.2 1.4 %losses.1 = (f32[1,4]{1,0:T(1,128)}, f32[1,1]{1,0:T(1,128)}, f32[1,1]{1,0:T(1,128)}) custom-call(s32[6]{0:T(128)} %stack.64.place, f32[2,512]{1,0:T(2,128)} %copy-done.5, f32[2,512]{1,0:T(2,128)} %copy-done.7, f32[2,512]{1,0:T(2,128)} %copy-done.1, f32[2,512]{1,0:T(2,128)} %copy-done.6, f32[1,4]{1,0:T(1,128)} %ref.1), custom_call_target="tpu_custom_call" | custom-call | tf_op jit(solution)/shard_map/losses/pallas_call | solution.py:249
  (26 shorter events, 0.1 us)
Async XLA Ops:
  1.4 4.5 %collective-permute-start = (bf16[32,224]{1,0:T(8,128)(2,1)S(1)}, bf16[32,224]{1,0:T(8,128)(2,1)S(1)}, u32[]{:S(2)}, u32[]{:S(2)}) collective-permute-start(bf16[32,224]{1,0:T(8,128)(2,1)S(1)} %select_bitcast_fusion), channel_id=1, source_target_pairs={{0,1},{1,0},{2,3},{3,2},{4,5},{5,4},{6,7},{7,6},{8,9},{9,8},{10,11... | collective-permute-start | bytes 43016 | tf_op jit(solution)/shard_map/ppermute | solution.py:30
  4.6 1.3 %collective-permute-start.1 = (f32[1,4]{1,0:T(1,128)}, f32[1,4]{1,0:T(1,128)S(1)}, u32[]{:S(2)}, u32[]{:S(2)}) collective-permute-start(f32[1,4]{1,0:T(1,128)} %ref.1), channel_id=1, source_target_pairs={{0,1},{1,0},{2,3},{3,2},{4,5},{5,4},{6,7},{7,6},{8,9},{9,8},{10,11... | collective-permute-start | bytes 56 | tf_op jit(solution)/shard_map/ppermute | solution.py:30
  5.9 55.0 %collective-permute-start.12 = (bf16[1000,3584]{1,0:T(8,128)(2,1)}, bf16[1000,3584]{1,0:T(8,128)(2,1)}, u32[]{:S(2)}, u32[]{:S(2)}) collective-permute-start(bf16[1000,3584]{1,0:T(8,128)(2,1)} %wa), channel_id=1, source_target_pairs={{0,1},{1,0},{2,3},{3,2},{4,5},{5,4},{6,7},{7,6},{8,9},{9,8},{10,11... | collective-permute-start | bytes 21504008 | tf_op jit(solution)/shard_map/ppermute | solution.py:30
  6.9 5.6 %collective-permute-start.3 = (bf16[32,448]{1,0:T(8,128)(2,1)S(1)}, bf16[32,448]{1,0:T(8,128)(2,1)S(1)}, u32[]{:S(2)}, u32[]{:S(2)}) collective-permute-start(bf16[32,448]{1,0:T(8,128)(2,1)S(1)} %get-tuple-element.22), channel_id=1, source_target_pairs={{0,4},{2,6},{4,0},{6,2},{8,12},{10,14},{12,8},{14,10},{1,5},{3,7},... | collective-permute-start | bytes 86024 | tf_op jit(solution)/shard_map/ppermute | solution.py:34
  8.2 4.3 %collective-permute-start.2 = (bf16[32,448]{1,0:T(8,128)(2,1)S(1)}, bf16[32,448]{1,0:T(8,128)(2,1)S(1)}, u32[]{:S(2)}, u32[]{:S(2)}) collective-permute-start(bf16[32,448]{1,0:T(8,128)(2,1)S(1)} %get-tuple-element.22), channel_id=1, source_target_pairs={{0,2},{2,0},{4,6},{6,4},{8,10},{10,8},{12,14},{14,12},{1,3},{3,1},... | collective-permute-start | bytes 86024 | tf_op jit(solution)/shard_map/ppermute | solution.py:34
  9.8 4.6 %collective-permute-start.4 = (bf16[32,448]{1,0:T(8,128)(2,1)S(1)}, bf16[32,448]{1,0:T(8,128)(2,1)S(1)}, u32[]{:S(2)}, u32[]{:S(2)}) collective-permute-start(bf16[32,448]{1,0:T(8,128)(2,1)S(1)} %get-tuple-element.22), channel_id=1, source_target_pairs={{0,6},{2,4},{4,2},{6,0},{8,14},{10,12},{12,10},{14,8},{1,7},{3,5},... | collective-permute-start | bytes 86024 | tf_op jit(solution)/shard_map/ppermute | solution.py:34
  14.4 7.9 %copy-start.3 = (bf16[4,32,448]{2,1,0:T(8,128)(2,1)}, bf16[4,32,448]{2,1,0:T(8,128)(2,1)S(1)}, u32[]{:S(2)}) copy-start(bf16[4,32,448]{2,1,0:T(8,128)(2,1)S(1)} %pad_maximum_fusion.1.own4) | copy-start | bytes 344068
  14.4 7.9 %collective-permute-start.5 = (bf16[4,32,448]{2,1,0:T(8,128)(2,1)S(1)}, bf16[4,32,448]{2,1,0:T(8,128)(2,1)S(1)}, u32[]{:S(2)}, u32[]{:S(2)}) collective-permute-start(bf16[4,32,448]{2,1,0:T(8,128)(2,1)S(1)} %pad_maximum_fusion.1.own4), channel_id=1, source_target_pairs={{0,8},{2,10},{4,12},{6,14},{8,0},{10,2},{12,4},{14,6},{1,9},{3,11}... | collective-permute-start | bytes 344072 | tf_op jit(solution)/shard_map/ppermute | solution.py:34
  22.3 0.6 copy-start.4
  24.8 8.7 %collective-permute-start.8 = (bf16[32,3712]{1,0:T(8,128)(2,1)}, bf16[32,3712]{1,0:T(8,128)(2,1)S(1)}, u32[]{:S(2)}, u32[]{:S(2)}) collective-permute-start(bf16[32,3712]{1,0:T(8,128)(2,1)} %assemble.1), channel_id=1, source_target_pairs={{0,192},{1,49},{16,208},{17,33},{32,224},{33,17},{48,240},{49,1},{... | collective-permute-start | bytes 712712 | tf_op jit(solution)/shard_map/ppermute | solution.py:47
  27.5 6.7 %collective-permute-start.7 = (bf16[32,3712]{1,0:T(8,128)(2,1)}, bf16[32,3712]{1,0:T(8,128)(2,1)S(1)}, u32[]{:S(2)}, u32[]{:S(2)}) collective-permute-start(bf16[32,3712]{1,0:T(8,128)(2,1)} %assemble.1), channel_id=1, source_target_pairs={{0,128},{1,33},{16,144},{17,49},{32,160},{33,1},{48,176},{49,17},{... | collective-permute-start | bytes 712712 | tf_op jit(solution)/shard_map/ppermute | solution.py:47
  27.9 6.8 %collective-permute-start.6 = (bf16[32,3712]{1,0:T(8,128)(2,1)}, bf16[32,3712]{1,0:T(8,128)(2,1)S(1)}, u32[]{:S(2)}, u32[]{:S(2)}) collective-permute-start(bf16[32,3712]{1,0:T(8,128)(2,1)} %assemble.1), channel_id=1, source_target_pairs={{0,64},{1,17},{16,80},{17,1},{32,96},{33,49},{48,112},{49,33},{64,... | collective-permute-start | bytes 712712 | tf_op jit(solution)/shard_map/ppermute | solution.py:47
  35.8 24.4 %collective-permute-start.11 = (bf16[4,32,3712]{2,1,0:T(8,128)(2,1)S(1)}, bf16[4,32,3712]{2,1,0:T(8,128)(2,1)S(1)}, u32[]{:S(2)}, u32[]{:S(2)}) collective-permute-start(bf16[4,32,3712]{2,1,0:T(8,128)(2,1)S(1)} %pad_maximum_fusion.q0), channel_id=1, source_target_pairs={{0,48},{1,193},{16,32},{17,209},{32,16},{33,225},{48,0},{49,241},{... | collective-permute-start | bytes 2850824 | tf_op jit(solution)/shard_map/ppermute | solution.py:47
  38.3 21.8 %collective-permute-start.10 = (bf16[4,32,3712]{2,1,0:T(8,128)(2,1)S(1)}, bf16[4,32,3712]{2,1,0:T(8,128)(2,1)S(1)}, u32[]{:S(2)}, u32[]{:S(2)}) collective-permute-start(bf16[4,32,3712]{2,1,0:T(8,128)(2,1)S(1)} %pad_maximum_fusion.q0), channel_id=1, source_target_pairs={{0,32},{1,129},{16,48},{17,145},{32,0},{33,161},{48,16},{49,177},{... | collective-permute-start | bytes 2850824 | tf_op jit(solution)/shard_map/ppermute | solution.py:47
  38.9 22.0 %collective-permute-start.9 = (bf16[4,32,3712]{2,1,0:T(8,128)(2,1)S(1)}, bf16[4,32,3712]{2,1,0:T(8,128)(2,1)}, u32[]{:S(2)}, u32[]{:S(2)}) collective-permute-start(bf16[4,32,3712]{2,1,0:T(8,128)(2,1)S(1)} %pad_maximum_fusion.q0), channel_id=1, source_target_pairs={{0,16},{1,65},{16,0},{17,81},{32,48},{33,97},{48,32},{49,113},{64,... | collective-permute-start | bytes 2850824 | tf_op jit(solution)/shard_map/ppermute | solution.py:47
  60.9 0.6 copy-start
  61.5 3.0 %copy-start.2 = (bf16[1000,3584]{1,0:T(8,128)(2,1)S(1)}, bf16[1000,3584]{1,0:T(8,128)(2,1)}, u32[]{:S(2)}) copy-start(bf16[1000,3584]{1,0:T(8,128)(2,1)} %wa) | copy-start | bytes 21504004
  75.9 37.8 %copy-start.1 = (f32[2,512]{1,0:T(2,128)}, f32[2,512]{1,0:T(2,128)S(1)}, u32[]{:S(2)}) copy-start(f32[2,512]{1,0:T(2,128)S(1)} %get-tuple-element.15.own_stat) | copy-start | bytes 12292
  75.9 3.8 %collective-permute-start.15 = (f32[2,512]{1,0:T(2,128)S(1)}, f32[2,512]{1,0:T(2,128)S(1)}, u32[]{:S(2)}, u32[]{:S(2)}) collective-permute-start(f32[2,512]{1,0:T(2,128)S(1)} %get-tuple-element.14), channel_id=1, source_target_pairs={{0,192},{64,128},{128,64},{192,0},{1,193},{65,129},{129,65},{193,1... | collective-permute-start | bytes 12296 | tf_op jit(solution)/shard_map/ppermute | solution.py:34
  78.4 4.0 %collective-permute-start.14 = (f32[2,512]{1,0:T(2,128)S(1)}, f32[2,512]{1,0:T(2,128)S(1)}, u32[]{:S(2)}, u32[]{:S(2)}) collective-permute-start(f32[2,512]{1,0:T(2,128)S(1)} %get-tuple-element.14), channel_id=1, source_target_pairs={{0,128},{64,192},{128,0},{192,64},{1,129},{65,193},{129,1},{193,65... | collective-permute-start | bytes 12296 | tf_op jit(solution)/shard_map/ppermute | solution.py:34
  78.9 3.4 %collective-permute-start.13 = (f32[2,512]{1,0:T(2,128)S(1)}, f32[2,512]{1,0:T(2,128)S(1)}, u32[]{:S(2)}, u32[]{:S(2)}) collective-permute-start(f32[2,512]{1,0:T(2,128)S(1)} %get-tuple-element.14), channel_id=1, source_target_pairs={{0,64},{64,0},{128,192},{192,128},{1,65},{65,1},{129,193},{193,129... | collective-permute-start | bytes 12296 | tf_op jit(solution)/shard_map/ppermute | solution.py:34
  82.4 3.9 %collective-permute-start.18 = (f32[2,512]{1,0:T(2,128)S(1)}, f32[2,512]{1,0:T(2,128)S(1)}, u32[]{:S(2)}, u32[]{:S(2)}) collective-permute-start(f32[2,512]{1,0:T(2,128)S(1)} %add_add_fusion.2), channel_id=1, source_target_pairs={{0,48},{16,32},{32,16},{48,0},{1,49},{17,33},{33,17},{49,1},{2,50}... | collective-permute-start | bytes 12296 | tf_op jit(solution)/shard_map/ppermute | solution.py:34
  85.3 4.0 %collective-permute-start.17 = (f32[2,512]{1,0:T(2,128)S(1)}, f32[2,512]{1,0:T(2,128)S(1)}, u32[]{:S(2)}, u32[]{:S(2)}) collective-permute-start(f32[2,512]{1,0:T(2,128)S(1)} %add_add_fusion.2), channel_id=1, source_target_pairs={{0,32},{16,48},{32,0},{48,16},{1,33},{17,49},{33,1},{49,17},{2,34}... | collective-permute-start | bytes 12296 | tf_op jit(solution)/shard_map/ppermute | solution.py:34
  85.7 3.6 %collective-permute-start.16 = (f32[2,512]{1,0:T(2,128)S(1)}, f32[2,512]{1,0:T(2,128)S(1)}, u32[]{:S(2)}, u32[]{:S(2)}) collective-permute-start(f32[2,512]{1,0:T(2,128)S(1)} %add_add_fusion.2), channel_id=1, source_target_pairs={{0,16},{16,0},{32,48},{48,32},{1,17},{17,1},{33,49},{49,33},{2,18}... | collective-permute-start | bytes 12296 | tf_op jit(solution)/shard_map/ppermute | solution.py:34
  89.3 4.3 %collective-permute-start.21 = (f32[2,512]{1,0:T(2,128)S(1)}, f32[2,512]{1,0:T(2,128)S(1)}, u32[]{:S(2)}, u32[]{:S(2)}) collective-permute-start(f32[2,512]{1,0:T(2,128)S(1)} %add_add_fusion.1), channel_id=1, source_target_pairs={{0,6},{2,4},{4,2},{6,0},{8,14},{10,12},{12,10},{14,8},{1,7},{3,5},... | collective-permute-start | bytes 12296 | tf_op jit(solution)/shard_map/ppermute | solution.py:34
  90.4 3.4 %collective-permute-start.20 = (f32[2,512]{1,0:T(2,128)S(1)}, f32[2,512]{1,0:T(2,128)S(1)}, u32[]{:S(2)}, u32[]{:S(2)}) collective-permute-start(f32[2,512]{1,0:T(2,128)S(1)} %add_add_fusion.1), channel_id=1, source_target_pairs={{0,4},{2,6},{4,0},{6,2},{8,12},{10,14},{12,8},{14,10},{1,5},{3,7},... | collective-permute-start | bytes 12296 | tf_op jit(solution)/shard_map/ppermute | solution.py:34
  90.4 3.5 %collective-permute-start.19 = (f32[2,512]{1,0:T(2,128)S(1)}, f32[2,512]{1,0:T(2,128)S(1)}, u32[]{:S(2)}, u32[]{:S(2)}) collective-permute-start(f32[2,512]{1,0:T(2,128)S(1)} %add_add_fusion.1), channel_id=1, source_target_pairs={{0,2},{2,0},{4,6},{6,4},{8,10},{10,8},{12,14},{14,12},{1,3},{3,1},... | collective-permute-start | bytes 12296 | tf_op jit(solution)/shard_map/ppermute | solution.py:34
  93.9 15.8 %collective-permute-start.22 = (f32[2,512]{1,0:T(2,128)S(1)}, f32[2,512]{1,0:T(2,128)S(1)}, u32[]{:S(2)}, u32[]{:S(2)}) collective-permute-start(f32[2,512]{1,0:T(2,128)S(1)} %add_add_fusion), channel_id=1, source_target_pairs={{0,8},{2,10},{4,12},{6,14},{8,0},{10,2},{12,4},{14,6},{1,9},{3,11}... | collective-permute-start | bytes 12296 | tf_op jit(solution)/shard_map/ppermute | solution.py:34
  99.2 13.6 %collective-permute-start.24 = (f32[2,512]{1,0:T(2,128)S(1)}, f32[2,512]{1,0:T(2,128)S(1)}, u32[]{:S(2)}, u32[]{:S(2)}) collective-permute-start(f32[2,512]{1,0:T(2,128)S(1)} %get-tuple-element.15.own_stat), channel_id=1, source_target_pairs={{0,1},{1,0},{2,3},{3,2},{4,5},{5,4},{6,7},{7,6},{8,9},{9,8},{10,11... | collective-permute-start | bytes 12296 | tf_op jit(solution)/shard_map/ppermute | solution.py:30
  109.7 3.9 %copy-start.5 = (f32[2,512]{1,0:T(2,128)}, f32[2,512]{1,0:T(2,128)S(1)}, u32[]{:S(2)}) copy-start(f32[2,512]{1,0:T(2,128)S(1)} %add.114.own) | copy-start | bytes 12292
  109.7 3.9 %collective-permute-start.23 = (f32[2,512]{1,0:T(2,128)S(1)}, f32[2,512]{1,0:T(2,128)S(1)}, u32[]{:S(2)}, u32[]{:S(2)}) collective-permute-start(f32[2,512]{1,0:T(2,128)S(1)} %add.114.own), channel_id=1, source_target_pairs={{0,1},{1,0},{2,3},{3,2},{4,5},{5,4},{6,7},{7,6},{8,9},{9,8},{10,11... | collective-permute-start | bytes 12296 | tf_op jit(solution)/shard_map/ppermute | solution.py:30
  112.8 0.8 copy-start.6
  113.6 0.6 copy-start.7

commit v2 on v1

v2 whole, which is shorter than its diff:
```python
import itertools

import jax
import jax.numpy as jnp
from jax import lax
from jax.experimental import pallas as pl
from jax.experimental.pallas import tpu as pltpu
from jax.sharding import Mesh
from jax.sharding import PartitionSpec as P

NX, NY, NZ, NC = 4, 4, 8, 2
DP = ("x", "y")
VOCAB = ("z", "c")
LEN = 32
SEQS = NX * NY
ROWS = SEQS * LEN
D = 3584
PIECE = D // NZ
META = 128
VOCAB_ROWS = 1000
TILE = 256
MIB = 1024 * 1024

kto_beta = 0.1
desirable_weight = 1.0
undesirable_weight = 1.33


def swap_cores(array):
    return lax.ppermute(array, "c", [(0, 1), (1, 0)])


def xor_along(array, axis, k):
    return lax.ppermute(array, axis, [(i, i ^ k) for i in range(lax.axis_size(axis))])


def split_pairs(k, first):
    pairs = []
    for x, y, c in itertools.product(range(NX), range(NY), range(NC)):
        along_x = (c == 0) == first
        u, v = (x ^ k, y) if along_x else (x, y ^ k)
        pairs.append(((x * NY + y) * NC + c, (u * NY + v) * NC + c))
    return pairs


def split_xor(array, k, first):
    return lax.ppermute(array, ("x", "y", "c"), split_pairs(k, first))


def bit_xor(a, b):
    return jnp.bitwise_xor(a, b)


def seq_of(place, far, near):
    x, y, c = place[0], place[1], place[3]
    u = jnp.where(c == 0, bit_xor(x, near), bit_xor(x, far))
    v = jnp.where(c == 0, bit_xor(y, far), bit_xor(y, near))
    return u * NY + v


def fields_kernel(place, m0, m1, m2, m3, meta, table, moved):
    for far, block in enumerate((m0, m1, m2, m3)):
        for near in range(4):
            table[pl.ds(seq_of(place, far, near), 1), :] = block[near]
    rows = table[...]
    partner = rows[:, 2 * LEN : 2 * LEN + 1]
    paired = jnp.zeros_like(rows)
    for s in range(SEQS):
        paired = jnp.where(partner == float(s), rows[s : s + 1], paired)
    moved[...] = paired
    seq = place[0] * NY + place[1]
    own = jnp.where(place[3] == 0, table[pl.ds(seq, 1), :], moved[pl.ds(seq, 1), :])
    label = own.astype(jnp.int32)
    digit = lax.broadcasted_iota(jnp.int32, (META, META), 0)
    digits = jnp.where(
        digit == 0,
        label & 255,
        jnp.where(digit == 1, (label >> 8) & 255, jnp.where(digit == 2, label >> 16, 0)),
    )
    meta[...] = jnp.transpose(digits.astype(jnp.float32))[:LEN].astype(jnp.bfloat16)


def assemble_kernel(place, p0, p1, p2, p3, meta, out):
    z = place[2]
    pieces = (p0, p1, p2, p3)
    for pair in range(NZ // 2):
        halves = []
        for p in (2 * pair, 2 * pair + 1):
            k = bit_xor(z, p)
            low, high = jnp.bitwise_and(k, 3), k // 4
            chosen = pieces[0][high]
            for i in (1, 2, 3):
                chosen = jnp.where(low == i, pieces[i][high], chosen)
            halves.append(chosen)
        out[:, pair * 2 * PIECE : (pair + 1) * 2 * PIECE] = jnp.concatenate(halves, axis=1)
    out[:, D:] = meta[...]


EARLY = ((0, (0, 1)), (0, (2, 3)), (1, (0, 1)), (3, (2, 3)))
LATE = ((1, (2, 3)), (3, (0, 1)), (2, (0, 1)), (2, (2, 3)))
HALF = ROWS // 2


def half_of_rows(place, arrays, wa, wb, rows, target, sums):
    step = pl.program_id(0)

    @pl.when(step == 0)
    def _():
        for i, array in enumerate(arrays):
            for k in range(2):
                rows[(2 * i + k) * LEN : (2 * i + k + 1) * LEN, :] = array[k]
        digits = jnp.transpose(rows[:, D:].astype(jnp.float32))
        value = digits[0:1] + 256.0 * digits[1:2] + 65536.0 * digits[2:3]
        target[...] = value.astype(jnp.int32)
        sums[...] = jnp.zeros_like(sums)

    vocab = step * TILE + lax.broadcasted_iota(jnp.int32, (TILE, HALF), 0)
    valid = vocab < VOCAB_ROWS
    for weight, base in ((wa, place[4]), (wb, place[5])):
        logits = lax.dot_general(
            weight[...],
            rows[:, :D],
            (((1,), (1,)), ((), ())),
            preferred_element_type=jnp.float32,
        )
        sums[0:1] += jnp.sum(jnp.where(valid, jnp.exp(logits), 0.0), axis=0, keepdims=True)
        hit = valid & (vocab + base == target[...])
        sums[1:2] += jnp.sum(jnp.where(hit, logits, 0.0), axis=0, keepdims=True)


def early_kernel(place, q0, q1, q2, q3, wa, wb, out, rows, target, sums):
    half_of_rows(place, (q0, q1, q2, q3), wa, wb, rows, target, sums)

    @pl.when(pl.program_id(0) == pl.num_programs(0) - 1)
    def _():
        out[...] = jnp.transpose(sums[...])


def late_kernel(place, q0, q1, q2, q3, early, ref, wa, wb, out, rows, target, sums, late, whole):
    half_of_rows(place, (q0, q1, q2, q3), wa, wb, rows, target, sums)

    @pl.when(pl.program_id(0) == pl.num_programs(0) - 1)
    def _():
        late[...] = jnp.transpose(sums[...])
        for source, order in ((early, EARLY), (late, LATE)):
            for i, (far, nears) in enumerate(order):
                for k, near in enumerate(nears):
                    start = pl.multiple_of(seq_of(place, far, near) * LEN, LEN)
                    at = (2 * i + k) * LEN
                    whole[pl.ds(start, LEN), :] = source[at : at + LEN, :]
        turned = jnp.transpose(whole[...])
        out[0:1] = turned[0:1]
        out[1:2] = turned[1:2] - ref[...]


def losses_kernel(place, own, other, table, moved, ref, logps, own_loss, loss):
    x, y, z, c = place[0], place[1], place[2], place[3]
    first = c == 0
    lane = lax.broadcasted_iota(jnp.int32, (SEQS, ROWS), 1)
    row = lax.broadcasted_iota(jnp.int32, (SEQS, ROWS), 0)
    inside = lane // LEN == row
    lane = lax.broadcasted_iota(jnp.int32, (SEQS, META), 1)
    picked = []
    sums = []
    for a, b, masks in ((own, other, table), (other, own, moved)):
        partition = jnp.where(first, a[0:1], b[0:1])
        chosen = jnp.where(first, a[1:2], b[1:2])
        mask = jnp.where(lane // LEN == 1, masks[...], 0.0)
        mask = (mask + pltpu.roll(mask, LEN, 1)) + (
            pltpu.roll(mask, 2 * LEN, 1) + pltpu.roll(mask, 3 * LEN, 1)
        )
        weight = jnp.concatenate([mask] * (ROWS // META), axis=1)
        value = chosen - jnp.log(partition)
        picked.append(value)
        sums.append(jnp.sum(jnp.where(inside, weight * value, 0.0), axis=1, keepdims=True))
    desirable = table[:, 2 * LEN + 1 : 2 * LEN + 2]
    logratio, kl_terms = sums
    kl_estimate = jnp.sum(kl_terms, axis=0, keepdims=True) / SEQS
    wanted = desirable_weight * (1.0 - jax.nn.sigmoid(kto_beta * (logratio - kl_estimate)))
    unwanted = undesirable_weight * (1.0 - jax.nn.sigmoid(kto_beta * (kl_estimate - logratio)))
    losses = jnp.where(desirable > 0.5, wanted, unwanted)
    seq = x * NY + y
    here = lax.broadcasted_iota(jnp.int32, (SEQS, 1), 0) == seq
    own_loss[...] = jnp.sum(jnp.where(here, losses, 0.0), axis=0, keepdims=True)
    loss[...] = jnp.sum(losses, axis=0, keepdims=True) / SEQS
    half = jnp.where(z < NZ // 2, picked[0], picked[1])
    start = seq * LEN + (z % (NZ // 2)) * 8 + c * 4
    hit = lax.broadcasted_iota(jnp.int32, (8, ROWS), 1) == (
        start + lax.broadcasted_iota(jnp.int32, (8, ROWS), 0)
    )
    column = jnp.sum(jnp.where(hit, half, 0.0), axis=1, keepdims=True)
    square = lax.broadcasted_iota(jnp.int32, (8, META), 0) == lax.broadcasted_iota(
        jnp.int32, (8, META), 1
    )
    line = jnp.sum(jnp.where(square, column, 0.0), axis=0, keepdims=True)
    logps[...] = line[:, :4] + ref[...]


def whole_block(array):
    zeros = (0,) * array.ndim
    return pl.BlockSpec(array.shape, lambda i: zeros)


def small_call(kernel, name, out_shapes, place, *arrays):
    return pl.pallas_call(
        kernel,
        grid=(1,),
        out_shape=out_shapes,
        in_specs=[pl.BlockSpec(memory_space=pltpu.SMEM)] + [whole_block(a) for a in arrays],
        out_specs=[whole_block(a) for a in out_shapes],
        name=name,
    )(place, *arrays)


def head_call(kernel, name, out_shape, place, arrays, weights, scratch):
    tile = pl.BlockSpec((TILE, D), lambda i: (i, 0))
    return pl.pallas_call(
        kernel,
        grid=(pl.cdiv(VOCAB_ROWS, TILE),),
        out_shape=out_shape,
        in_specs=[pl.BlockSpec(memory_space=pltpu.SMEM)]
        + [whole_block(a) for a in arrays]
        + [tile, tile],
        out_specs=whole_block(out_shape),
        scratch_shapes=[
            pltpu.VMEM((HALF, D + META), jnp.bfloat16),
            pltpu.VMEM((1, HALF), jnp.int32),
            pltpu.VMEM((META, HALF), jnp.float32),
        ]
        + scratch,
        compiler_params=pltpu.CompilerParams(vmem_limit_bytes=24 * MIB),
        cost_estimate=pl.CostEstimate(
            flops=4 * HALF * VOCAB_ROWS * D,
            bytes_accessed=2 * (2 * VOCAB_ROWS + HALF) * D,
            transcendentals=2 * HALF * VOCAB_ROWS,
        ),
        name=name,
    )(place, *arrays, *weights)


def add4(array, parts):
    one, two, three = parts
    return (array + one) + (two + three)


def on_device(hidden, kl_hidden, head_weight, labels, token_mask, kl_pair, desirable, ref_logps):
    x, y, z, c = (lax.axis_index(a) for a in ("x", "y", "z", "c"))
    first = c == 0
    shard = ((x * NY + y) * NZ + z) * NC
    place = jnp.stack(
        [x, y, z, c, (shard + c) * VOCAB_ROWS, (shard + 1 - c) * VOCAB_ROWS]
    ).astype(jnp.int32)

    keep = jnp.where(first, hidden[0], kl_hidden[0])
    give = jnp.where(first, kl_hidden[0], hidden[0])
    came = swap_cores(give)
    ref_came = swap_cores(ref_logps)
    head_weight, came, ref_came = lax.optimization_barrier((head_weight, came, ref_came))
    other_weight = swap_cores(head_weight)
    piece = jnp.concatenate(
        [jnp.where(first, keep, came), jnp.where(first, came, keep)], axis=1
    )

    seq = x * NY + y
    line = jnp.concatenate(
        [labels[0], token_mask[0], kl_pair, desirable, jnp.zeros((META - 2 * LEN - 2,), jnp.int32)]
    ).astype(jnp.float32)[None]
    lines = jnp.stack([line] + [split_xor(line, k, True) for k in (1, 2, 3)])
    groups = [lines] + [split_xor(lines, k, False) for k in (1, 2, 3)]
    f32 = jnp.float32
    table_shape = jax.ShapeDtypeStruct((SEQS, META), f32)
    meta, table, moved = small_call(
        fields_kernel,
        "fields",
        [jax.ShapeDtypeStruct((LEN, META), jnp.bfloat16), table_shape, table_shape],
        place,
        *groups,
    )

    pair_ref = jnp.concatenate(
        [jnp.where(first, ref_logps, ref_came), jnp.where(first, ref_came, ref_logps)], axis=1
    )
    mine = (z // (NZ // 2)) == c
    ref_rows = lax.dynamic_update_slice(
        jnp.zeros((1, ROWS), jnp.float32),
        jnp.where(mine, pair_ref, 0.0),
        (0, seq * LEN + (z % (NZ // 2)) * 8),
    )

    two = jnp.stack([piece, xor_along(piece, "z", 4)])
    pieces = [two] + [xor_along(two, "z", k) for k in (1, 2, 3)]
    (rows,) = small_call(
        assemble_kernel,
        "assemble",
        [jax.ShapeDtypeStruct((LEN, D + META), jnp.bfloat16)],
        place,
        *pieces,
        meta,
    )
    rows, other_weight = lax.optimization_barrier((rows, other_weight))

    came = [split_xor(rows, k, True) for k in (1, 2, 3)]
    near_a = jnp.stack([rows, came[0]])
    near_b = jnp.stack([came[1], came[2]])
    one_a = split_xor(near_a, 1, False)
    three_b = split_xor(near_b, 3, False)
    one_b = split_xor(near_b, 1, False)
    three_a = split_xor(near_a, 3, False)
    two_a = split_xor(one_a, 3, False)
    two_b = split_xor(three_b, 1, False)

    weights = (head_weight, other_weight)
    columns = jax.ShapeDtypeStruct((HALF, META), f32)
    early = head_call(
        early_kernel, "early", columns, place, (near_a, near_b, one_a, three_b), weights, []
    )
    sums = head_call(
        late_kernel,
        "late",
        jax.ShapeDtypeStruct((2, ROWS), f32),
        place,
        (one_b, three_a, two_a, two_b, early, ref_rows),
        weights,
        [pltpu.VMEM((HALF, META), f32), pltpu.VMEM((ROWS, META), f32)],
    )

    sums = add4(sums, [xor_along(sums, "x", k) for k in (1, 2, 3)])
    sums = add4(sums, [xor_along(sums, "y", k) for k in (1, 2, 3)])
    sums = add4(sums, [xor_along(sums, "z", k) for k in (1, 2, 3)])
    sums = sums + xor_along(sums, "z", 4)
    logps, own_loss, loss = small_call(
        losses_kernel,
        "losses",
        [jax.ShapeDtypeStruct(shape, f32) for shape in ((1, 4), (1, 1), (1, 1))],
        place,
        sums,
        swap_cores(sums),
        table,
        moved,
        ref_logps,
    )
    return (logps, own_loss.reshape(1), loss.reshape(()))


def solution(mesh):
    split = Mesh(mesh.devices.reshape(NX, NY, NZ, NC), DP + VOCAB)
    in_specs = (
        P(DP, None, VOCAB),
        P(DP, None, VOCAB),
        P(DP + VOCAB, None),
        P(DP, None),
        P(DP, None),
        P(DP),
        P(DP),
        P(DP, VOCAB),
    )
    out_specs = (P(DP, VOCAB), P(DP), P())
    return jax.shard_map(
        on_device, mesh=split, in_specs=in_specs, out_specs=out_specs, check_vma=False
    )
```

time: 116 us -> 124 us (1.069)
  starting transfers between devices: 47.6 us -> 58.4 us
  waiting for transfers between devices: 40.3 us -> 32.4 us
  Pallas kernels: 14.6 us -> 19.3 us
  local copies, waits for them, and re-layouts: 6.37 us -> 7.81 us
  other arithmetic: 4.74 us -> 3.38 us
    ppermute x6 -> x15, starting transfers between devices: 6.67 us -> 19.3 us  [split_xor(): return lax.ppermute(array, ('x', 'y', 'c'), split_pairs(k, first))]
    ppermute x6 -> x15, waiting for transfers between devices: 27.5 us -> 17.5 us  [split_xor(): return lax.ppermute(array, ('x', 'y', 'c'), split_pairs(k, first))]
    pallas_call x3 -> x5, Pallas kernels: 14.6 us -> 19.3 us  [the longest x2 14.3 us: head_call(): pl.pallas_call(kernel, grid=(pl.cdiv(VOCAB_ROWS, TILE),), out_shape=out_s...]
    ppermute x14, starting transfers between devices: 23.8 us -> 21.7 us  [xor_along(): lax.ppermute(array, axis, [(i, i ^ k) for i in range(lax.axis_size(axis))])]
    ppermute x14, waiting for transfers between devices: 10.8 us -> 12.9 us  [xor_along(): lax.ppermute(array, axis, [(i, i ^ k) for i in range(lax.axis_size(axis))])]
    concatenate x0 -> x2, local copies, waits for them, and re-layouts: none -> 1.53 us  [on_device(): jnp.concatenate([labels[0], token_mask[0], kl_pair, desirable, jnp.zeros(...]
    another operation x5, other arithmetic: 2.52 us -> 1.14 us  [the longest x1 0.99 us: on_device(): near_a = jnp.stack([rows, came[0]])]
    unnamed x16 -> x24, local copies, waits for them, and re-layouts: 4.89 us -> 5.52 us
  transfers between devices with their start and end apart: 25 -> 33, of which waited for: 16 -> 16; matrix products, arithmetic and copies ran while one was open for 5% -> 4% of each run, Pallas kernels for 2% -> 9%
where the time goes in v2:
time: 124 us; the launch traced here: 123 us
  starting transfers between devices  58.4 us (47%)
  waiting for transfers between devices  32.4 us (26%)
  Pallas kernels  19.3 us (16%)
  local copies, waits for them, and re-layouts  7.81 us (6%)
  other arithmetic  3.38 us (3%)
  between operations  2.15 us (2%)
    ppermute x14, starting transfers between devices, xor_along(): lax.ppermute(array, axis, [(i, i ^ k) for i in range(lax.axis_size(axis))])  21.7 us
    ppermute x15, starting transfers between devices, split_xor(): return lax.ppermute(array, ('x', 'y', 'c'), split_pairs(k, first))  19.3 us
    ppermute x15, waiting for transfers between devices, split_xor(): return lax.ppermute(array, ('x', 'y', 'c'), split_pairs(k, first))  17.5 us
    ppermute x4, starting transfers between devices, swap_cores(): return lax.ppermute(array, 'c', [(0, 1), (1, 0)])  17.4 us
    pallas_call x2, Pallas kernels, head_call(): pl.pallas_call(kernel, grid=(pl.cdiv(VOCAB_ROWS, TILE),), out_shape=out_s...  14.3 us
    ppermute x14, waiting for transfers between devices, xor_along(): lax.ppermute(array, axis, [(i, i ^ k) for i in range(lax.axis_size(axis))])  12.9 us
    unnamed x24, local copies, waits for them, and re-layouts  5.52 us
    pallas_call x3, Pallas kernels, small_call(): pl.pallas_call(kernel, grid=(1,), out_shape=out_shapes, in_specs=[pl.Bloc...  4.95 us
  transfers between devices with their start and end apart: 33, of which 16 were waited for; matrix products, arithmetic and copies ran while one was open for 4% of the time, Pallas kernels for 9%

profile of v2, /device:TPU:1, one launch (start us, length us, event | category | flops | bytes accessed | tf_op | source)
XLA Modules:
  0.0 123.4 jit_solution(9304747488090497563)
XLA Ops:
  0.6 0.7 select_bitcast_fusion
  1.4 3.2 %collective-permute-start = (bf16[32,224]{1,0:T(8,128)(2,1)S(1)}, bf16[32,224]{1,0:T(8,128)(2,1)S(1)}, u32[]{:S(2)}, u32[]{:S(2)}) collective-permute-start(bf16[32,224]{1,0:T(8,128)(2,1)S(1)} %select_bitcast_fusion), channel_id=1, source_target_pairs={{0,1},{1,0},{2,3},{3,2},{4,5},{5,4},{6,7},{7,6},{8,9},{9,8},{10,11... | collective-permute-start | bytes 43016 | tf_op jit(solution)/shard_map/ppermute | solution.py:30
  4.6 0.1 collective-permute-start.1
  4.7 1.2 collective-permute-done.1
  5.9 0.2 collective-permute-start.12
  6.1 0.7 bitcast_select_fusion.1
  6.8 0.1 fusion
  6.9 5.2 %collective-permute-start.2 = (bf16[32,448]{1,0:T(8,128)(2,1)S(1)}, bf16[32,448]{1,0:T(8,128)(2,1)S(1)}, u32[]{:S(2)}, u32[]{:S(2)}) collective-permute-start(bf16[32,448]{1,0:T(8,128)(2,1)S(1)} %get-tuple-element.28), channel_id=1, source_target_pairs={{0,8},{2,10},{4,12},{6,14},{8,0},{10,2},{12,4},{14,6},{1,9},{3,11}... | collective-permute-start | bytes 86024 | tf_op jit(solution)/shard_map/ppermute | solution.py:34
  13.4 0.8 concatenate.53
  14.2 1.4 %collective-permute-start.6 = (f32[1,128]{1,0:T(1,128)S(1)}, f32[1,128]{1,0:T(1,128)S(1)}, u32[]{:S(2)}, u32[]{:S(2)}) collective-permute-start(f32[1,128]{1,0:T(1,128)S(1)} %convert_element_type.20), channel_id=1, source_target_pairs={{0,64},{1,17},{16,80},{17,1},{32,96},{33,49},{48,112},{49,33},{64,... | collective-permute-start | bytes 1544 | tf_op jit(solution)/shard_map/ppermute | solution.py:47
  15.5 2.6 %collective-permute-start.7 = (f32[1,128]{1,0:T(1,128)S(1)}, f32[1,128]{1,0:T(1,128)S(1)}, u32[]{:S(2)}, u32[]{:S(2)}) collective-permute-start(f32[1,128]{1,0:T(1,128)S(1)} %convert_element_type.20), channel_id=1, source_target_pairs={{0,128},{1,33},{16,144},{17,49},{32,160},{33,1},{48,176},{49,17},{... | collective-permute-start | bytes 1544 | tf_op jit(solution)/shard_map/ppermute | solution.py:47
  18.2 0.8 concatenate.50
  19.0 0.8 collective-permute-start.3
  19.8 1.2 collective-permute-start.4
  21.0 1.6 %collective-permute-start.5 = (bf16[2,32,448]{2,1,0:T(8,128)(2,1)S(1)}, bf16[2,32,448]{2,1,0:T(8,128)(2,1)S(1)}, u32[]{:S(2)}, u32[]{:S(2)}) collective-permute-start(bf16[2,32,448]{2,1,0:T(8,128)(2,1)S(1)} %pad_maximum_fusion.2.p0), channel_id=1, source_target_pairs={{0,6},{2,4},{4,2},{6,0},{8,14},{10,12},{12,10},{14,8},{1,7},{3,5},... | collective-permute-start | bytes 172040 | tf_op jit(solution)/shard_map/ppermute | solution.py:34
  22.6 2.8 %collective-permute-start.10 = (f32[4,1,128]{2,1,0:T(1,128)S(1)}, f32[4,1,128]{2,1,0:T(1,128)S(1)}, u32[]{:S(2)}, u32[]{:S(2)}) collective-permute-start(f32[4,1,128]{2,1,0:T(1,128)S(1)} %pad_maximum_fusion.4.m0), channel_id=1, source_target_pairs={{0,32},{1,129},{16,48},{17,145},{32,0},{33,161},{48,16},{49,177},{... | collective-permute-start | bytes 6152 | tf_op jit(solution)/shard_map/ppermute | solution.py:47
  25.5 1.2 collective-permute-done.10.m2
  26.7 2.5 %collective-permute-start.11 = (f32[4,1,128]{2,1,0:T(1,128)S(1)}, f32[4,1,128]{2,1,0:T(1,128)S(1)}, u32[]{:S(2)}, u32[]{:S(2)}) collective-permute-start(f32[4,1,128]{2,1,0:T(1,128)S(1)} %pad_maximum_fusion.4.m0), channel_id=1, source_target_pairs={{0,48},{1,193},{16,32},{17,209},{32,16},{33,225},{48,0},{49,241},{... | collective-permute-start | bytes 6152 | tf_op jit(solution)/shard_map/ppermute | solution.py:47
  29.1 1.2 collective-permute-done.11.m3
  30.3 0.3 collective-permute-start.9
  30.6 0.7 stack.66.place
  31.3 1.5 %collective-permute-done.9.m1 = f32[4,1,128]{2,1,0:T(1,128)S(1)} collective-permute-done((f32[4,1,128]{2,1,0:T(1,128)S(1)}, f32[4,1,128]{2,1,0:T(1,128)S(1)}, u32[]{:S(2)}, u32[]{:S(2)}) %collective-permute-start.9) | collective-permute-done | bytes 2080 | tf_op jit(solution)/shard_map/ppermute | solution.py:47
  32.8 0.6 copy-done.11
  33.3 1.6 %fields.1 = (bf16[32,128]{1,0:T(8,128)(2,1)}, f32[16,128]{1,0:T(8,128)}, f32[16,128]{1,0:T(8,128)}) custom-call(s32[6]{0:T(128)} %stack.66.place, f32[4,1,128]{2,1,0:T(1,128)} %copy-done.7, f32[4,1,128]{2,1,0:T(1,128)} %copy-done.11, f32[4,1,128]{2,1,0:T(1,128)} %copy-done.9, f32[4,1,128]{2,1,0:T(1,128)} %copy-done.10), custom_call_target="tpu_custom_call" | custom-call | tf_op jit(solution)/shard_map/fields/pallas_call | solution.py:205
  35.0 0.6 copy-done.3
  35.7 1.8 %assemble.1 = bf16[32,3712]{1,0:T(8,128)(2,1)} custom-call(s32[6]{0:T(128)} %stack.66.place, bf16[2,32,448]{2,1,0:T(8,128)(2,1)} %copy-done.2, bf16[2,32,448]{2,1,0:T(8,128)(2,1)} %copy-done.3, bf16[2,32,448]{2,1,0:T(8,128)(2,1)} %copy-done.4, bf16[2,32,448]{2,1,0:T(8,128)(2,1)} %copy-done.5, bf16[32,128]{1,0:T(8,128)(2,1)} %get-tuple-element.15.meta), custom_call_target="tpu_custom_call" | custom-call | tf_op jit(solution)/shard_map/assemble/pallas_call | solution.py:205
  37.5 3.8 %collective-permute-start.13 = (bf16[32,3712]{1,0:T(8,128)(2,1)}, bf16[32,3712]{1,0:T(8,128)(2,1)S(1)}, u32[]{:S(2)}, u32[]{:S(2)}) collective-permute-start(bf16[32,3712]{1,0:T(8,128)(2,1)} %assemble.1), channel_id=1, source_target_pairs={{0,128},{1,33},{16,144},{17,49},{32,160},{33,1},{48,176},{49,17},{... | collective-permute-start | bytes 712712 | tf_op jit(solution)/shard_map/ppermute | solution.py:47
  41.3 1.3 %collective-permute-done.16 = bf16[32,3712]{1,0:T(8,128)(2,1)S(1)} collective-permute-done((bf16[32,3712]{1,0:T(8,128)(2,1)}, bf16[32,3712]{1,0:T(8,128)(2,1)S(1)}, u32[]{:S(2)}, u32[]{:S(2)}) %collective-permute-start.16) | collective-permute-done | bytes 237600 | tf_op jit(solution)/shard_map/ppermute | solution.py:47
  42.6 1.0 pad_maximum_fusion.1.q0
  43.6 0.4 collective-permute-start.18
  44.0 3.7 %collective-permute-done.13 = bf16[32,3712]{1,0:T(8,128)(2,1)S(1)} collective-permute-done((bf16[32,3712]{1,0:T(8,128)(2,1)}, bf16[32,3712]{1,0:T(8,128)(2,1)S(1)}, u32[]{:S(2)}, u32[]{:S(2)}) %collective-permute-start.13) | collective-permute-done | bytes 237600 | tf_op jit(solution)/shard_map/ppermute | solution.py:47
  47.6 2.4 %collective-permute-done.14 = bf16[32,3712]{1,0:T(8,128)(2,1)S(1)} collective-permute-done((bf16[32,3712]{1,0:T(8,128)(2,1)}, bf16[32,3712]{1,0:T(8,128)(2,1)S(1)}, u32[]{:S(2)}, u32[]{:S(2)}) %collective-permute-start.14) | collective-permute-done | bytes 237600 | tf_op jit(solution)/shard_map/ppermute | solution.py:47
  50.1 2.9 %collective-permute-start.20 = (bf16[2,32,3712]{2,1,0:T(8,128)(2,1)S(1)}, bf16[2,32,3712]{2,1,0:T(8,128)(2,1)}, u32[]{:S(2)}, u32[]{:S(2)}) collective-permute-start(bf16[2,32,3712]{2,1,0:T(8,128)(2,1)S(1)} %pad_maximum_fusion.q1), channel_id=1, source_target_pairs={{0,48},{1,193},{16,32},{17,209},{32,16},{33,225},{48,0},{49,241},{... | collective-permute-start | bytes 1425416 | tf_op jit(solution)/shard_map/ppermute | solution.py:47
  53.0 0.1 collective-permute-start.17
  53.1 3.4 %collective-permute-done.18.q2 = bf16[2,32,3712]{2,1,0:T(8,128)(2,1)S(1)} collective-permute-done((bf16[2,32,3712]{2,1,0:T(8,128)(2,1)S(1)}, bf16[2,32,3712]{2,1,0:T(8,128)(2,1)S(1)}, u32[]{:S(2)}, u32[]{:S(2)}) %collective-permute-start.18) | collective-permute-done | bytes 475168 | tf_op jit(solution)/shard_map/ppermute | solution.py:47
  56.5 2.5 %collective-permute-start.19 = (bf16[2,32,3712]{2,1,0:T(8,128)(2,1)S(1)}, bf16[2,32,3712]{2,1,0:T(8,128)(2,1)S(1)}, u32[]{:S(2)}, u32[]{:S(2)}) collective-permute-start(bf16[2,32,3712]{2,1,0:T(8,128)(2,1)S(1)} %collective-permute-done.18.q2), channel_id=1, source_target_pairs={{0,48},{1,193},{16,32},{17,209},{32,16},{33,225},{48,0},{49,241},{... | collective-permute-start | bytes 1425416 | tf_op jit(solution)/shard_map/ppermute | solution.py:47
  59.0 2.9 %collective-permute-done.20.q3 = bf16[2,32,3712]{2,1,0:T(8,128)(2,1)} collective-permute-done((bf16[2,32,3712]{2,1,0:T(8,128)(2,1)S(1)}, bf16[2,32,3712]{2,1,0:T(8,128)(2,1)}, u32[]{:S(2)}, u32[]{:S(2)}) %collective-permute-start.20) | collective-permute-done | bytes 475168 | tf_op jit(solution)/shard_map/ppermute | solution.py:47
  61.9 0.7 broadcast_select_fusion.2
  62.6 0.1 broadcast_select_fusion.3
  62.6 0.1 dynamic_update_slice.3.ref
  62.8 3.0 %copy-done = bf16[1000,3584]{1,0:T(8,128)(2,1)S(1)} copy-done((bf16[1000,3584]{1,0:T(8,128)(2,1)S(1)}, bf16[1000,3584]{1,0:T(8,128)(2,1)}, u32[]{:S(2)}) %copy-start) | copy-done | bytes 7168024
  65.8 0.7 copy-done.1
  66.4 7.1 %early.1 = f32[256,128]{1,0:T(8,128)S(1)} custom-call(s32[6]{0:T(128)S(1)} %copy-done.1, bf16[2,32,3712]{2,1,0:T(8,128)(2,1)S(1)} %pad_maximum_fusion.1.q0, bf16[2,32,3712]{2,1,0:T(8,128)(2,1)S(1)} %pad_maximum_fusion.q1, bf16[2,32,3712]{2,1,0:T(8,128)(2,1)S(1)} %collective-permute-done.18.q2, bf16[2,32,3712]{2,1,0:T(8,128)(2,1)} %collective-permute-done.20.q3, ...), custom_call_target="tpu_custom_call" | custom-call | flops 3670016000 | bytes 16171008 | tf_op jit(solution)/shard_map/early/pallas_call | solution.py:217
  73.6 7.2 %late.1 = f32[2,512]{1,0:T(2,128)S(1)} custom-call(s32[6]{0:T(128)S(1)} %copy-done.1, bf16[2,32,3712]{2,1,0:T(8,128)(2,1)S(1)} %collective-permute-done.15.q0, bf16[2,32,3712]{2,1,0:T(8,128)(2,1)S(1)} %collective-permute-done.17.q1, bf16[2,32,3712]{2,1,0:T(8,128)(2,1)S(1)} %collective-permute-done.19.q2, ...), custom_call_target="tpu_custom_call" | custom-call | flops 3670016000 | bytes 16171008 | tf_op jit(solution)/shard_map/late/pallas_call | solution.py:217
  80.8 1.5 %collective-permute-start.22 = (f32[2,512]{1,0:T(2,128)S(1)}, f32[2,512]{1,0:T(2,128)S(1)}, u32[]{:S(2)}, u32[]{:S(2)}) collective-permute-start(f32[2,512]{1,0:T(2,128)S(1)} %late.1), channel_id=1, source_target_pairs={{0,64},{64,0},{128,192},{192,128},{1,65},{65,1},{129,193},{193,129... | collective-permute-start | bytes 12296 | tf_op jit(solution)/shard_map/ppermute | solution.py:34
  82.3 0.8 collective-permute-start.23
  83.2 1.7 %collective-permute-start.24 = (f32[2,512]{1,0:T(2,128)S(1)}, f32[2,512]{1,0:T(2,128)S(1)}, u32[]{:S(2)}, u32[]{:S(2)}) collective-permute-start(f32[2,512]{1,0:T(2,128)S(1)} %late.1), channel_id=1, source_target_pairs={{0,192},{64,128},{128,64},{192,0},{1,193},{65,129},{129,65},{193,1... | collective-permute-start | bytes 12296 | tf_op jit(solution)/shard_map/ppermute | solution.py:34
  84.8 1.5 %collective-permute-done.23 = f32[2,512]{1,0:T(2,128)S(1)} collective-permute-done((f32[2,512]{1,0:T(2,128)S(1)}, f32[2,512]{1,0:T(2,128)S(1)}, u32[]{:S(2)}, u32[]{:S(2)}) %collective-permute-start.23) | collective-permute-done | bytes 4128 | tf_op jit(solution)/shard_map/ppermute | solution.py:34
  86.3 0.5 collective-permute-done.24
  86.8 0.1 collective-permute-start.25
  86.9 3.2 %collective-permute-start.26 = (f32[2,512]{1,0:T(2,128)S(1)}, f32[2,512]{1,0:T(2,128)S(1)}, u32[]{:S(2)}, u32[]{:S(2)}) collective-permute-start(f32[2,512]{1,0:T(2,128)S(1)} %add_add_fusion.2), channel_id=1, source_target_pairs={{0,32},{16,48},{32,0},{48,16},{1,33},{17,49},{33,1},{49,17},{2,34}... | collective-permute-start | bytes 12296 | tf_op jit(solution)/shard_map/ppermute | solution.py:34
  90.2 0.6 collective-permute-start.27
  90.8 0.4 collective-permute-done.26
  91.2 2.6 %collective-permute-done.27 = f32[2,512]{1,0:T(2,128)S(1)} collective-permute-done((f32[2,512]{1,0:T(2,128)S(1)}, f32[2,512]{1,0:T(2,128)S(1)}, u32[]{:S(2)}, u32[]{:S(2)}) %collective-permute-start.27) | collective-permute-done | bytes 4128 | tf_op jit(solution)/shard_map/ppermute | solution.py:34
  93.8 0.1 collective-permute-start.28
  93.9 1.9 %collective-permute-start.29 = (f32[2,512]{1,0:T(2,128)S(1)}, f32[2,512]{1,0:T(2,128)S(1)}, u32[]{:S(2)}, u32[]{:S(2)}) collective-permute-start(f32[2,512]{1,0:T(2,128)S(1)} %add_add_fusion.1), channel_id=1, source_target_pairs={{0,4},{2,6},{4,0},{6,2},{8,12},{10,14},{12,8},{14,10},{1,5},{3,7},... | collective-permute-start | bytes 12296 | tf_op jit(solution)/shard_map/ppermute | solution.py:34
  95.8 1.6 %collective-permute-start.30 = (f32[2,512]{1,0:T(2,128)S(1)}, f32[2,512]{1,0:T(2,128)S(1)}, u32[]{:S(2)}, u32[]{:S(2)}) collective-permute-start(f32[2,512]{1,0:T(2,128)S(1)} %add_add_fusion.1), channel_id=1, source_target_pairs={{0,6},{2,4},{4,2},{6,0},{8,14},{10,12},{12,10},{14,8},{1,7},{3,5},... | collective-permute-start | bytes 12296 | tf_op jit(solution)/shard_map/ppermute | solution.py:34
  97.5 2.6 %collective-permute-done.30 = f32[2,512]{1,0:T(2,128)S(1)} collective-permute-done((f32[2,512]{1,0:T(2,128)S(1)}, f32[2,512]{1,0:T(2,128)S(1)}, u32[]{:S(2)}, u32[]{:S(2)}) %collective-permute-start.30) | collective-permute-done | bytes 4128 | tf_op jit(solution)/shard_map/ppermute | solution.py:34
  100.1 1.2 collective-permute-start.31
  101.3 5.2 %collective-permute-done.31 = f32[2,512]{1,0:T(2,128)S(1)} collective-permute-done((f32[2,512]{1,0:T(2,128)S(1)}, f32[2,512]{1,0:T(2,128)S(1)}, u32[]{:S(2)}, u32[]{:S(2)}) %collective-permute-start.31) | collective-permute-done | bytes 4128 | tf_op jit(solution)/shard_map/ppermute | solution.py:34
  106.6 13.8 %collective-permute-start.32 = (f32[2,512]{1,0:T(2,128)S(1)}, f32[2,512]{1,0:T(2,128)S(1)}, u32[]{:S(2)}, u32[]{:S(2)}) collective-permute-start(f32[2,512]{1,0:T(2,128)S(1)} %add.70.own), channel_id=1, source_target_pairs={{0,1},{1,0},{2,3},{3,2},{4,5},{5,4},{6,7},{7,6},{8,9},{9,8},{10,11... | collective-permute-start | bytes 12296 | tf_op jit(solution)/shard_map/ppermute | solution.py:30
  120.4 0.8 collective-permute-done.32.other
  121.2 0.6 copy-done.8
  121.8 1.6 %losses.1 = (f32[1,4]{1,0:T(1,128)}, f32[1,1]{1,0:T(1,128)}, f32[1,1]{1,0:T(1,128)}) custom-call(s32[6]{0:T(128)} %stack.66.place, f32[2,512]{1,0:T(2,128)} %copy-done.6, f32[2,512]{1,0:T(2,128)} %copy-done.8, f32[16,128]{1,0:T(8,128)} %get-tuple-element.20.table, f32[16,128]{1,0:T(8,128)} %get-tuple-element.21.moved, f32[1,4]{1,0:T(1,128)} %ref.1), custom_call_target="tpu_custom_call" | custom-call | tf_op jit(solution)/shard_map/losses/pallas_call | solution.py:205
  (53 shorter events, 0.3 us)
Async XLA Ops:
  1.4 4.5 %collective-permute-start = (bf16[32,224]{1,0:T(8,128)(2,1)S(1)}, bf16[32,224]{1,0:T(8,128)(2,1)S(1)}, u32[]{:S(2)}, u32[]{:S(2)}) collective-permute-start(bf16[32,224]{1,0:T(8,128)(2,1)S(1)} %select_bitcast_fusion), channel_id=1, source_target_pairs={{0,1},{1,0},{2,3},{3,2},{4,5},{5,4},{6,7},{7,6},{8,9},{9,8},{10,11... | collective-permute-start | bytes 43016 | tf_op jit(solution)/shard_map/ppermute | solution.py:30
  4.6 1.3 %collective-permute-start.1 = (f32[1,4]{1,0:T(1,128)}, f32[1,4]{1,0:T(1,128)S(1)}, u32[]{:S(2)}, u32[]{:S(2)}) collective-permute-start(f32[1,4]{1,0:T(1,128)} %ref.1), channel_id=1, source_target_pairs={{0,1},{1,0},{2,3},{3,2},{4,5},{5,4},{6,7},{7,6},{8,9},{9,8},{10,11... | collective-permute-start | bytes 56 | tf_op jit(solution)/shard_map/ppermute | solution.py:30
  5.9 31.6 %collective-permute-start.12 = (bf16[1000,3584]{1,0:T(8,128)(2,1)}, bf16[1000,3584]{1,0:T(8,128)(2,1)}, u32[]{:S(2)}, u32[]{:S(2)}) collective-permute-start(bf16[1000,3584]{1,0:T(8,128)(2,1)} %wa.1), channel_id=1, source_target_pairs={{0,1},{1,0},{2,3},{3,2},{4,5},{5,4},{6,7},{7,6},{8,9},{9,8},{10,11... | collective-permute-start | bytes 21504008 | tf_op jit(solution)/shard_map/ppermute | solution.py:30
  6.9 12.1 %collective-permute-start.2 = (bf16[32,448]{1,0:T(8,128)(2,1)S(1)}, bf16[32,448]{1,0:T(8,128)(2,1)S(1)}, u32[]{:S(2)}, u32[]{:S(2)}) collective-permute-start(bf16[32,448]{1,0:T(8,128)(2,1)S(1)} %get-tuple-element.28), channel_id=1, source_target_pairs={{0,8},{2,10},{4,12},{6,14},{8,0},{10,2},{12,4},{14,6},{1,9},{3,11}... | collective-permute-start | bytes 86024 | tf_op jit(solution)/shard_map/ppermute | solution.py:34
  14.2 5.6 %collective-permute-start.6 = (f32[1,128]{1,0:T(1,128)S(1)}, f32[1,128]{1,0:T(1,128)S(1)}, u32[]{:S(2)}, u32[]{:S(2)}) collective-permute-start(f32[1,128]{1,0:T(1,128)S(1)} %convert_element_type.20), channel_id=1, source_target_pairs={{0,64},{1,17},{16,80},{17,1},{32,96},{33,49},{48,112},{49,33},{64,... | collective-permute-start | bytes 1544 | tf_op jit(solution)/shard_map/ppermute | solution.py:47
  15.5 5.5 %collective-permute-start.7 = (f32[1,128]{1,0:T(1,128)S(1)}, f32[1,128]{1,0:T(1,128)S(1)}, u32[]{:S(2)}, u32[]{:S(2)}) collective-permute-start(f32[1,128]{1,0:T(1,128)S(1)} %convert_element_type.20), channel_id=1, source_target_pairs={{0,128},{1,33},{16,144},{17,49},{32,160},{33,1},{48,176},{49,17},{... | collective-permute-start | bytes 1544 | tf_op jit(solution)/shard_map/ppermute | solution.py:47
  18.2 4.5 %collective-permute-start.8 = (f32[1,128]{1,0:T(1,128)S(1)}, f32[1,128]{1,0:T(1,128)S(1)}, u32[]{:S(2)}, u32[]{:S(2)}) collective-permute-start(f32[1,128]{1,0:T(1,128)S(1)} %convert_element_type.20), channel_id=1, source_target_pairs={{0,192},{1,49},{16,208},{17,33},{32,224},{33,17},{48,240},{49,1},{... | collective-permute-start | bytes 1544 | tf_op jit(solution)/shard_map/ppermute | solution.py:47
  19.0 16.1 %copy-start.2 = (bf16[2,32,448]{2,1,0:T(8,128)(2,1)}, bf16[2,32,448]{2,1,0:T(8,128)(2,1)S(1)}, u32[]{:S(2)}) copy-start(bf16[2,32,448]{2,1,0:T(8,128)(2,1)S(1)} %pad_maximum_fusion.2.p0) | copy-start | bytes 172036
  19.0 16.0 %collective-permute-start.3 = (bf16[2,32,448]{2,1,0:T(8,128)(2,1)S(1)}, bf16[2,32,448]{2,1,0:T(8,128)(2,1)S(1)}, u32[]{:S(2)}, u32[]{:S(2)}) collective-permute-start(bf16[2,32,448]{2,1,0:T(8,128)(2,1)S(1)} %pad_maximum_fusion.2.p0), channel_id=1, source_target_pairs={{0,2},{2,0},{4,6},{6,4},{8,10},{10,8},{12,14},{14,12},{1,3},{3,1},... | collective-permute-start | bytes 172040 | tf_op jit(solution)/shard_map/ppermute | solution.py:34
  19.8 15.2 %collective-permute-start.4 = (bf16[2,32,448]{2,1,0:T(8,128)(2,1)S(1)}, bf16[2,32,448]{2,1,0:T(8,128)(2,1)S(1)}, u32[]{:S(2)}, u32[]{:S(2)}) collective-permute-start(bf16[2,32,448]{2,1,0:T(8,128)(2,1)S(1)} %pad_maximum_fusion.2.p0), channel_id=1, source_target_pairs={{0,4},{2,6},{4,0},{6,2},{8,12},{10,14},{12,8},{14,10},{1,5},{3,7},... | collective-permute-start | bytes 172040 | tf_op jit(solution)/shard_map/ppermute | solution.py:34
  21.0 14.0 %collective-permute-start.5 = (bf16[2,32,448]{2,1,0:T(8,128)(2,1)S(1)}, bf16[2,32,448]{2,1,0:T(8,128)(2,1)S(1)}, u32[]{:S(2)}, u32[]{:S(2)}) collective-permute-start(bf16[2,32,448]{2,1,0:T(8,128)(2,1)S(1)} %pad_maximum_fusion.2.p0), channel_id=1, source_target_pairs={{0,6},{2,4},{4,2},{6,0},{8,14},{10,12},{12,10},{14,8},{1,7},{3,5},... | collective-permute-start | bytes 172040 | tf_op jit(solution)/shard_map/ppermute | solution.py:34
  22.6 10.1 %copy-start.7 = (f32[4,1,128]{2,1,0:T(1,128)}, f32[4,1,128]{2,1,0:T(1,128)S(1)}, u32[]{:S(2)}) copy-start(f32[4,1,128]{2,1,0:T(1,128)S(1)} %pad_maximum_fusion.4.m0) | copy-start | bytes 6148
  22.6 4.0 %collective-permute-start.10 = (f32[4,1,128]{2,1,0:T(1,128)S(1)}, f32[4,1,128]{2,1,0:T(1,128)S(1)}, u32[]{:S(2)}, u32[]{:S(2)}) collective-permute-start(f32[4,1,128]{2,1,0:T(1,128)S(1)} %pad_maximum_fusion.4.m0), channel_id=1, source_target_pairs={{0,32},{1,129},{16,48},{17,145},{32,0},{33,161},{48,16},{49,177},{... | collective-permute-start | bytes 6152 | tf_op jit(solution)/shard_map/ppermute | solution.py:47
  26.7 6.1 %copy-start.9 = (f32[4,1,128]{2,1,0:T(1,128)}, f32[4,1,128]{2,1,0:T(1,128)S(1)}, u32[]{:S(2)}) copy-start(f32[4,1,128]{2,1,0:T(1,128)S(1)} %collective-permute-done.10.m2) | copy-start | bytes 6148
  26.7 3.6 %collective-permute-start.11 = (f32[4,1,128]{2,1,0:T(1,128)S(1)}, f32[4,1,128]{2,1,0:T(1,128)S(1)}, u32[]{:S(2)}, u32[]{:S(2)}) collective-permute-start(f32[4,1,128]{2,1,0:T(1,128)S(1)} %pad_maximum_fusion.4.m0), channel_id=1, source_target_pairs={{0,48},{1,193},{16,32},{17,209},{32,16},{33,225},{48,0},{49,241},{... | collective-permute-start | bytes 6152 | tf_op jit(solution)/shard_map/ppermute | solution.py:47
  30.3 2.4 %copy-start.10 = (f32[4,1,128]{2,1,0:T(1,128)}, f32[4,1,128]{2,1,0:T(1,128)S(1)}, u32[]{:S(2)}) copy-start(f32[4,1,128]{2,1,0:T(1,128)S(1)} %collective-permute-done.11.m3) | copy-start | bytes 6148
  30.3 2.4 %collective-permute-start.9 = (f32[4,1,128]{2,1,0:T(1,128)S(1)}, f32[4,1,128]{2,1,0:T(1,128)S(1)}, u32[]{:S(2)}, u32[]{:S(2)}) collective-permute-start(f32[4,1,128]{2,1,0:T(1,128)S(1)} %pad_maximum_fusion.4.m0), channel_id=1, source_target_pairs={{0,16},{1,65},{16,0},{17,81},{32,48},{33,97},{48,32},{49,113},{64,... | collective-permute-start | bytes 6152 | tf_op jit(solution)/shard_map/ppermute | solution.py:47
  32.8 0.6 copy-start.11
  35.0 0.6 copy-start.3
  35.0 0.7 copy-start.4
  35.0 0.7 copy-start.5
  37.4 5.2 %collective-permute-start.16 = (bf16[32,3712]{1,0:T(8,128)(2,1)}, bf16[32,3712]{1,0:T(8,128)(2,1)S(1)}, u32[]{:S(2)}, u32[]{:S(2)}) collective-permute-start(bf16[32,3712]{1,0:T(8,128)(2,1)} %assemble.1), channel_id=1, source_target_pairs={{0,64},{1,17},{16,80},{17,1},{32,96},{33,49},{48,112},{49,33},{64,... | collective-permute-start | bytes 712712 | tf_op jit(solution)/shard_map/ppermute | solution.py:47
  37.5 10.2 %collective-permute-start.13 = (bf16[32,3712]{1,0:T(8,128)(2,1)}, bf16[32,3712]{1,0:T(8,128)(2,1)S(1)}, u32[]{:S(2)}, u32[]{:S(2)}) collective-permute-start(bf16[32,3712]{1,0:T(8,128)(2,1)} %assemble.1), channel_id=1, source_target_pairs={{0,128},{1,33},{16,144},{17,49},{32,160},{33,1},{48,176},{49,17},{... | collective-permute-start | bytes 712712 | tf_op jit(solution)/shard_map/ppermute | solution.py:47
  41.3 8.8 %collective-permute-start.14 = (bf16[32,3712]{1,0:T(8,128)(2,1)}, bf16[32,3712]{1,0:T(8,128)(2,1)S(1)}, u32[]{:S(2)}, u32[]{:S(2)}) collective-permute-start(bf16[32,3712]{1,0:T(8,128)(2,1)} %assemble.1), channel_id=1, source_target_pairs={{0,192},{1,49},{16,208},{17,33},{32,224},{33,17},{48,240},{49,1},{... | collective-permute-start | bytes 712712 | tf_op jit(solution)/shard_map/ppermute | solution.py:47
  43.6 12.9 %collective-permute-start.18 = (bf16[2,32,3712]{2,1,0:T(8,128)(2,1)S(1)}, bf16[2,32,3712]{2,1,0:T(8,128)(2,1)S(1)}, u32[]{:S(2)}, u32[]{:S(2)}) collective-permute-start(bf16[2,32,3712]{2,1,0:T(8,128)(2,1)S(1)} %pad_maximum_fusion.1.q0), channel_id=1, source_target_pairs={{0,16},{1,65},{16,0},{17,81},{32,48},{33,97},{48,32},{49,113},{64,... | collective-permute-start | bytes 1425416 | tf_op jit(solution)/shard_map/ppermute | solution.py:47
  50.1 11.7 %collective-permute-start.20 = (bf16[2,32,3712]{2,1,0:T(8,128)(2,1)S(1)}, bf16[2,32,3712]{2,1,0:T(8,128)(2,1)}, u32[]{:S(2)}, u32[]{:S(2)}) collective-permute-start(bf16[2,32,3712]{2,1,0:T(8,128)(2,1)S(1)} %pad_maximum_fusion.q1), channel_id=1, source_target_pairs={{0,48},{1,193},{16,32},{17,209},{32,16},{33,225},{48,0},{49,241},{... | collective-permute-start | bytes 1425416 | tf_op jit(solution)/shard_map/ppermute | solution.py:47
  53.0 20.6 %collective-permute-start.17 = (bf16[2,32,3712]{2,1,0:T(8,128)(2,1)S(1)}, bf16[2,32,3712]{2,1,0:T(8,128)(2,1)S(1)}, u32[]{:S(2)}, u32[]{:S(2)}) collective-permute-start(bf16[2,32,3712]{2,1,0:T(8,128)(2,1)S(1)} %pad_maximum_fusion.1.q0), channel_id=1, source_target_pairs={{0,48},{1,193},{16,32},{17,209},{32,16},{33,225},{48,0},{49,241},{... | collective-permute-start | bytes 1425416 | tf_op jit(solution)/shard_map/ppermute | solution.py:47
  53.1 20.5 %collective-permute-start.15 = (bf16[2,32,3712]{2,1,0:T(8,128)(2,1)S(1)}, bf16[2,32,3712]{2,1,0:T(8,128)(2,1)S(1)}, u32[]{:S(2)}, u32[]{:S(2)}) collective-permute-start(bf16[2,32,3712]{2,1,0:T(8,128)(2,1)S(1)} %pad_maximum_fusion.q1), channel_id=1, source_target_pairs={{0,16},{1,65},{16,0},{17,81},{32,48},{33,97},{48,32},{49,113},{64,... | collective-permute-start | bytes 1425416 | tf_op jit(solution)/shard_map/ppermute | solution.py:47
  56.5 17.1 %collective-permute-start.19 = (bf16[2,32,3712]{2,1,0:T(8,128)(2,1)S(1)}, bf16[2,32,3712]{2,1,0:T(8,128)(2,1)S(1)}, u32[]{:S(2)}, u32[]{:S(2)}) collective-permute-start(bf16[2,32,3712]{2,1,0:T(8,128)(2,1)S(1)} %collective-permute-done.18.q2), channel_id=1, source_target_pairs={{0,48},{1,193},{16,32},{17,209},{32,16},{33,225},{48,0},{49,241},{... | collective-permute-start | bytes 1425416 | tf_op jit(solution)/shard_map/ppermute | solution.py:47
  61.9 11.7 %collective-permute-start.21 = (bf16[2,32,3712]{2,1,0:T(8,128)(2,1)}, bf16[2,32,3712]{2,1,0:T(8,128)(2,1)S(1)}, u32[]{:S(2)}, u32[]{:S(2)}) collective-permute-start(bf16[2,32,3712]{2,1,0:T(8,128)(2,1)} %collective-permute-done.20.q3), channel_id=1, source_target_pairs={{0,16},{1,65},{16,0},{17,81},{32,48},{33,97},{48,32},{49,113},{64,... | collective-permute-start | bytes 1425416 | tf_op jit(solution)/shard_map/ppermute | solution.py:47
  62.7 3.0 %copy-start = (bf16[1000,3584]{1,0:T(8,128)(2,1)S(1)}, bf16[1000,3584]{1,0:T(8,128)(2,1)}, u32[]{:S(2)}) copy-start(bf16[1000,3584]{1,0:T(8,128)(2,1)} %wa.1) | copy-start | bytes 21504004
  65.8 0.7 copy-start.1
  80.8 4.0 %collective-permute-start.22 = (f32[2,512]{1,0:T(2,128)S(1)}, f32[2,512]{1,0:T(2,128)S(1)}, u32[]{:S(2)}, u32[]{:S(2)}) collective-permute-start(f32[2,512]{1,0:T(2,128)S(1)} %late.1), channel_id=1, source_target_pairs={{0,64},{64,0},{128,192},{192,128},{1,65},{65,1},{129,193},{193,129... | collective-permute-start | bytes 12296 | tf_op jit(solution)/shard_map/ppermute | solution.py:34
  82.3 4.0 %collective-permute-start.23 = (f32[2,512]{1,0:T(2,128)S(1)}, f32[2,512]{1,0:T(2,128)S(1)}, u32[]{:S(2)}, u32[]{:S(2)}) collective-permute-start(f32[2,512]{1,0:T(2,128)S(1)} %late.1), channel_id=1, source_target_pairs={{0,128},{64,192},{128,0},{192,64},{1,129},{65,193},{129,1},{193,65... | collective-permute-start | bytes 12296 | tf_op jit(solution)/shard_map/ppermute | solution.py:34
  83.2 3.7 %collective-permute-start.24 = (f32[2,512]{1,0:T(2,128)S(1)}, f32[2,512]{1,0:T(2,128)S(1)}, u32[]{:S(2)}, u32[]{:S(2)}) collective-permute-start(f32[2,512]{1,0:T(2,128)S(1)} %late.1), channel_id=1, source_target_pairs={{0,192},{64,128},{128,64},{192,0},{1,193},{65,129},{129,65},{193,1... | collective-permute-start | bytes 12296 | tf_op jit(solution)/shard_map/ppermute | solution.py:34
  86.8 3.9 %collective-permute-start.25 = (f32[2,512]{1,0:T(2,128)S(1)}, f32[2,512]{1,0:T(2,128)S(1)}, u32[]{:S(2)}, u32[]{:S(2)}) collective-permute-start(f32[2,512]{1,0:T(2,128)S(1)} %add_add_fusion.2), channel_id=1, source_target_pairs={{0,16},{16,0},{32,48},{48,32},{1,17},{17,1},{33,49},{49,33},{2,18}... | collective-permute-start | bytes 12296 | tf_op jit(solution)/shard_map/ppermute | solution.py:34
  86.9 4.3 %collective-permute-start.26 = (f32[2,512]{1,0:T(2,128)S(1)}, f32[2,512]{1,0:T(2,128)S(1)}, u32[]{:S(2)}, u32[]{:S(2)}) collective-permute-start(f32[2,512]{1,0:T(2,128)S(1)} %add_add_fusion.2), channel_id=1, source_target_pairs={{0,32},{16,48},{32,0},{48,16},{1,33},{17,49},{33,1},{49,17},{2,34}... | collective-permute-start | bytes 12296 | tf_op jit(solution)/shard_map/ppermute | solution.py:34
  90.2 3.7 %collective-permute-start.27 = (f32[2,512]{1,0:T(2,128)S(1)}, f32[2,512]{1,0:T(2,128)S(1)}, u32[]{:S(2)}, u32[]{:S(2)}) collective-permute-start(f32[2,512]{1,0:T(2,128)S(1)} %add_add_fusion.2), channel_id=1, source_target_pairs={{0,48},{16,32},{32,16},{48,0},{1,49},{17,33},{33,17},{49,1},{2,50}... | collective-permute-start | bytes 12296 | tf_op jit(solution)/shard_map/ppermute | solution.py:34
  93.8 3.6 %collective-permute-start.28 = (f32[2,512]{1,0:T(2,128)S(1)}, f32[2,512]{1,0:T(2,128)S(1)}, u32[]{:S(2)}, u32[]{:S(2)}) collective-permute-start(f32[2,512]{1,0:T(2,128)S(1)} %add_add_fusion.1), channel_id=1, source_target_pairs={{0,2},{2,0},{4,6},{6,4},{8,10},{10,8},{12,14},{14,12},{1,3},{3,1},... | collective-permute-start | bytes 12296 | tf_op jit(solution)/shard_map/ppermute | solution.py:34
  93.9 3.5 %collective-permute-start.29 = (f32[2,512]{1,0:T(2,128)S(1)}, f32[2,512]{1,0:T(2,128)S(1)}, u32[]{:S(2)}, u32[]{:S(2)}) collective-permute-start(f32[2,512]{1,0:T(2,128)S(1)} %add_add_fusion.1), channel_id=1, source_target_pairs={{0,4},{2,6},{4,0},{6,2},{8,12},{10,14},{12,8},{14,10},{1,5},{3,7},... | collective-permute-start | bytes 12296 | tf_op jit(solution)/shard_map/ppermute | solution.py:34
  95.8 4.3 %collective-permute-start.30 = (f32[2,512]{1,0:T(2,128)S(1)}, f32[2,512]{1,0:T(2,128)S(1)}, u32[]{:S(2)}, u32[]{:S(2)}) collective-permute-start(f32[2,512]{1,0:T(2,128)S(1)} %add_add_fusion.1), channel_id=1, source_target_pairs={{0,6},{2,4},{4,2},{6,0},{8,14},{10,12},{12,10},{14,8},{1,7},{3,5},... | collective-permute-start | bytes 12296 | tf_op jit(solution)/shard_map/ppermute | solution.py:34
  100.1 6.4 %collective-permute-start.31 = (f32[2,512]{1,0:T(2,128)S(1)}, f32[2,512]{1,0:T(2,128)S(1)}, u32[]{:S(2)}, u32[]{:S(2)}) collective-permute-start(f32[2,512]{1,0:T(2,128)S(1)} %add_add_fusion), channel_id=1, source_target_pairs={{0,8},{2,10},{4,12},{6,14},{8,0},{10,2},{12,4},{14,6},{1,9},{3,11}... | collective-permute-start | bytes 12296 | tf_op jit(solution)/shard_map/ppermute | solution.py:34
  106.6 14.7 %copy-start.6 = (f32[2,512]{1,0:T(2,128)}, f32[2,512]{1,0:T(2,128)S(1)}, u32[]{:S(2)}) copy-start(f32[2,512]{1,0:T(2,128)S(1)} %add.70.own) | copy-start | bytes 12292
  106.6 14.7 %collective-permute-start.32 = (f32[2,512]{1,0:T(2,128)S(1)}, f32[2,512]{1,0:T(2,128)S(1)}, u32[]{:S(2)}, u32[]{:S(2)}) collective-permute-start(f32[2,512]{1,0:T(2,128)S(1)} %add.70.own), channel_id=1, source_target_pairs={{0,1},{1,0},{2,3},{3,2},{4,5},{5,4},{6,7},{7,6},{8,9},{9,8},{10,11... | collective-permute-start | bytes 12296 | tf_op jit(solution)/shard_map/ppermute | solution.py:30
  121.2 0.6 copy-start.8

commit v3 on v1

v3 whole, which is shorter than its diff:
```python
import itertools

import jax
import jax.numpy as jnp
from jax import lax
from jax.experimental import pallas as pl
from jax.experimental.pallas import tpu as pltpu
from jax.sharding import Mesh
from jax.sharding import PartitionSpec as P

NX, NY, NZ, NC = 4, 4, 8, 2
DP = ("x", "y")
VOCAB = ("z", "c")
LEN = 32
SEQS = NX * NY
ROWS = SEQS * LEN
D = 3584
PIECE = D // NZ // NC
META = 128
VOCAB_ROWS = 1000
TILE = 256
MIB = 1024 * 1024

kto_beta = 0.1
desirable_weight = 1.0
undesirable_weight = 1.33


def swap_cores(array):
    return lax.ppermute(array, "c", [(0, 1), (1, 0)])


def split_pairs(k, first):
    pairs = []
    for x, y, c in itertools.product(range(NX), range(NY), range(NC)):
        along_x = (c == 0) == first
        u, v = (x ^ k, y) if along_x else (x, y ^ k)
        pairs.append(((x * NY + y) * NC + c, (u * NY + v) * NC + c))
    return pairs


def split_xor(array, k, first):
    return lax.ppermute(array, ("x", "y", "c"), split_pairs(k, first))


def bit_xor(a, b):
    return jnp.bitwise_xor(a, b)


def seq_of(place, far, near):
    x, y, c = place[0], place[1], place[3]
    u = jnp.where(c == 0, bit_xor(x, near), bit_xor(x, far))
    v = jnp.where(c == 0, bit_xor(y, far), bit_xor(y, near))
    return u * NY + v


def assemble_kernel(place, pair, flag, pieces, labels, masks, out):
    for group in range(NZ * NC // 4):
        out[:, 4 * group * PIECE : 4 * (group + 1) * PIECE] = jnp.concatenate(
            [pieces[4 * group + i] for i in range(4)], axis=1
        )
    diagonal = lax.broadcasted_iota(jnp.int32, (LEN, LEN), 0) == lax.broadcasted_iota(
        jnp.int32, (LEN, LEN), 1
    )

    def column(line):
        return jnp.sum(
            jnp.where(diagonal, line[...].astype(jnp.float32), 0.0), axis=1, keepdims=True
        )

    label = column(labels).astype(jnp.int32)
    partner = jnp.where(place[3] == 0, place[0] * NY + place[1], pair[0])
    fields = (
        (label & 255).astype(jnp.float32),
        ((label >> 8) & 255).astype(jnp.float32),
        (label >> 16).astype(jnp.float32),
        column(masks),
        partner.astype(jnp.float32),
        flag[0].astype(jnp.float32),
    )
    lane = lax.broadcasted_iota(jnp.int32, (LEN, META), 1)
    meta = jnp.zeros((LEN, META), jnp.float32)
    for i, field in enumerate(fields):
        meta = jnp.where(lane == i, field, meta)
    out[:, D:] = meta.astype(jnp.bfloat16)


ORDER = (
    (0, (0, 1)),
    (0, (2, 3)),
    (1, (0, 1)),
    (3, (2, 3)),
    (1, (2, 3)),
    (3, (0, 1)),
    (2, (0, 1)),
    (2, (2, 3)),
)
TILES = -(-VOCAB_ROWS // TILE)


def logits_kernel(place, *refs):
    blocks, (ref, wa, wb, out, stat, rows, target, sums, held, arrived) = refs[:8], refs[8:]
    step = pl.program_id(0)
    copy = pltpu.make_async_copy(wb, held, arrived)

    @pl.when(step == 0)
    def _():
        copy.start()
        for block, (far, nears) in zip(blocks, ORDER):
            for k, near in enumerate(nears):
                start = pl.multiple_of(seq_of(place, far, near) * LEN, LEN)
                rows[pl.ds(start, LEN), :] = block[k]
        meta = rows[:, D:]
        partner = meta[:, 4:5].astype(jnp.float32).astype(jnp.int32)
        left = lax.broadcasted_iota(jnp.int32, (ROWS, ROWS), 0)
        right = lax.broadcasted_iota(jnp.int32, (ROWS, ROWS), 1)
        same = (partner == right // LEN) & (left % LEN == right % LEN)
        moved = lax.dot_general(
            meta,
            same.astype(jnp.float32).astype(jnp.bfloat16),
            (((0,), (1,)), ((), ())),
            preferred_element_type=jnp.float32,
        )
        target[...] = (moved[0:1] + 256.0 * moved[1:2] + 65536.0 * moved[2:3]).astype(jnp.int32)
        stat[0:1] = moved[3:4]
        stat[1:2] = moved[5:6]
        sums[0:1] = jnp.zeros((1, ROWS), jnp.float32)
        sums[1:2] = -ref[...]

    def add(weight, first, base):
        count = weight.shape[0]
        logits = lax.dot_general(
            weight,
            rows[:, :D],
            (((1,), (1,)), ((), ())),
            preferred_element_type=jnp.float32,
        )
        vocab = first + lax.broadcasted_iota(jnp.int32, (count, ROWS), 0)
        valid = vocab < VOCAB_ROWS
        sums[0:1] += jnp.sum(jnp.where(valid, jnp.exp(logits), 0.0), axis=0, keepdims=True)
        hit = valid & (vocab + base == target[...])
        sums[1:2] += jnp.sum(jnp.where(hit, logits, 0.0), axis=0, keepdims=True)

    @pl.when(step < TILES)
    def _():
        add(wa[...], step * TILE, place[4])

    @pl.when(step == TILES)
    def _():
        copy.wait()

    for i in range(TILES):

        @pl.when(step == TILES + i)
        def _(i=i):
            add(held[i * TILE : min((i + 1) * TILE, VOCAB_ROWS), :], i * TILE, place[5])

    @pl.when(step == 2 * TILES - 1)
    def _():
        out[...] = jnp.broadcast_to(sums[...][None], out.shape)


def losses_kernel(place, parts, own_stat, other_stat, ref, logps, own_loss, loss):
    x, y, z, c = place[0], place[1], place[2], place[3]
    first = c == 0
    lane = lax.broadcasted_iota(jnp.int32, (SEQS, ROWS), 1)
    row = lax.broadcasted_iota(jnp.int32, (SEQS, ROWS), 0)
    inside = lane // LEN == row
    picked = []
    sums = []
    for core, (sa, sb) in enumerate(((own_stat, other_stat), (other_stat, own_stat))):
        total = parts[core]
        for i in range(1, NZ):
            total = total + parts[NC * i + core]
        weight = jnp.where(first, sa[0:1], sb[0:1])
        value = total[1:2] - jnp.log(total[0:1])
        picked.append(value)
        sums.append(jnp.sum(jnp.where(inside, weight * value, 0.0), axis=1, keepdims=True))
    flags = jnp.where(first, own_stat[1:2], other_stat[1:2])
    desirable = jnp.sum(
        jnp.where(inside & (lane % LEN == 0), flags, 0.0), axis=1, keepdims=True
    )
    logratio, kl_terms = sums
    kl_estimate = jnp.sum(kl_terms, axis=0, keepdims=True) / SEQS
    wanted = desirable_weight * (1.0 - jax.nn.sigmoid(kto_beta * (logratio - kl_estimate)))
    unwanted = undesirable_weight * (1.0 - jax.nn.sigmoid(kto_beta * (kl_estimate - logratio)))
    losses = jnp.where(desirable > 0.5, wanted, unwanted)
    seq = x * NY + y
    here = lax.broadcasted_iota(jnp.int32, (SEQS, 1), 0) == seq
    own_loss[...] = jnp.sum(jnp.where(here, losses, 0.0), axis=0, keepdims=True)
    loss[...] = jnp.sum(losses, axis=0, keepdims=True) / SEQS
    half = jnp.where(z < NZ // 2, picked[0], picked[1])
    start = seq * LEN + (z % (NZ // 2)) * 8 + c * 4
    hit = lax.broadcasted_iota(jnp.int32, (8, ROWS), 1) == (
        start + lax.broadcasted_iota(jnp.int32, (8, ROWS), 0)
    )
    column = jnp.sum(jnp.where(hit, half, 0.0), axis=1, keepdims=True)
    square = lax.broadcasted_iota(jnp.int32, (8, META), 0) == lax.broadcasted_iota(
        jnp.int32, (8, META), 1
    )
    line = jnp.sum(jnp.where(square, column, 0.0), axis=0, keepdims=True)
    logps[...] = line[:, :4] + ref[...]


def whole_block(array):
    zeros = (0,) * array.ndim
    return pl.BlockSpec(array.shape, lambda i: zeros)


def smem():
    return pl.BlockSpec(memory_space=pltpu.SMEM)


def small_call(kernel, name, out_shapes, scalars, *arrays):
    return pl.pallas_call(
        kernel,
        grid=(1,),
        out_shape=out_shapes,
        in_specs=[smem()] * len(scalars) + [whole_block(a) for a in arrays],
        out_specs=[whole_block(a) for a in out_shapes],
        compiler_params=pltpu.CompilerParams(vmem_limit_bytes=8 * MIB),
        name=name,
    )(*scalars, *arrays)


def head_call(place, blocks, ref, weight, other_weight):
    out_shapes = [
        jax.ShapeDtypeStruct((SEQS, 2, ROWS), jnp.float32),
        jax.ShapeDtypeStruct((2, ROWS), jnp.float32),
    ]
    return pl.pallas_call(
        logits_kernel,
        grid=(2 * TILES,),
        out_shape=out_shapes,
        in_specs=[smem()]
        + [whole_block(a) for a in (*blocks, ref)]
        + [
            pl.BlockSpec((TILE, D), lambda i: (jnp.minimum(i, TILES - 1), 0)),
            pl.BlockSpec(memory_space=pl.ANY),
        ],
        out_specs=[whole_block(a) for a in out_shapes],
        scratch_shapes=[
            pltpu.VMEM((ROWS, D + META), jnp.bfloat16),
            pltpu.VMEM((1, ROWS), jnp.int32),
            pltpu.VMEM((2, ROWS), jnp.float32),
            pltpu.VMEM((VOCAB_ROWS, D), jnp.bfloat16),
            pltpu.SemaphoreType.DMA,
        ],
        compiler_params=pltpu.CompilerParams(vmem_limit_bytes=54 * MIB),
        cost_estimate=pl.CostEstimate(
            flops=4 * ROWS * VOCAB_ROWS * D,
            bytes_accessed=2 * (2 * VOCAB_ROWS + ROWS) * D,
            transcendentals=2 * ROWS * VOCAB_ROWS,
        ),
        name="logits",
    )(place, *blocks, ref, weight, other_weight)


def on_device(hidden, kl_hidden, head_weight, labels, token_mask, kl_pair, desirable, ref_logps):
    x, y, z, c = (lax.axis_index(a) for a in ("x", "y", "z", "c"))
    first = c == 0
    shard = ((x * NY + y) * NZ + z) * NC
    place = jnp.stack(
        [x, y, z, c, (shard + c) * VOCAB_ROWS, (shard + 1 - c) * VOCAB_ROWS]
    ).astype(jnp.int32)

    seq = x * NY + y
    f32 = jnp.float32

    copies = jnp.tile(jnp.concatenate([hidden, kl_hidden]), (NZ, 1, 1))
    pieces = lax.all_to_all(copies, VOCAB, 0, 0, tiled=True)
    pieces, head_weight, ref_logps = lax.optimization_barrier((pieces, head_weight, ref_logps))
    ref_came = swap_cores(ref_logps)
    other_weight = swap_cores(head_weight)
    (rows,) = small_call(
        assemble_kernel,
        "assemble",
        [jax.ShapeDtypeStruct((LEN, D + META), jnp.bfloat16)],
        (place, kl_pair, desirable),
        pieces,
        labels,
        token_mask,
    )

    came = [split_xor(rows, k, True) for k in (1, 2, 3)]
    near_a = jnp.stack([rows, came[0]])
    near_b = jnp.stack([came[1], came[2]])
    one_a = split_xor(near_a, 1, False)
    three_b = split_xor(near_b, 3, False)
    one_b = split_xor(near_b, 1, False)
    three_a = split_xor(near_a, 3, False)
    two_a = split_xor(one_a, 3, False)
    two_b = split_xor(three_b, 1, False)

    pair_ref = jnp.concatenate(
        [jnp.where(first, ref_logps, ref_came), jnp.where(first, ref_came, ref_logps)], axis=1
    )
    mine = (z // (NZ // 2)) == c
    ref_rows = lax.dynamic_update_slice(
        jnp.zeros((1, ROWS), f32),
        jnp.where(mine, pair_ref, 0.0),
        (0, seq * LEN + (z % (NZ // 2)) * 8),
    )
    sums, stat = head_call(
        place,
        (near_a, near_b, one_a, three_b, one_b, three_a, two_a, two_b),
        ref_rows,
        head_weight,
        other_weight,
    )

    other_stat = swap_cores(stat)
    sums = jnp.sum(lax.all_to_all(sums, DP, 0, 0, tiled=True), axis=0)
    sums = jnp.broadcast_to(sums[None], (NZ * NC, 2, ROWS))
    parts = lax.all_to_all(sums, VOCAB, 0, 0, tiled=True)
    logps, own_loss, loss = small_call(
        losses_kernel,
        "losses",
        [jax.ShapeDtypeStruct(shape, f32) for shape in ((1, 4), (1, 1), (1, 1))],
        (place,),
        parts,
        stat,
        other_stat,
        ref_logps,
    )
    return (logps, own_loss.reshape(1), loss.reshape(()))


def solution(mesh):
    split = Mesh(mesh.devices.reshape(NX, NY, NZ, NC), DP + VOCAB)
    in_specs = (
        P(DP, None, VOCAB),
        P(DP, None, VOCAB),
        P(DP + VOCAB, None),
        P(DP, None),
        P(DP, None),
        P(DP),
        P(DP),
        P(DP, VOCAB),
    )
    out_specs = (P(DP, VOCAB), P(DP), P())
    return jax.shard_map(
        on_device, mesh=split, in_specs=in_specs, out_specs=out_specs, check_vma=False
    )
```

time: 116 us -> 103 us (0.89)
  blocking collectives: 0 us -> 32.8 us
  starting transfers between devices: 47.6 us -> 21.8 us
  waiting for transfers between devices: 40.3 us -> 23.3 us
  other arithmetic: 4.74 us -> 1.65 us
  local copies, waits for them, and re-layouts: 6.37 us -> 3.52 us
  Pallas kernels: 14.6 us -> 16.8 us
    all_to_all x0 -> x2, blocking collectives: none -> 32.8 us  [the longest x1 21.5 us: on_device(): pieces = lax.all_to_all(copies, VOCAB, 0, 0, tiled=True)]
    ppermute x14 -> x0, starting transfers between devices: 23.8 us -> none  [xor_along(): lax.ppermute(array, axis, [(i, i ^ k) for i in range(lax.axis_size(axis))])]
    ppermute x5 -> x3, starting transfers between devices: 17.1 us -> 3.32 us  [swap_cores(): return lax.ppermute(array, 'c', [(0, 1), (1, 0)])]
    ppermute x6 -> x9, waiting for transfers between devices: 27.5 us -> 15.8 us  [split_xor(): return lax.ppermute(array, ('x', 'y', 'c'), split_pairs(k, first))]
    ppermute x14 -> x0, waiting for transfers between devices: 10.8 us -> none  [xor_along(): lax.ppermute(array, axis, [(i, i ^ k) for i in range(lax.axis_size(axis))])]
    all_to_all x0 -> x1, starting transfers between devices: none -> 7.85 us  [on_device(): parts = lax.all_to_all(sums, VOCAB, 0, 0, tiled=True)]
    all_to_all x0 -> x1, waiting for transfers between devices: none -> 6.46 us  [on_device(): parts = lax.all_to_all(sums, VOCAB, 0, 0, tiled=True)]
    ppermute x6 -> x9, starting transfers between devices: 6.67 us -> 10.7 us  [split_xor(): return lax.ppermute(array, ('x', 'y', 'c'), split_pairs(k, first))]
  transfers between devices with their start and end apart: 25 -> 13, of which waited for: 16 -> 10; matrix products, arithmetic and copies ran while one was open for 5% -> 1% of each run, Pallas kernels for 2% -> 1%
where the time goes in v3:
time: 103 us; the launch traced here: 102 us
  blocking collectives  32.8 us (32%)
  waiting for transfers between devices  23.3 us (23%)
  starting transfers between devices  21.8 us (21%)
  Pallas kernels  16.8 us (16%)
  local copies, waits for them, and re-layouts  3.52 us (3%)
  between operations  2.08 us (2%)
  other arithmetic  1.65 us (2%)
    all_to_all x1, blocking collectives, on_device(): pieces = lax.all_to_all(copies, VOCAB, 0, 0, tiled=True)  21.5 us
    ppermute x9, waiting for transfers between devices, split_xor(): return lax.ppermute(array, ('x', 'y', 'c'), split_pairs(k, first))  15.8 us
    pallas_call x1, Pallas kernels, head_call(): pl.pallas_call(logits_kernel, grid=(2 * TILES,), out_shape=out_shapes, in...  14.9 us
    all_to_all x1, blocking collectives, on_device(): sums = jnp.sum(lax.all_to_all(sums, DP, 0, 0, tiled=True), axis=0)  11.4 us
    ppermute x9, starting transfers between devices, split_xor(): return lax.ppermute(array, ('x', 'y', 'c'), split_pairs(k, first))  10.7 us
    all_to_all x1, starting transfers between devices, on_device(): parts = lax.all_to_all(sums, VOCAB, 0, 0, tiled=True)  7.85 us
    all_to_all x1, waiting for transfers between devices, on_device(): parts = lax.all_to_all(sums, VOCAB, 0, 0, tiled=True)  6.46 us
    ppermute x3, starting transfers between devices, swap_cores(): return lax.ppermute(array, 'c', [(0, 1), (1, 0)])  3.32 us
  transfers between devices with their start and end apart: 13, of which 10 were waited for; matrix products, arithmetic and copies ran while one was open for 1% of the time, Pallas kernels for 1%

profile of v3, /device:TPU:1, one launch (start us, length us, event | category | flops | bytes accessed | tf_op | source)
XLA Modules:
  0.0 102.0 jit_solution(14621379842060997749)
XLA Ops:
  0.6 0.7 pad_maximum_fusion.2
  1.4 21.5 %all_to_all.15.pieces = bf16[16,32,224]{2,1,0:T(8,128)(2,1)S(1)} all-to-all(bf16[16,32,224]{2,1,0:T(8,128)(2,1)S(1)} %bitcast.14), channel_id=1, replica_groups=mesh['x'=4,'y'=4,'z'=8,'c'=2] {'z','c'}, dimensions={0} | all-to-all | bytes 458752 | tf_op jit(solution)/shard_map/all_to_all | solution.py:271
  22.9 0.0 collective-permute-start.10
  24.2 0.1 stack.45.place
  24.3 0.0 copy-start.4
  24.3 0.7 copy-done.4
  24.9 0.0 copy-start.5
  24.9 0.7 copy-done.5
  25.6 0.0 copy-start
  25.6 0.7 assemble.1
  26.3 1.4 %collective-permute-start = (bf16[32,3712]{1,0:T(8,128)(2,1)S(1)}, bf16[32,3712]{1,0:T(8,128)(2,1)S(1)}, u32[]{:S(2)}, u32[]{:S(2)}) collective-permute-start(bf16[32,3712]{1,0:T(8,128)(2,1)S(1)} %assemble.1), channel_id=1, source_target_pairs={{0,64},{1,17},{16,80},{17,1},{32,96},{33,49},{48,112},{49,33},{64,... | collective-permute-start | bytes 712712 | tf_op jit(solution)/shard_map/ppermute | solution.py:43
  27.7 1.9 %collective-permute-start.2 = (bf16[32,3712]{1,0:T(8,128)(2,1)S(1)}, bf16[32,3712]{1,0:T(8,128)(2,1)S(1)}, u32[]{:S(2)}, u32[]{:S(2)}) collective-permute-start(bf16[32,3712]{1,0:T(8,128)(2,1)S(1)} %assemble.1), channel_id=1, source_target_pairs={{0,192},{1,49},{16,208},{17,33},{32,224},{33,17},{48,240},{49,1},{... | collective-permute-start | bytes 712712 | tf_op jit(solution)/shard_map/ppermute | solution.py:43
  29.6 0.7 collective-permute-start.1
  30.3 1.3 %collective-permute-done = bf16[32,3712]{1,0:T(8,128)(2,1)S(1)} collective-permute-done((bf16[32,3712]{1,0:T(8,128)(2,1)S(1)}, bf16[32,3712]{1,0:T(8,128)(2,1)S(1)}, u32[]{:S(2)}, u32[]{:S(2)}) %collective-permute-start) | collective-permute-done | bytes 237600 | tf_op jit(solution)/shard_map/ppermute | solution.py:43
  31.6 0.1 pad_maximum_fusion.refs_0_
  31.7 0.0 copy-start.6
  31.7 1.3 %collective-permute-start.3 = (bf16[2,32,3712]{2,1,0:T(8,128)(2,1)S(1)}, bf16[2,32,3712]{2,1,0:T(8,128)(2,1)S(1)}, u32[]{:S(2)}, u32[]{:S(2)}) collective-permute-start(bf16[2,32,3712]{2,1,0:T(8,128)(2,1)S(1)} %pad_maximum_fusion.refs_0_), channel_id=1, source_target_pairs={{0,16},{1,65},{16,0},{17,81},{32,48},{33,97},{48,32},{49,113},{64,... | collective-permute-start | bytes 1425416 | tf_op jit(solution)/shard_map/ppermute | solution.py:43
  33.0 2.2 %collective-permute-done.2 = bf16[32,3712]{1,0:T(8,128)(2,1)S(1)} collective-permute-done((bf16[32,3712]{1,0:T(8,128)(2,1)S(1)}, bf16[32,3712]{1,0:T(8,128)(2,1)S(1)}, u32[]{:S(2)}, u32[]{:S(2)}) %collective-permute-start.2) | collective-permute-done | bytes 237600 | tf_op jit(solution)/shard_map/ppermute | solution.py:43
  35.2 1.5 %collective-permute-done.1 = bf16[32,3712]{1,0:T(8,128)(2,1)S(1)} collective-permute-done((bf16[32,3712]{1,0:T(8,128)(2,1)S(1)}, bf16[32,3712]{1,0:T(8,128)(2,1)S(1)}, u32[]{:S(2)}, u32[]{:S(2)}) %collective-permute-start.1) | collective-permute-done | bytes 237600 | tf_op jit(solution)/shard_map/ppermute | solution.py:43
  36.6 0.1 pad_maximum_fusion.1.refs_1_
  36.7 0.0 copy-start.7
  36.7 2.6 %collective-permute-start.4 = (bf16[2,32,3712]{2,1,0:T(8,128)(2,1)S(1)}, bf16[2,32,3712]{2,1,0:T(8,128)(2,1)S(1)}, u32[]{:S(2)}, u32[]{:S(2)}) collective-permute-start(bf16[2,32,3712]{2,1,0:T(8,128)(2,1)S(1)} %pad_maximum_fusion.1.refs_1_), channel_id=1, source_target_pairs={{0,48},{1,193},{16,32},{17,209},{32,16},{33,225},{48,0},{49,241},{... | collective-permute-start | bytes 1425416 | tf_op jit(solution)/shard_map/ppermute | solution.py:43
  39.3 3.0 %collective-permute-start.9 = (f32[1,4]{1,0:T(1,128)}, f32[1,4]{1,0:T(1,128)S(1)}, u32[]{:S(2)}, u32[]{:S(2)}) collective-permute-start(f32[1,4]{1,0:T(1,128)} %ref), channel_id=1, source_target_pairs={{0,1},{1,0},{2,3},{3,2},{4,5},{5,4},{6,7},{7,6},{8,9},{9,8},{10,11... | collective-permute-start | bytes 56 | tf_op jit(solution)/shard_map/ppermute | solution.py:30
  42.3 1.5 %collective-permute-start.6 = (bf16[2,32,3712]{2,1,0:T(8,128)(2,1)S(1)}, bf16[2,32,3712]{2,1,0:T(8,128)(2,1)S(1)}, u32[]{:S(2)}, u32[]{:S(2)}) collective-permute-start(bf16[2,32,3712]{2,1,0:T(8,128)(2,1)S(1)} %pad_maximum_fusion.refs_0_), channel_id=1, source_target_pairs={{0,48},{1,193},{16,32},{17,209},{32,16},{33,225},{48,0},{49,241},{... | collective-permute-start | bytes 1425416 | tf_op jit(solution)/shard_map/ppermute | solution.py:43
  43.8 0.0 collective-permute-done.9
  43.8 0.1 collective-permute-start.5
  43.9 0.0 collective-permute-done.3.refs_2_
  43.9 0.0 copy-start.9
  43.9 1.2 %collective-permute-start.7 = (bf16[2,32,3712]{2,1,0:T(8,128)(2,1)S(1)}, bf16[2,32,3712]{2,1,0:T(8,128)(2,1)}, u32[]{:S(2)}, u32[]{:S(2)}) collective-permute-start(bf16[2,32,3712]{2,1,0:T(8,128)(2,1)S(1)} %collective-permute-done.3.refs_2_), channel_id=1, source_target_pairs={{0,48},{1,193},{16,32},{17,209},{32,16},{33,225},{48,0},{49,241},{... | collective-permute-start | bytes 1425416 | tf_op jit(solution)/shard_map/ppermute | solution.py:43
  45.1 0.7 collective-permute-done.4.refs_3_
  45.8 0.0 copy-start.10
  45.8 0.0 collective-permute-start.8
  45.8 0.7 broadcast_select_fusion.1
  46.5 0.1 broadcast_select_fusion.2
  46.6 0.1 dynamic_update_slice.3.refs_8_
  46.7 0.0 copy-start.8
  46.7 0.0 copy-start.3
  46.7 4.6 %collective-permute-done.6.refs_5_ = bf16[2,32,3712]{2,1,0:T(8,128)(2,1)S(1)} collective-permute-done((bf16[2,32,3712]{2,1,0:T(8,128)(2,1)S(1)}, bf16[2,32,3712]{2,1,0:T(8,128)(2,1)S(1)}, u32[]{:S(2)}, u32[]{:S(2)}) %collective-permute-start.6) | collective-permute-done | bytes 475168 | tf_op jit(solution)/shard_map/ppermute | solution.py:43
  51.3 0.0 copy-start.11
  51.3 0.3 collective-permute-done.5.refs_4_
  51.6 0.0 copy-start.12
  51.6 4.9 %collective-permute-done.7.refs_6_ = bf16[2,32,3712]{2,1,0:T(8,128)(2,1)} collective-permute-done((bf16[2,32,3712]{2,1,0:T(8,128)(2,1)S(1)}, bf16[2,32,3712]{2,1,0:T(8,128)(2,1)}, u32[]{:S(2)}, u32[]{:S(2)}) %collective-permute-start.7) | collective-permute-done | bytes 475168 | tf_op jit(solution)/shard_map/ppermute | solution.py:43
  56.5 0.3 collective-permute-done.8.refs_7_
  56.8 0.0 collective-permute-done.10.refs_10_
  56.8 0.0 copy-done
  56.8 0.0 copy-done.6
  56.8 0.0 copy-done.7
  56.8 0.0 copy-done.9
  56.8 0.0 copy-done.10
  56.8 0.0 copy-done.8
  56.8 0.0 copy-done.11
  56.8 0.0 copy-done.12
  56.9 14.9 %logits.1 = (f32[16,2,512]{2,1,0:T(2,128)}, f32[2,512]{1,0:T(2,128)}) custom-call(s32[6]{0:T(128)} %copy-done, bf16[2,32,3712]{2,1,0:T(8,128)(2,1)} %copy-done.6, bf16[2,32,3712]{2,1,0:T(8,128)(2,1)} %copy-done.7, bf16[2,32,3712]{2,1,0:T(8,128)(2,1)} %copy-done.9, bf16[2,32,3712]{2,1,0:T(8,128)(2,1)} %copy-done.10, bf16[2,32,3712]{2,1,0:T(8,128)(2,1)} %copy-done.12, ...), custom_call_target="tpu_custom_call" | custom-call | flops 7340032000 | bytes 18006016 | tf_op jit(solution)/shard_map/logits/pallas_call | solution.py:231
  71.8 11.4 %all_to_all.16 = f32[16,2,512]{2,1,0:T(2,128)S(1)} all-to-all(f32[16,2,512]{2,1,0:T(2,128)} %get-tuple-element.14), channel_id=1, replica_groups=mesh['x'=4,'y'=4,'z'=8,'c'=2] {'x','y'}, dimensions={0} | all-to-all | bytes 131072 | tf_op jit(solution)/shard_map/all_to_all | solution.py:313
  83.2 0.6 broadcast_in_dim.15
  83.8 7.8 %all-to-all-start.2 = ((f32[16,2,512]{2,1,0:T(2,128)}), f32[16,2,512]{2,1,0:T(2,128)S(1)}, u32[]{:S(2)}, u32[]{:S(2)}) async-start(f32[16,2,512]{2,1,0:T(2,128)} %broadcast_in_dim.15), calls=%async_computation.2 | async-start | bytes 131072 | tf_op jit(solution)/shard_map/all_to_all | solution.py:315
  91.7 0.3 collective-permute-start.11
  92.0 1.1 %collective-permute-done.11.other_stat = f32[2,512]{1,0:T(2,128)S(1)} collective-permute-done((f32[2,512]{1,0:T(2,128)}, f32[2,512]{1,0:T(2,128)S(1)}, u32[]{:S(2)}, u32[]{:S(2)}) %collective-permute-start.11) | collective-permute-done | bytes 4128 | tf_op jit(solution)/shard_map/ppermute | solution.py:30
  93.0 6.5 %all-to-all-done.2.parts = f32[16,2,512]{2,1,0:T(2,128)S(1)} async-done(((f32[16,2,512]{2,1,0:T(2,128)}), f32[16,2,512]{2,1,0:T(2,128)S(1)}, u32[]{:S(2)}, u32[]{:S(2)}) %all-to-all-start.2) | async-done | bytes 65568 | tf_op jit(solution)/shard_map/all_to_all | solution.py:315
  99.5 0.0 copy-done.3
  99.5 0.0 copy-start.1
  99.5 0.7 copy-done.1
  100.2 0.7 copy-done.2
  100.8 1.2 %losses.1 = (f32[1,4]{1,0:T(1,128)}, f32[1,1]{1,0:T(1,128)}, f32[1,1]{1,0:T(1,128)}) custom-call(s32[6]{0:T(128)S(1)} %copy-done.1, f32[16,2,512]{2,1,0:T(2,128)S(1)} %all-to-all-done.2.parts, f32[2,512]{1,0:T(2,128)S(1)} %copy-done.2, f32[2,512]{1,0:T(2,128)S(1)} %collective-permute-done.11.other_stat, f32[1,4]{1,0:T(1,128)S(1)} %copy-done.3), custom_call_target="tpu_custom_call" | custom-call | tf_op jit(solution)/shard_map/losses/pallas_call | solution.py:215
  (4 shorter events, 0.1 us)
Async XLA Ops:
  22.9 33.9 %collective-permute-start.10 = (bf16[1000,3584]{1,0:T(8,128)(2,1)}, bf16[1000,3584]{1,0:T(8,128)(2,1)}, u32[]{:S(2)}, u32[]{:S(2)}) collective-permute-start(bf16[1000,3584]{1,0:T(8,128)(2,1)} %refs_9_), channel_id=1, source_target_pairs={{0,1},{1,0},{2,3},{3,2},{4,5},{5,4},{6,7},{7,6},{8,9},{9,8},{10,11... | collective-permute-start | bytes 21504008 | tf_op jit(solution)/shard_map/ppermute | solution.py:30
  24.3 0.7 copy-start.4
  24.9 0.7 copy-start.5
  25.6 31.2 %copy-start = (s32[6]{0:T(128)}, s32[6]{0:T(128)S(1)}, u32[]{:S(2)}) copy-start(s32[6]{0:T(128)S(1)} %stack.45.place) | copy-start | bytes 76
  26.3 5.3 %collective-permute-start = (bf16[32,3712]{1,0:T(8,128)(2,1)S(1)}, bf16[32,3712]{1,0:T(8,128)(2,1)S(1)}, u32[]{:S(2)}, u32[]{:S(2)}) collective-permute-start(bf16[32,3712]{1,0:T(8,128)(2,1)S(1)} %assemble.1), channel_id=1, source_target_pairs={{0,64},{1,17},{16,80},{17,1},{32,96},{33,49},{48,112},{49,33},{64,... | collective-permute-start | bytes 712712 | tf_op jit(solution)/shard_map/ppermute | solution.py:43
  27.7 7.5 %collective-permute-start.2 = (bf16[32,3712]{1,0:T(8,128)(2,1)S(1)}, bf16[32,3712]{1,0:T(8,128)(2,1)S(1)}, u32[]{:S(2)}, u32[]{:S(2)}) collective-permute-start(bf16[32,3712]{1,0:T(8,128)(2,1)S(1)} %assemble.1), channel_id=1, source_target_pairs={{0,192},{1,49},{16,208},{17,33},{32,224},{33,17},{48,240},{49,1},{... | collective-permute-start | bytes 712712 | tf_op jit(solution)/shard_map/ppermute | solution.py:43
  29.6 7.1 %collective-permute-start.1 = (bf16[32,3712]{1,0:T(8,128)(2,1)S(1)}, bf16[32,3712]{1,0:T(8,128)(2,1)S(1)}, u32[]{:S(2)}, u32[]{:S(2)}) collective-permute-start(bf16[32,3712]{1,0:T(8,128)(2,1)S(1)} %assemble.1), channel_id=1, source_target_pairs={{0,128},{1,33},{16,144},{17,49},{32,160},{33,1},{48,176},{49,17},{... | collective-permute-start | bytes 712712 | tf_op jit(solution)/shard_map/ppermute | solution.py:43
  31.7 25.1 %copy-start.6 = (bf16[2,32,3712]{2,1,0:T(8,128)(2,1)}, bf16[2,32,3712]{2,1,0:T(8,128)(2,1)S(1)}, u32[]{:S(2)}) copy-start(bf16[2,32,3712]{2,1,0:T(8,128)(2,1)S(1)} %pad_maximum_fusion.refs_0_) | copy-start | bytes 1425412
  31.7 12.2 %collective-permute-start.3 = (bf16[2,32,3712]{2,1,0:T(8,128)(2,1)S(1)}, bf16[2,32,3712]{2,1,0:T(8,128)(2,1)S(1)}, u32[]{:S(2)}, u32[]{:S(2)}) collective-permute-start(bf16[2,32,3712]{2,1,0:T(8,128)(2,1)S(1)} %pad_maximum_fusion.refs_0_), channel_id=1, source_target_pairs={{0,16},{1,65},{16,0},{17,81},{32,48},{33,97},{48,32},{49,113},{64,... | collective-permute-start | bytes 1425416 | tf_op jit(solution)/shard_map/ppermute | solution.py:43
  36.7 20.1 %copy-start.7 = (bf16[2,32,3712]{2,1,0:T(8,128)(2,1)}, bf16[2,32,3712]{2,1,0:T(8,128)(2,1)S(1)}, u32[]{:S(2)}) copy-start(bf16[2,32,3712]{2,1,0:T(8,128)(2,1)S(1)} %pad_maximum_fusion.1.refs_1_) | copy-start | bytes 1425412
  36.7 9.1 %collective-permute-start.4 = (bf16[2,32,3712]{2,1,0:T(8,128)(2,1)S(1)}, bf16[2,32,3712]{2,1,0:T(8,128)(2,1)S(1)}, u32[]{:S(2)}, u32[]{:S(2)}) collective-permute-start(bf16[2,32,3712]{2,1,0:T(8,128)(2,1)S(1)} %pad_maximum_fusion.1.refs_1_), channel_id=1, source_target_pairs={{0,48},{1,193},{16,32},{17,209},{32,16},{33,225},{48,0},{49,241},{... | collective-permute-start | bytes 1425416 | tf_op jit(solution)/shard_map/ppermute | solution.py:43
  39.3 4.5 %collective-permute-start.9 = (f32[1,4]{1,0:T(1,128)}, f32[1,4]{1,0:T(1,128)S(1)}, u32[]{:S(2)}, u32[]{:S(2)}) collective-permute-start(f32[1,4]{1,0:T(1,128)} %ref), channel_id=1, source_target_pairs={{0,1},{1,0},{2,3},{3,2},{4,5},{5,4},{6,7},{7,6},{8,9},{9,8},{10,11... | collective-permute-start | bytes 56 | tf_op jit(solution)/shard_map/ppermute | solution.py:30
  42.3 9.0 %collective-permute-start.6 = (bf16[2,32,3712]{2,1,0:T(8,128)(2,1)S(1)}, bf16[2,32,3712]{2,1,0:T(8,128)(2,1)S(1)}, u32[]{:S(2)}, u32[]{:S(2)}) collective-permute-start(bf16[2,32,3712]{2,1,0:T(8,128)(2,1)S(1)} %pad_maximum_fusion.refs_0_), channel_id=1, source_target_pairs={{0,48},{1,193},{16,32},{17,209},{32,16},{33,225},{48,0},{49,241},{... | collective-permute-start | bytes 1425416 | tf_op jit(solution)/shard_map/ppermute | solution.py:43
  43.8 7.8 %collective-permute-start.5 = (bf16[2,32,3712]{2,1,0:T(8,128)(2,1)S(1)}, bf16[2,32,3712]{2,1,0:T(8,128)(2,1)S(1)}, u32[]{:S(2)}, u32[]{:S(2)}) collective-permute-start(bf16[2,32,3712]{2,1,0:T(8,128)(2,1)S(1)} %pad_maximum_fusion.1.refs_1_), channel_id=1, source_target_pairs={{0,16},{1,65},{16,0},{17,81},{32,48},{33,97},{48,32},{49,113},{64,... | collective-permute-start | bytes 1425416 | tf_op jit(solution)/shard_map/ppermute | solution.py:43
  43.9 12.9 %copy-start.9 = (bf16[2,32,3712]{2,1,0:T(8,128)(2,1)}, bf16[2,32,3712]{2,1,0:T(8,128)(2,1)S(1)}, u32[]{:S(2)}) copy-start(bf16[2,32,3712]{2,1,0:T(8,128)(2,1)S(1)} %collective-permute-done.3.refs_2_) | copy-start | bytes 1425412
  43.9 12.6 %collective-permute-start.7 = (bf16[2,32,3712]{2,1,0:T(8,128)(2,1)S(1)}, bf16[2,32,3712]{2,1,0:T(8,128)(2,1)}, u32[]{:S(2)}, u32[]{:S(2)}) collective-permute-start(bf16[2,32,3712]{2,1,0:T(8,128)(2,1)S(1)} %collective-permute-done.3.refs_2_), channel_id=1, source_target_pairs={{0,48},{1,193},{16,32},{17,209},{32,16},{33,225},{48,0},{49,241},{... | collective-permute-start | bytes 1425416 | tf_op jit(solution)/shard_map/ppermute | solution.py:43
  45.8 11.0 %copy-start.10 = (bf16[2,32,3712]{2,1,0:T(8,128)(2,1)}, bf16[2,32,3712]{2,1,0:T(8,128)(2,1)S(1)}, u32[]{:S(2)}) copy-start(bf16[2,32,3712]{2,1,0:T(8,128)(2,1)S(1)} %collective-permute-done.4.refs_3_) | copy-start | bytes 1425412
  45.8 11.0 %collective-permute-start.8 = (bf16[2,32,3712]{2,1,0:T(8,128)(2,1)S(1)}, bf16[2,32,3712]{2,1,0:T(8,128)(2,1)}, u32[]{:S(2)}, u32[]{:S(2)}) collective-permute-start(bf16[2,32,3712]{2,1,0:T(8,128)(2,1)S(1)} %collective-permute-done.4.refs_3_), channel_id=1, source_target_pairs={{0,16},{1,65},{16,0},{17,81},{32,48},{33,97},{48,32},{49,113},{64,... | collective-permute-start | bytes 1425416 | tf_op jit(solution)/shard_map/ppermute | solution.py:43
  46.7 10.1 %copy-start.8 = (f32[1,512]{1,0:T(1,128)}, f32[1,512]{1,0:T(1,128)S(1)}, u32[]{:S(2)}) copy-start(f32[1,512]{1,0:T(1,128)S(1)} %dynamic_update_slice.3.refs_8_) | copy-start | bytes 6148
  46.7 52.8 %copy-start.3 = (f32[1,4]{1,0:T(1,128)S(1)}, f32[1,4]{1,0:T(1,128)}, u32[]{:S(2)}) copy-start(f32[1,4]{1,0:T(1,128)} %ref) | copy-start | bytes 52
  51.3 5.6 %copy-start.11 = (bf16[2,32,3712]{2,1,0:T(8,128)(2,1)}, bf16[2,32,3712]{2,1,0:T(8,128)(2,1)S(1)}, u32[]{:S(2)}) copy-start(bf16[2,32,3712]{2,1,0:T(8,128)(2,1)S(1)} %collective-permute-done.6.refs_5_) | copy-start | bytes 1425412
  51.6 5.3 %copy-start.12 = (bf16[2,32,3712]{2,1,0:T(8,128)(2,1)}, bf16[2,32,3712]{2,1,0:T(8,128)(2,1)S(1)}, u32[]{:S(2)}) copy-start(bf16[2,32,3712]{2,1,0:T(8,128)(2,1)S(1)} %collective-permute-done.5.refs_4_) | copy-start | bytes 1425412
  83.8 15.7 %all-to-all-start.2 = ((f32[16,2,512]{2,1,0:T(2,128)}), f32[16,2,512]{2,1,0:T(2,128)S(1)}, u32[]{:S(2)}, u32[]{:S(2)}) async-start(f32[16,2,512]{2,1,0:T(2,128)} %broadcast_in_dim.15), calls=%async_computation.2 | async-start | bytes 131072 | tf_op jit(solution)/shard_map/all_to_all | solution.py:315
  91.7 1.4 %collective-permute-start.11 = (f32[2,512]{1,0:T(2,128)}, f32[2,512]{1,0:T(2,128)S(1)}, u32[]{:S(2)}, u32[]{:S(2)}) collective-permute-start(f32[2,512]{1,0:T(2,128)} %get-tuple-element.15.own_stat), channel_id=1, source_target_pairs={{0,1},{1,0},{2,3},{3,2},{4,5},{5,4},{6,7},{7,6},{8,9},{9,8},{10,11... | collective-permute-start | bytes 12296 | tf_op jit(solution)/shard_map/ppermute | solution.py:30
  99.5 0.7 copy-start.1
  100.2 0.7 copy-start.2

commit v4 on v3

v4 whole, which is shorter than its diff:
```python
import itertools

import jax
import jax.numpy as jnp
from jax import lax
from jax.experimental import pallas as pl
from jax.experimental.pallas import tpu as pltpu
from jax.sharding import Mesh
from jax.sharding import PartitionSpec as P

NX, NY, NZ, NC = 4, 4, 8, 2
DP = ("x", "y")
VOCAB = ("z", "c")
LEN = 32
SEQS = NX * NY
ROWS = SEQS * LEN
D = 3584
PIECE = D // NZ // NC
META = 128
VOCAB_ROWS = 1000
TILE = 256
MIB = 1024 * 1024
LIMIT = 48

kto_beta = 0.1
desirable_weight = 1.0
undesirable_weight = 1.33


def swap_cores(array):
    return lax.ppermute(array, "c", [(0, 1), (1, 0)])


def split_pairs(k, first):
    pairs = []
    for x, y, c in itertools.product(range(NX), range(NY), range(NC)):
        along_x = (c == 0) == first
        u, v = (x ^ k, y) if along_x else (x, y ^ k)
        pairs.append(((x * NY + y) * NC + c, (u * NY + v) * NC + c))
    return pairs


def split_xor(array, k, first):
    return lax.ppermute(array, ("x", "y", "c"), split_pairs(k, first))


def bit_xor(a, b):
    return jnp.bitwise_xor(a, b)


def seq_of(far, near):
    x, y, c = (lax.axis_index(a) for a in ("x", "y", "c"))
    u = jnp.where(c == 0, bit_xor(x, near), bit_xor(x, far))
    v = jnp.where(c == 0, bit_xor(y, far), bit_xor(y, near))
    return u * NY + v


def assemble_kernel(pieces, line, out):
    for group in range(NZ * NC // 4):
        out[:, 4 * group * PIECE : 4 * (group + 1) * PIECE] = jnp.concatenate(
            [pieces[4 * group + i] for i in range(4)], axis=1
        )
    row = lax.broadcasted_iota(jnp.int32, (LEN, META), 0)
    lane = lax.broadcasted_iota(jnp.int32, (LEN, META), 1)

    def column(offset):
        return jnp.sum(jnp.where(lane == row + offset, line[...], 0.0), axis=1, keepdims=True)

    label = column(0).astype(jnp.int32)
    seq = lax.axis_index("x") * NY + lax.axis_index("y")
    partner = jnp.where(
        lax.axis_index("c") == 0, seq.astype(jnp.float32), line[:, 2 * LEN : 2 * LEN + 1]
    )
    fields = (
        (label & 255).astype(jnp.float32),
        ((label >> 8) & 255).astype(jnp.float32),
        (label >> 16).astype(jnp.float32),
        column(LEN),
        partner,
        line[:, 2 * LEN + 1 : 2 * LEN + 2],
    )
    meta = jnp.zeros((LEN, META), jnp.float32)
    for i, field in enumerate(fields):
        meta = jnp.where(lane == i, field, meta)
    out[:, D:] = meta.astype(jnp.bfloat16)


ORDER = tuple((far, group) for far in (0, 1, 3, 2) for group in ((0, 1), (2, 3)))
TILES = -(-VOCAB_ROWS // TILE)


def logits_kernel(*refs):
    blocks, rest = refs[: len(ORDER)], refs[len(ORDER) :]
    ref, wa, wb, out, stat, rows, target, sums = rest
    step = pl.program_id(0)
    c = lax.axis_index("c")
    chip = (lax.axis_index("x") * NY + lax.axis_index("y")) * NZ + lax.axis_index("z")

    @pl.when(step == 0)
    def _():
        for block, (far, nears) in zip(blocks, ORDER):
            for k, near in enumerate(nears):
                start = pl.multiple_of(seq_of(far, near) * LEN, LEN)
                rows[pl.ds(start, LEN), :] = block[k]
        meta = rows[:, D:]
        partner = meta[:, 4:5].astype(jnp.float32).astype(jnp.int32)
        left = lax.broadcasted_iota(jnp.int32, (ROWS, ROWS), 0)
        right = lax.broadcasted_iota(jnp.int32, (ROWS, ROWS), 1)
        same = (partner == right // LEN) & (left % LEN == right % LEN)
        moved = lax.dot_general(
            meta,
            same.astype(jnp.float32).astype(jnp.bfloat16),
            (((0,), (1,)), ((), ())),
            preferred_element_type=jnp.float32,
        )
        target[...] = (moved[0:1] + 256.0 * moved[1:2] + 65536.0 * moved[2:3]).astype(jnp.int32)
        stat[0:1] = moved[3:4]
        stat[1:2] = moved[5:6]
        sums[0:1] = jnp.zeros((1, ROWS), jnp.float32)
        sums[1:2] = -ref[...]

    vocab = step * TILE + lax.broadcasted_iota(jnp.int32, (TILE, ROWS), 0)
    valid = vocab < VOCAB_ROWS
    for weight, core in ((wa, c), (wb, 1 - c)):
        logits = lax.dot_general(
            weight[...],
            rows[:, :D],
            (((1,), (1,)), ((), ())),
            preferred_element_type=jnp.float32,
        )
        sums[0:1] += jnp.sum(jnp.where(valid, jnp.exp(logits), 0.0), axis=0, keepdims=True)
        hit = valid & (vocab == target[...] - (chip * NC + core) * VOCAB_ROWS)
        sums[1:2] += jnp.sum(jnp.where(hit, logits, 0.0), axis=0, keepdims=True)

    @pl.when(step == TILES - 1)
    def _():
        out[...] = jnp.broadcast_to(sums[...][None], out.shape)


def losses_kernel(parts, ref, logps, own_loss, loss):
    x, y, z, c = (lax.axis_index(a) for a in ("x", "y", "z", "c"))
    lane = lax.broadcasted_iota(jnp.int32, (SEQS, ROWS), 1)
    row = lax.broadcasted_iota(jnp.int32, (SEQS, ROWS), 0)
    inside = lane // LEN == row
    picked = []
    sums = []
    for core in range(NC):
        total = parts[core, 0:2]
        for i in range(1, NZ):
            total = total + parts[NC * i + core, 0:2]
        value = total[1:2] - jnp.log(total[0:1])
        picked.append(value)
        weighted = parts[core, 2:3] * value
        sums.append(jnp.sum(jnp.where(inside, weighted, 0.0), axis=1, keepdims=True))
    desirable = jnp.sum(
        jnp.where(inside & (lane % LEN == 0), parts[0, 3:4], 0.0), axis=1, keepdims=True
    )
    logratio, kl_terms = sums
    kl_estimate = jnp.sum(kl_terms, axis=0, keepdims=True) / SEQS
    wanted = desirable_weight * (1.0 - jax.nn.sigmoid(kto_beta * (logratio - kl_estimate)))
    unwanted = undesirable_weight * (1.0 - jax.nn.sigmoid(kto_beta * (kl_estimate - logratio)))
    losses = jnp.where(desirable > 0.5, wanted, unwanted)
    seq = x * NY + y
    here = lax.broadcasted_iota(jnp.int32, (SEQS, 1), 0) == seq
    own_loss[...] = jnp.sum(jnp.where(here, losses, 0.0), axis=0, keepdims=True)
    loss[...] = jnp.sum(losses, axis=0, keepdims=True) / SEQS
    half = jnp.where(z < NZ // 2, picked[0], picked[1])
    start = seq * LEN + (z % (NZ // 2)) * 8 + c * 4
    hit = lax.broadcasted_iota(jnp.int32, (8, ROWS), 1) == (
        start + lax.broadcasted_iota(jnp.int32, (8, ROWS), 0)
    )
    column = jnp.sum(jnp.where(hit, half, 0.0), axis=1, keepdims=True)
    square = lax.broadcasted_iota(jnp.int32, (8, META), 0) == lax.broadcasted_iota(
        jnp.int32, (8, META), 1
    )
    line = jnp.sum(jnp.where(square, column, 0.0), axis=0, keepdims=True)
    logps[...] = line[:, :4] + ref[...]


def whole_block(array):
    zeros = (0,) * array.ndim
    return pl.BlockSpec(array.shape, lambda i: zeros)


def small_call(kernel, name, out_shapes, *arrays):
    return pl.pallas_call(
        kernel,
        grid=(1,),
        out_shape=out_shapes,
        in_specs=[whole_block(a) for a in arrays],
        out_specs=[whole_block(a) for a in out_shapes],
        compiler_params=pltpu.CompilerParams(vmem_limit_bytes=8 * MIB),
        name=name,
    )(*arrays)


def head_call(blocks, ref, weight, other_weight):
    out_shapes = [
        jax.ShapeDtypeStruct((SEQS, 2, ROWS), jnp.float32),
        jax.ShapeDtypeStruct((2, ROWS), jnp.float32),
    ]
    tile = pl.BlockSpec((TILE, D), lambda i: (i, 0))
    return pl.pallas_call(
        logits_kernel,
        grid=(TILES,),
        out_shape=out_shapes,
        in_specs=[whole_block(a) for a in (*blocks, ref)] + [tile, tile],
        out_specs=[whole_block(a) for a in out_shapes],
        scratch_shapes=[
            pltpu.VMEM((ROWS, D + META), jnp.bfloat16),
            pltpu.VMEM((1, ROWS), jnp.int32),
            pltpu.VMEM((2, ROWS), jnp.float32),
        ],
        compiler_params=pltpu.CompilerParams(vmem_limit_bytes=LIMIT * MIB),
        cost_estimate=pl.CostEstimate(
            flops=4 * ROWS * VOCAB_ROWS * D,
            bytes_accessed=2 * (2 * VOCAB_ROWS + ROWS) * D,
            transcendentals=2 * ROWS * VOCAB_ROWS,
        ),
        name="logits",
    )(*blocks, ref, weight, other_weight)


def on_device(hidden, kl_hidden, head_weight, labels, token_mask, kl_pair, desirable, ref_logps):
    x, y, z, c = (lax.axis_index(a) for a in ("x", "y", "z", "c"))
    first = c == 0
    seq = x * NY + y
    f32 = jnp.float32
    other_weight = swap_cores(head_weight)
    ref_came = swap_cores(ref_logps)

    line = jnp.concatenate(
        [labels[0], token_mask[0], kl_pair, desirable, jnp.zeros((META - 2 * LEN - 2,), jnp.int32)]
    ).astype(f32)[None]

    copies = jnp.tile(jnp.concatenate([hidden, kl_hidden]), (NZ, 1, 1))
    pieces = lax.all_to_all(copies, VOCAB, 0, 0, tiled=True)
    pieces, other_weight, ref_came, line = lax.optimization_barrier(
        (pieces, other_weight, ref_came, line)
    )
    (rows,) = small_call(
        assemble_kernel,
        "assemble",
        [jax.ShapeDtypeStruct((LEN, D + META), jnp.bfloat16)],
        pieces,
        line,
    )

    one, three, two = lax.optimization_barrier([split_xor(rows, k, True) for k in (1, 3, 2)])
    groups = (jnp.stack([rows, one]), jnp.stack([two, three]))
    over_one = [split_xor(group, 1, False) for group in groups]
    over_three = [split_xor(group, 3, False) for group in groups]
    over_two = [split_xor(over_one[0], 3, False), split_xor(over_three[1], 1, False)]

    pair_ref = jnp.concatenate(
        [jnp.where(first, ref_logps, ref_came), jnp.where(first, ref_came, ref_logps)], axis=1
    )
    mine = (z // (NZ // 2)) == c
    ref_rows = lax.dynamic_update_slice(
        jnp.zeros((1, ROWS), f32),
        jnp.where(mine, pair_ref, 0.0),
        (0, seq * LEN + (z % (NZ // 2)) * 8),
    )
    sums, stat = head_call(
        (*groups, *over_one, *over_three, *over_two), ref_rows, head_weight, other_weight
    )

    sums = jnp.sum(lax.all_to_all(sums, DP, 0, 0, tiled=True), axis=0)
    sums = jnp.concatenate([sums, stat])
    sums = jnp.broadcast_to(sums[None], (NZ * NC, 4, ROWS))
    parts = lax.all_to_all(sums, VOCAB, 0, 0, tiled=True)
    logps, own_loss, loss = small_call(
        losses_kernel,
        "losses",
        [jax.ShapeDtypeStruct(shape, f32) for shape in ((1, 4), (1, 1), (1, 1))],
        parts,
        ref_logps,
    )
    return (logps, own_loss.reshape(1), loss.reshape(()))


def solution(mesh):
    split = Mesh(mesh.devices.reshape(NX, NY, NZ, NC), DP + VOCAB)
    in_specs = (
        P(DP, None, VOCAB),
        P(DP, None, VOCAB),
        P(DP + VOCAB, None),
        P(DP, None),
        P(DP, None),
        P(DP),
        P(DP),
        P(DP, VOCAB),
    )
    out_specs = (P(DP, VOCAB), P(DP), P())
    return jax.shard_map(
        on_device, mesh=split, in_specs=in_specs, out_specs=out_specs, check_vma=False
    )
```

time: 103 us -> 93.6 us (0.909)
  blocking collectives: 32.8 us -> 26.1 us
  waiting for transfers between devices: 23.3 us -> 29.6 us
  Pallas kernels: 16.8 us -> 12.5 us
  starting transfers between devices: 21.8 us -> 19.5 us
  local copies, waits for them, and re-layouts: 3.52 us -> 1.63 us
    all_to_all x1, blocking collectives: 21.5 us -> 15 us  [on_device(): parts = lax.all_to_all(sums, VOCAB, 0, 0, tiled=True)]
    ppermute x9, waiting for transfers between devices: 15.8 us -> 20.2 us  [split_xor(): return lax.ppermute(array, ('x', 'y', 'c'), split_pairs(k, first))]
    pallas_call x3, Pallas kernels: 16.8 us -> 12.5 us  [the longest x1 11.7 us: head_call(): pl.pallas_call(logits_kernel, grid=(TILES,), out_shape=out_shapes, in_spe...]
    unnamed x26 -> x2, local copies, waits for them, and re-layouts: 2.68 us -> 0.01 us
    all_to_all x1, waiting for transfers between devices: 6.46 us -> 8.77 us  [on_device(): pieces = lax.all_to_all(copies, VOCAB, 0, 0, tiled=True)]
    ppermute x9, starting transfers between devices: 10.7 us -> 9.16 us  [split_xor(): return lax.ppermute(array, ('x', 'y', 'c'), split_pairs(k, first))]
    ppermute x3 -> x2, starting transfers between devices: 3.32 us -> 3.51 us  [swap_cores(): return lax.ppermute(array, 'c', [(0, 1), (1, 0)])]
  transfers between devices with their start and end apart: 13 -> 12, of which waited for: 10 -> 9; matrix products, arithmetic and copies ran while one was open for 1% -> 3% of each run, Pallas kernels for 1% -> 0%
where the time goes in v4:
time: 93.6 us; the launch traced here: 93.1 us
  waiting for transfers between devices  29.6 us (32%)
  blocking collectives  26.1 us (28%)
  starting transfers between devices  19.5 us (21%)
  Pallas kernels  12.5 us (13%)
  between operations  2.01 us (2%)
  other arithmetic  1.64 us (2%)
  local copies, waits for them, and re-layouts  1.63 us (2%)
    ppermute x9, waiting for transfers between devices, split_xor(): return lax.ppermute(array, ('x', 'y', 'c'), split_pairs(k, first))  20.2 us
    all_to_all x1, blocking collectives, on_device(): parts = lax.all_to_all(sums, VOCAB, 0, 0, tiled=True)  15 us
    pallas_call x1, Pallas kernels, head_call(): pl.pallas_call(logits_kernel, grid=(TILES,), out_shape=out_shapes, in_spe...  11.7 us
    all_to_all x1, blocking collectives, on_device(): sums = jnp.sum(lax.all_to_all(sums, DP, 0, 0, tiled=True), axis=0)  11.1 us
    ppermute x9, starting transfers between devices, split_xor(): return lax.ppermute(array, ('x', 'y', 'c'), split_pairs(k, first))  9.16 us
    all_to_all x1, waiting for transfers between devices, on_device(): pieces = lax.all_to_all(copies, VOCAB, 0, 0, tiled=True)  8.77 us
    all_to_all x1, starting transfers between devices, on_device(): pieces = lax.all_to_all(copies, VOCAB, 0, 0, tiled=True)  6.86 us
    ppermute x2, starting transfers between devices, swap_cores(): return lax.ppermute(array, 'c', [(0, 1), (1, 0)])  3.51 us
  transfers between devices with their start and end apart: 12, of which 9 were waited for; matrix products, arithmetic and copies ran while one was open for 3% of the time, Pallas kernels for 0%

profile of v4, /device:TPU:1, one launch (start us, length us, event | category | flops | bytes accessed | tf_op | source)
XLA Modules:
  0.0 93.1 jit_solution(18034776425521158122)
XLA Ops:
  0.6 3.3 %collective-permute-start = (bf16[1000,3584]{1,0:T(8,128)(2,1)}, bf16[1000,3584]{1,0:T(8,128)(2,1)}, u32[]{:S(2)}, u32[]{:S(2)}) collective-permute-start(bf16[1000,3584]{1,0:T(8,128)(2,1)} %refs_9_.1), channel_id=1, source_target_pairs={{0,1},{1,0},{2,3},{3,2},{4,5},{5,4},{6,7},{7,6},{8,9},{9,8},{10,11... | collective-permute-start | bytes 21504008 | tf_op jit(solution)/shard_map/ppermute | solution.py:31
  4.0 0.7 pad_maximum_fusion.2
  4.7 0.7 tile.4
  5.4 6.9 %all-to-all-start = ((bf16[16,32,224]{2,1,0:T(8,128)(2,1)}), bf16[16,32,224]{2,1,0:T(8,128)(2,1)S(1)}, u32[]{:S(2)}, u32[]{:S(2)}) async-start(bf16[16,32,224]{2,1,0:T(8,128)(2,1)} %bitcast), calls=%async_computation | async-start | bytes 524288 | tf_op jit(solution)/shard_map/all_to_all | solution.py:237
  12.3 0.2 collective-permute-start.1
  13.8 0.8 concatenate.34
  14.6 0.7 collective-permute-done.1
  15.2 8.8 %all-to-all-done.pieces = bf16[16,32,224]{2,1,0:T(8,128)(2,1)S(1)} async-done(((bf16[16,32,224]{2,1,0:T(8,128)(2,1)}), bf16[16,32,224]{2,1,0:T(8,128)(2,1)S(1)}, u32[]{:S(2)}, u32[]{:S(2)}) %all-to-all-start) | async-done | bytes 229408 | tf_op jit(solution)/shard_map/all_to_all | solution.py:237
  24.0 0.0 collective-permute-done.refs_10_
  24.0 0.2 assemble.1
  24.2 3.0 %collective-permute-start.4 = (bf16[32,3712]{1,0:T(8,128)(2,1)S(1)}, bf16[32,3712]{1,0:T(8,128)(2,1)S(1)}, u32[]{:S(2)}, u32[]{:S(2)}) collective-permute-start(bf16[32,3712]{1,0:T(8,128)(2,1)S(1)} %assemble.1), channel_id=1, source_target_pairs={{0,128},{1,33},{16,144},{17,49},{32,160},{33,1},{48,176},{49,17},{... | collective-permute-start | bytes 712712 | tf_op jit(solution)/shard_map/ppermute | solution.py:44
  27.2 0.8 collective-permute-start.3
  27.9 0.0 collective-permute-start.2
  27.9 3.1 %collective-permute-done.4 = bf16[32,3712]{1,0:T(8,128)(2,1)S(1)} collective-permute-done((bf16[32,3712]{1,0:T(8,128)(2,1)S(1)}, bf16[32,3712]{1,0:T(8,128)(2,1)S(1)}, u32[]{:S(2)}, u32[]{:S(2)}) %collective-permute-start.4) | collective-permute-done | bytes 237600 | tf_op jit(solution)/shard_map/ppermute | solution.py:44
  31.0 2.6 %collective-permute-done.3 = bf16[32,3712]{1,0:T(8,128)(2,1)S(1)} collective-permute-done((bf16[32,3712]{1,0:T(8,128)(2,1)S(1)}, bf16[32,3712]{1,0:T(8,128)(2,1)S(1)}, u32[]{:S(2)}, u32[]{:S(2)}) %collective-permute-start.3) | collective-permute-done | bytes 237600 | tf_op jit(solution)/shard_map/ppermute | solution.py:44
  33.6 0.1 collective-permute-done.2
  33.8 0.1 pad_maximum_fusion.1.refs_1_
  33.8 2.4 %collective-permute-start.8 = (bf16[2,32,3712]{2,1,0:T(8,128)(2,1)S(1)}, bf16[2,32,3712]{2,1,0:T(8,128)(2,1)S(1)}, u32[]{:S(2)}, u32[]{:S(2)}) collective-permute-start(bf16[2,32,3712]{2,1,0:T(8,128)(2,1)S(1)} %pad_maximum_fusion.1.refs_1_), channel_id=1, source_target_pairs={{0,48},{1,193},{16,32},{17,209},{32,16},{33,225},{48,0},{49,241},{... | collective-permute-start | bytes 1425416 | tf_op jit(solution)/shard_map/ppermute | solution.py:44
  36.3 0.1 pad_maximum_fusion.refs_0_
  36.3 0.1 collective-permute-start.5
  36.4 1.5 %collective-permute-start.6 = (bf16[2,32,3712]{2,1,0:T(8,128)(2,1)S(1)}, bf16[2,32,3712]{2,1,0:T(8,128)(2,1)S(1)}, u32[]{:S(2)}, u32[]{:S(2)}) collective-permute-start(bf16[2,32,3712]{2,1,0:T(8,128)(2,1)S(1)} %pad_maximum_fusion.1.refs_1_), channel_id=1, source_target_pairs={{0,16},{1,65},{16,0},{17,81},{32,48},{33,97},{48,32},{49,113},{64,... | collective-permute-start | bytes 1425416 | tf_op jit(solution)/shard_map/ppermute | solution.py:44
  37.9 0.3 collective-permute-start.7
  38.2 4.7 %collective-permute-done.8.refs_5_ = bf16[2,32,3712]{2,1,0:T(8,128)(2,1)S(1)} collective-permute-done((bf16[2,32,3712]{2,1,0:T(8,128)(2,1)S(1)}, bf16[2,32,3712]{2,1,0:T(8,128)(2,1)S(1)}, u32[]{:S(2)}, u32[]{:S(2)}) %collective-permute-start.8) | collective-permute-done | bytes 475168 | tf_op jit(solution)/shard_map/ppermute | solution.py:44
  42.9 0.0 collective-permute-start.10
  42.9 1.3 %collective-permute-done.5.refs_2_ = bf16[2,32,3712]{2,1,0:T(8,128)(2,1)S(1)} collective-permute-done((bf16[2,32,3712]{2,1,0:T(8,128)(2,1)S(1)}, bf16[2,32,3712]{2,1,0:T(8,128)(2,1)S(1)}, u32[]{:S(2)}, u32[]{:S(2)}) %collective-permute-start.5) | collective-permute-done | bytes 475168 | tf_op jit(solution)/shard_map/ppermute | solution.py:44
  44.2 1.1 %collective-permute-start.9 = (bf16[2,32,3712]{2,1,0:T(8,128)(2,1)S(1)}, bf16[2,32,3712]{2,1,0:T(8,128)(2,1)}, u32[]{:S(2)}, u32[]{:S(2)}) collective-permute-start(bf16[2,32,3712]{2,1,0:T(8,128)(2,1)S(1)} %collective-permute-done.5.refs_2_), channel_id=1, source_target_pairs={{0,48},{1,193},{16,32},{17,209},{32,16},{33,225},{48,0},{49,241},{... | collective-permute-start | bytes 1425416 | tf_op jit(solution)/shard_map/ppermute | solution.py:44
  45.3 0.7 broadcast_select_fusion.1
  45.9 0.1 broadcast_select_fusion.2
  46.0 0.1 dynamic_update_slice.3.refs_8_
  46.1 0.0 copy-start
  46.1 3.2 %collective-permute-done.6.refs_3_ = bf16[2,32,3712]{2,1,0:T(8,128)(2,1)S(1)} collective-permute-done((bf16[2,32,3712]{2,1,0:T(8,128)(2,1)S(1)}, bf16[2,32,3712]{2,1,0:T(8,128)(2,1)S(1)}, u32[]{:S(2)}, u32[]{:S(2)}) %collective-permute-start.6) | collective-permute-done | bytes 475168 | tf_op jit(solution)/shard_map/ppermute | solution.py:44
  49.3 0.0 collective-permute-done.7.refs_4_
  49.3 5.2 %collective-permute-done.10.refs_7_ = bf16[2,32,3712]{2,1,0:T(8,128)(2,1)S(1)} collective-permute-done((bf16[2,32,3712]{2,1,0:T(8,128)(2,1)S(1)}, bf16[2,32,3712]{2,1,0:T(8,128)(2,1)S(1)}, u32[]{:S(2)}, u32[]{:S(2)}) %collective-permute-start.10) | collective-permute-done | bytes 475168 | tf_op jit(solution)/shard_map/ppermute | solution.py:44
  54.5 0.0 collective-permute-done.9.refs_6_
  54.5 11.7 %logits.1 = (f32[16,2,512]{2,1,0:T(2,128)S(1)}, f32[2,512]{1,0:T(2,128)S(1)}) custom-call(bf16[2,32,3712]{2,1,0:T(8,128)(2,1)S(1)} %pad_maximum_fusion.refs_0_, bf16[2,32,3712]{2,1,0:T(8,128)(2,1)S(1)} %pad_maximum_fusion.1.refs_1_, bf16[2,32,3712]{2,1,0:T(8,128)(2,1)S(1)} %collective-permute-done.5.refs_2_, ...), custom_call_target="tpu_custom_call" | custom-call | flops 7340032000 | bytes 18006016 | tf_op jit(solution)/shard_map/logits/pallas_call | solution.py:203
  66.2 11.1 %all_to_all.15 = f32[16,2,512]{2,1,0:T(2,128)S(1)} all-to-all(f32[16,2,512]{2,1,0:T(2,128)S(1)} %get-tuple-element.22), channel_id=1, replica_groups=mesh['x'=4,'y'=4,'z'=8,'c'=2] {'x','y'}, dimensions={0} | all-to-all | bytes 131072 | tf_op jit(solution)/shard_map/all_to_all | solution.py:268
  77.4 15.0 %all_to_all.16.parts = f32[16,4,512]{2,1,0:T(4,128)S(1)} all-to-all(f32[16,4,512]{2,1,0:T(4,128)S(1)} %broadcast_in_dim.20), channel_id=1, replica_groups=mesh['x'=4,'y'=4,'z'=8,'c'=2] {'z','c'}, dimensions={0} | all-to-all | bytes 262144 | tf_op jit(solution)/shard_map/all_to_all | solution.py:271
  92.4 0.0 copy-done
  92.4 0.6 losses.1
  (6 shorter events, 0.1 us)
Async XLA Ops:
  0.6 23.4 %collective-permute-start = (bf16[1000,3584]{1,0:T(8,128)(2,1)}, bf16[1000,3584]{1,0:T(8,128)(2,1)}, u32[]{:S(2)}, u32[]{:S(2)}) collective-permute-start(bf16[1000,3584]{1,0:T(8,128)(2,1)} %refs_9_.1), channel_id=1, source_target_pairs={{0,1},{1,0},{2,3},{3,2},{4,5},{5,4},{6,7},{7,6},{8,9},{9,8},{10,11... | collective-permute-start | bytes 21504008 | tf_op jit(solution)/shard_map/ppermute | solution.py:31
  5.4 18.6 %all-to-all-start = ((bf16[16,32,224]{2,1,0:T(8,128)(2,1)}), bf16[16,32,224]{2,1,0:T(8,128)(2,1)S(1)}, u32[]{:S(2)}, u32[]{:S(2)}) async-start(bf16[16,32,224]{2,1,0:T(8,128)(2,1)} %bitcast), calls=%async_computation | async-start | bytes 524288 | tf_op jit(solution)/shard_map/all_to_all | solution.py:237
  12.3 2.9 %collective-permute-start.1 = (f32[1,4]{1,0:T(1,128)}, f32[1,4]{1,0:T(1,128)S(1)}, u32[]{:S(2)}, u32[]{:S(2)}) collective-permute-start(f32[1,4]{1,0:T(1,128)} %ref.1), channel_id=1, source_target_pairs={{0,1},{1,0},{2,3},{3,2},{4,5},{5,4},{6,7},{7,6},{8,9},{9,8},{10,11... | collective-permute-start | bytes 56 | tf_op jit(solution)/shard_map/ppermute | solution.py:31
  24.2 6.8 %collective-permute-start.4 = (bf16[32,3712]{1,0:T(8,128)(2,1)S(1)}, bf16[32,3712]{1,0:T(8,128)(2,1)S(1)}, u32[]{:S(2)}, u32[]{:S(2)}) collective-permute-start(bf16[32,3712]{1,0:T(8,128)(2,1)S(1)} %assemble.1), channel_id=1, source_target_pairs={{0,128},{1,33},{16,144},{17,49},{32,160},{33,1},{48,176},{49,17},{... | collective-permute-start | bytes 712712 | tf_op jit(solution)/shard_map/ppermute | solution.py:44
  27.2 6.5 %collective-permute-start.3 = (bf16[32,3712]{1,0:T(8,128)(2,1)S(1)}, bf16[32,3712]{1,0:T(8,128)(2,1)S(1)}, u32[]{:S(2)}, u32[]{:S(2)}) collective-permute-start(bf16[32,3712]{1,0:T(8,128)(2,1)S(1)} %assemble.1), channel_id=1, source_target_pairs={{0,192},{1,49},{16,208},{17,33},{32,224},{33,17},{48,240},{49,1},{... | collective-permute-start | bytes 712712 | tf_op jit(solution)/shard_map/ppermute | solution.py:44
  27.9 5.8 %collective-permute-start.2 = (bf16[32,3712]{1,0:T(8,128)(2,1)S(1)}, bf16[32,3712]{1,0:T(8,128)(2,1)S(1)}, u32[]{:S(2)}, u32[]{:S(2)}) collective-permute-start(bf16[32,3712]{1,0:T(8,128)(2,1)S(1)} %assemble.1), channel_id=1, source_target_pairs={{0,64},{1,17},{16,80},{17,1},{32,96},{33,49},{48,112},{49,33},{64,... | collective-permute-start | bytes 712712 | tf_op jit(solution)/shard_map/ppermute | solution.py:44
  33.8 9.1 %collective-permute-start.8 = (bf16[2,32,3712]{2,1,0:T(8,128)(2,1)S(1)}, bf16[2,32,3712]{2,1,0:T(8,128)(2,1)S(1)}, u32[]{:S(2)}, u32[]{:S(2)}) collective-permute-start(bf16[2,32,3712]{2,1,0:T(8,128)(2,1)S(1)} %pad_maximum_fusion.1.refs_1_), channel_id=1, source_target_pairs={{0,48},{1,193},{16,32},{17,209},{32,16},{33,225},{48,0},{49,241},{... | collective-permute-start | bytes 1425416 | tf_op jit(solution)/shard_map/ppermute | solution.py:44
  36.3 7.9 %collective-permute-start.5 = (bf16[2,32,3712]{2,1,0:T(8,128)(2,1)S(1)}, bf16[2,32,3712]{2,1,0:T(8,128)(2,1)S(1)}, u32[]{:S(2)}, u32[]{:S(2)}) collective-permute-start(bf16[2,32,3712]{2,1,0:T(8,128)(2,1)S(1)} %pad_maximum_fusion.refs_0_), channel_id=1, source_target_pairs={{0,16},{1,65},{16,0},{17,81},{32,48},{33,97},{48,32},{49,113},{64,... | collective-permute-start | bytes 1425416 | tf_op jit(solution)/shard_map/ppermute | solution.py:44
  36.4 12.9 %collective-permute-start.6 = (bf16[2,32,3712]{2,1,0:T(8,128)(2,1)S(1)}, bf16[2,32,3712]{2,1,0:T(8,128)(2,1)S(1)}, u32[]{:S(2)}, u32[]{:S(2)}) collective-permute-start(bf16[2,32,3712]{2,1,0:T(8,128)(2,1)S(1)} %pad_maximum_fusion.1.refs_1_), channel_id=1, source_target_pairs={{0,16},{1,65},{16,0},{17,81},{32,48},{33,97},{48,32},{49,113},{64,... | collective-permute-start | bytes 1425416 | tf_op jit(solution)/shard_map/ppermute | solution.py:44
  37.9 11.4 %collective-permute-start.7 = (bf16[2,32,3712]{2,1,0:T(8,128)(2,1)S(1)}, bf16[2,32,3712]{2,1,0:T(8,128)(2,1)S(1)}, u32[]{:S(2)}, u32[]{:S(2)}) collective-permute-start(bf16[2,32,3712]{2,1,0:T(8,128)(2,1)S(1)} %pad_maximum_fusion.refs_0_), channel_id=1, source_target_pairs={{0,48},{1,193},{16,32},{17,209},{32,16},{33,225},{48,0},{49,241},{... | collective-permute-start | bytes 1425416 | tf_op jit(solution)/shard_map/ppermute | solution.py:44
  42.9 11.6 %collective-permute-start.10 = (bf16[2,32,3712]{2,1,0:T(8,128)(2,1)S(1)}, bf16[2,32,3712]{2,1,0:T(8,128)(2,1)S(1)}, u32[]{:S(2)}, u32[]{:S(2)}) collective-permute-start(bf16[2,32,3712]{2,1,0:T(8,128)(2,1)S(1)} %collective-permute-done.8.refs_5_), channel_id=1, source_target_pairs={{0,16},{1,65},{16,0},{17,81},{32,48},{33,97},{48,32},{49,113},{64,... | collective-permute-start | bytes 1425416 | tf_op jit(solution)/shard_map/ppermute | solution.py:44
  44.2 10.3 %collective-permute-start.9 = (bf16[2,32,3712]{2,1,0:T(8,128)(2,1)S(1)}, bf16[2,32,3712]{2,1,0:T(8,128)(2,1)}, u32[]{:S(2)}, u32[]{:S(2)}) collective-permute-start(bf16[2,32,3712]{2,1,0:T(8,128)(2,1)S(1)} %collective-permute-done.5.refs_2_), channel_id=1, source_target_pairs={{0,48},{1,193},{16,32},{17,209},{32,16},{33,225},{48,0},{49,241},{... | collective-permute-start | bytes 1425416 | tf_op jit(solution)/shard_map/ppermute | solution.py:44
  46.1 46.3 %copy-start = (f32[1,4]{1,0:T(1,128)S(1)}, f32[1,4]{1,0:T(1,128)}, u32[]{:S(2)}) copy-start(f32[1,4]{1,0:T(1,128)} %ref.1) | copy-start | bytes 52

commit v5 on v4

--- a/solution.py
+++ b/solution.py
@@ -20,7 +20,7 @@
 VOCAB_ROWS = 1000
 TILE = 256
 MIB = 1024 * 1024
-LIMIT = 48
+LIMIT = 24
 
 kto_beta = 0.1
 desirable_weight = 1.0
@@ -85,56 +85,93 @@
     out[:, D:] = meta.astype(jnp.bfloat16)
 
 
-ORDER = tuple((far, group) for far in (0, 1, 3, 2) for group in ((0, 1), (2, 3)))
+EARLY = ((0, (0, 1)), (0, (2, 3)), (1, (0, 1)), (3, (2, 3)))
+LATE = ((1, (2, 3)), (3, (0, 1)), (2, (0, 1)), (2, (2, 3)))
+PLACES = tuple((far, near) for far, nears in EARLY + LATE for near in nears)
+HALF = ROWS // 2
 TILES = -(-VOCAB_ROWS // TILE)
 
 
-def logits_kernel(*refs):
-    blocks, rest = refs[: len(ORDER)], refs[len(ORDER) :]
-    ref, wa, wb, out, stat, rows, target, sums = rest
+def take_rows(blocks, rows):
+    for i, block in enumerate(blocks):
+        for k in range(2):
+            rows[(2 * i + k) * LEN : (2 * i + k + 1) * LEN, :] = block[k]
+
+
+def tile_logits(weight, rows):
+    return lax.dot_general(
+        weight[...], rows[:, :D], (((1,), (1,)), ((), ())), preferred_element_type=jnp.float32
+    )
+
+
+def early_kernel(q0, q1, q2, q3, wa, wb, out, total, rows):
+    step = pl.program_id(0)
+
+    @pl.when(step == 0)
+    def _():
+        take_rows((q0, q1, q2, q3), rows)
+        total[...] = jnp.zeros_like(total)
+
+    valid = step * TILE + lax.broadcasted_iota(jnp.int32, (TILE, HALF), 0) < VOCAB_ROWS
+    for i, weight in enumerate((wa, wb)):
+        logits = tile_logits(weight, rows)
+        out[i] = logits
+        total[...] += jnp.sum(jnp.where(valid, jnp.exp(logits), 0.0), axis=0, keepdims=True)
+
+
+def late_kernel(q0, q1, q2, q3, m0, m1, m2, m3, total, logits_in, ref, wa, wb, *refs):
+    out, stat, rows, meta, placed, target, sums, whole = refs
     step = pl.program_id(0)
     c = lax.axis_index("c")
     chip = (lax.axis_index("x") * NY + lax.axis_index("y")) * NZ + lax.axis_index("z")
 
     @pl.when(step == 0)
     def _():
-        for block, (far, nears) in zip(blocks, ORDER):
-            for k, near in enumerate(nears):
-                start = pl.multiple_of(seq_of(far, near) * LEN, LEN)
-                rows[pl.ds(start, LEN), :] = block[k]
-        meta = rows[:, D:]
+        take_rows((q0, q1, q2, q3), rows)
+        take_rows((m0, m1, m2, m3), meta)
+        meta[HALF:] = rows[:, D:]
+        for i, (far, near) in enumerate(PLACES):
+            start = pl.multiple_of(seq_of(far, near) * LEN, LEN)
+            placed[pl.ds(start, LEN), :] = meta[i * LEN : (i + 1) * LEN, :]
         partner = meta[:, 4:5].astype(jnp.float32).astype(jnp.int32)
         left = lax.broadcasted_iota(jnp.int32, (ROWS, ROWS), 0)
         right = lax.broadcasted_iota(jnp.int32, (ROWS, ROWS), 1)
         same = (partner == right // LEN) & (left % LEN == right % LEN)
         moved = lax.dot_general(
-            meta,
+            placed[...],
             same.astype(jnp.float32).astype(jnp.bfloat16),
             (((0,), (1,)), ((), ())),
             preferred_element_type=jnp.float32,
         )
         target[...] = (moved[0:1] + 256.0 * moved[1:2] + 65536.0 * moved[2:3]).astype(jnp.int32)
-        stat[0:1] = moved[3:4]
-        stat[1:2] = moved[5:6]
-        sums[0:1] = jnp.zeros((1, ROWS), jnp.float32)
-        sums[1:2] = -ref[...]
-
-    vocab = step * TILE + lax.broadcasted_iota(jnp.int32, (TILE, ROWS), 0)
+        sums[...] = jnp.zeros_like(sums)
+        sums[0:1, :HALF] = total[...]
+        sums[2:3] = moved[3:4]
+        sums[3:4] = moved[5:6]
+
+    vocab = step * TILE + lax.broadcasted_iota(jnp.int32, (TILE, HALF), 0)
     valid = vocab < VOCAB_ROWS
-    for weight, core in ((wa, c), (wb, 1 - c)):
-        logits = lax.dot_general(
-            weight[...],
-            rows[:, :D],
-            (((1,), (1,)), ((), ())),
-            preferred_element_type=jnp.float32,
+    for i, (weight, core) in enumerate(((wa, c), (wb, 1 - c))):
+        logits = tile_logits(weight, rows)
+        wanted = target[...] - (chip * NC + core) * VOCAB_ROWS
+        sums[0:1, HALF:] += jnp.sum(
+            jnp.where(valid, jnp.exp(logits), 0.0), axis=0, keepdims=True
         )
-        sums[0:1] += jnp.sum(jnp.where(valid, jnp.exp(logits), 0.0), axis=0, keepdims=True)
-        hit = valid & (vocab == target[...] - (chip * NC + core) * VOCAB_ROWS)
-        sums[1:2] += jnp.sum(jnp.where(hit, logits, 0.0), axis=0, keepdims=True)
+        for half, values in ((wanted[:, :HALF], logits_in[i]), (wanted[:, HALF:], logits)):
+            picked = jnp.where(valid & (vocab == half), values, 0.0)
+            at = slice(0, HALF) if values is not logits else slice(HALF, ROWS)
+            sums[1:2, at] += jnp.sum(picked, axis=0, keepdims=True)
 
     @pl.when(step == TILES - 1)
     def _():
-        out[...] = jnp.broadcast_to(sums[...][None], out.shape)
+        turned = jnp.transpose(sums[...])
+        for i, (far, near) in enumerate(PLACES):
+            start = pl.multiple_of(seq_of(far, near) * LEN, LEN)
+            whole[pl.ds(start, LEN), :] = turned[i * LEN : (i + 1) * LEN, :]
+        final = jnp.transpose(whole[...])
+        out[:, 0:1] = jnp.broadcast_to(final[0:1][None], (SEQS, 1, ROWS))
+        out[:, 1:2] = jnp.broadcast_to((final[1:2] - ref[...])[None], (SEQS, 1, ROWS))
+        stat[...] = final[2:4]
 
 
 def losses_kernel(parts, ref, logps, own_loss, loss):
@@ -194,31 +231,65 @@
     )(*arrays)
 
 
-def head_call(blocks, ref, weight, other_weight):
-    out_shapes = [
-        jax.ShapeDtypeStruct((SEQS, 2, ROWS), jnp.float32),
-        jax.ShapeDtypeStruct((2, ROWS), jnp.float32),
-    ]
+def head_call(kernel, name, outs, arrays, in_specs, scratch, weights):
     tile = pl.BlockSpec((TILE, D), lambda i: (i, 0))
     return pl.pallas_call(
-        logits_kernel,
+        kernel,
         grid=(TILES,),
-        out_shape=out_shapes,
-        in_specs=[whole_block(a) for a in (*blocks, ref)] + [tile, tile],
-        out_specs=[whole_block(a) for a in out_shapes],
-        scratch_shapes=[
-            pltpu.VMEM((ROWS, D + META), jnp.bfloat16),
-            pltpu.VMEM((1, ROWS), jnp.int32),
-            pltpu.VMEM((2, ROWS), jnp.float32),
-        ],
+        out_shape=[shape for shape, _ in outs],
+        in_specs=[*in_specs, tile, tile],
+        out_specs=[spec for _, spec in outs],
+        scratch_shapes=scratch,
         compiler_params=pltpu.CompilerParams(vmem_limit_bytes=LIMIT * MIB),
         cost_estimate=pl.CostEstimate(
-            flops=4 * ROWS * VOCAB_ROWS * D,
-            bytes_accessed=2 * (2 * VOCAB_ROWS + ROWS) * D,
-            transcendentals=2 * ROWS * VOCAB_ROWS,
+            flops=4 * HALF * VOCAB_ROWS * D,
+            bytes_accessed=2 * (2 * VOCAB_ROWS + HALF) * D,
+            transcendentals=2 * HALF * VOCAB_ROWS,
         ),
-        name="logits",
-    )(*blocks, ref, weight, other_weight)
+        name=name,
+    )(*arrays, *weights)
+
+
+def logit_sums(early, late, ref, weights):
+    f32 = jnp.float32
+    tiles = pl.BlockSpec((NC, TILE, HALF), lambda i: (0, i, 0))
+    line = jax.ShapeDtypeStruct((1, HALF), f32)
+    held = pltpu.VMEM((HALF, D + META), jnp.bfloat16)
+    logits, total = head_call(
+        early_kernel,
+        "early",
+        [
+            (jax.ShapeDtypeStruct((NC, TILES * TILE, HALF), f32), tiles),
+            (line, whole_block(line)),
+        ],
+        early,
+        [whole_block(a) for a in early],
+        [held],
+        weights,
+    )
+    outs = [
+        jax.ShapeDtypeStruct((SEQS, 2, ROWS), f32),
+        jax.ShapeDtypeStruct((2, ROWS), f32),
+    ]
+    meta = pl.BlockSpec((2, LEN, META), lambda i: (0, 0, D // META))
+    return head_call(
+        late_kernel,
+        "late",
+        [(a, whole_block(a)) for a in outs],
+        (*late, *early, total, logits, ref),
+        [whole_block(a) for a in late]
+        + [meta] * len(early)
+        + [whole_block(total), tiles, whole_block(ref)],
+        [
+            held,
+            pltpu.VMEM((ROWS, META), jnp.bfloat16),
+            pltpu.VMEM((ROWS, META), jnp.bfloat16),
+            pltpu.VMEM((1, ROWS), jnp.int32),
+            pltpu.VMEM((META, ROWS), f32),
+            pltpu.VMEM((ROWS, META), f32),
+        ],
+        weights,
+    )
 
 
 def on_device(hidden, kl_hidden, head_weight, labels, token_mask, kl_pair, desirable, ref_logps):
@@ -233,7 +304,9 @@
         [labels[0], token_mask[0], kl_pair, desirable, jnp.zeros((META - 2 * LEN - 2,), jnp.int32)]
     ).astype(f32)[None]
 
-    copies = jnp.tile(jnp.concatenate([hidden, kl_hidden]), (NZ, 1, 1))
+    shape = (NZ * NC, *hidden.shape[1:])
+    core = lax.broadcasted_iota(jnp.int32, shape, 0) % NC
+    copies = jnp.where(core == 0, hidden, kl_hidden)
     pieces = lax.all_to_all(copies, VOCAB, 0, 0, tiled=True)
     pieces, other_weight, ref_came, line = lax.optimization_barrier(
         (pieces, other_weight, ref_came, line)
@@ -261,8 +334,11 @@
         jnp.where(mine, pair_ref, 0.0),
         (0, seq * LEN + (z % (NZ // 2)) * 8),
     )
-    sums, stat = head_call(
-        (*groups, *over_one, *over_three, *over_two), ref_rows, head_weight, other_weight
+    sums, stat = logit_sums(
+        (*groups, over_one[0], over_three[1]),
+        (over_one[1], over_three[0], *over_two),
+        ref_rows,
+        (head_weight, other_weight),
     )
 
     sums = jnp.sum(lax.all_to_all(sums, DP, 0, 0, tiled=True), axis=0)

time: 93.6 us -> 92.7 us (level)
  waiting for transfers between devices: 29.6 us -> 19.3 us
  Pallas kernels: 12.5 us -> 15.5 us
  blocking collectives: 26.1 us -> 28.6 us
  local copies, waits for them, and re-layouts: 1.63 us -> 3.93 us
  starting transfers between devices: 19.5 us -> 20.5 us
    ppermute x9, waiting for transfers between devices: 20.2 us -> 9.81 us  [split_xor(): return lax.ppermute(array, ('x', 'y', 'c'), split_pairs(k, first))]
    unnamed x2 -> x4, local copies, waits for them, and re-layouts: 0.01 us -> 3.04 us
    pallas_call x1 -> x2, Pallas kernels: 11.7 us -> 14.7 us  [head_call(): pl.pallas_call(kernel, grid=(TILES,), out_shape=[shape for shape, _ in ou...]
    all_to_all x1, blocking collectives: 11.1 us -> 12.9 us  [on_device(): sums = jnp.sum(lax.all_to_all(sums, DP, 0, 0, tiled=True), axis=0)]
    select_n x0 -> x1, other arithmetic: none -> 1.55 us  [on_device(): copies = jnp.where(core == 0, hidden, kl_hidden)]
  transfers between devices with their start and end apart: 12 -> 12, of which waited for: 9 -> 7; matrix products, arithmetic and copies ran while one was open for 3% -> 3% of each run, Pallas kernels for 0% -> 7%
where the time goes in v5:
time: 92.7 us; the launch traced here: 92.2 us
  blocking collectives  28.6 us (31%)
  starting transfers between devices  20.5 us (22%)
  waiting for transfers between devices  19.3 us (21%)
  Pallas kernels  15.5 us (17%)
  local copies, waits for them, and re-layouts  3.93 us (4%)
  other arithmetic  2.45 us (3%)
  between operations  2.04 us (2%)
    all_to_all x1, blocking collectives, on_device(): parts = lax.all_to_all(sums, VOCAB, 0, 0, tiled=True)  15.8 us
    pallas_call x2, Pallas kernels, head_call(): pl.pallas_call(kernel, grid=(TILES,), out_shape=[shape for shape, _ in ou...  14.7 us
    all_to_all x1, blocking collectives, on_device(): sums = jnp.sum(lax.all_to_all(sums, DP, 0, 0, tiled=True), axis=0)  12.9 us
    ppermute x9, starting transfers between devices, split_xor(): return lax.ppermute(array, ('x', 'y', 'c'), split_pairs(k, first))  10.1 us
    ppermute x9, waiting for transfers between devices, split_xor(): return lax.ppermute(array, ('x', 'y', 'c'), split_pairs(k, first))  9.81 us
    all_to_all x1, waiting for transfers between devices, on_device(): pieces = lax.all_to_all(copies, VOCAB, 0, 0, tiled=True)  8.85 us
    all_to_all x1, starting transfers between devices, on_device(): pieces = lax.all_to_all(copies, VOCAB, 0, 0, tiled=True)  6.86 us
    ppermute x2, starting transfers between devices, swap_cores(): return lax.ppermute(array, 'c', [(0, 1), (1, 0)])  3.51 us
  transfers between devices with their start and end apart: 12, of which 7 were waited for; matrix products, arithmetic and copies ran while one was open for 3% of the time, Pallas kernels for 7%

profile of v5, /device:TPU:1, one launch (start us, length us, event | category | flops | bytes accessed | tf_op | source)
XLA Modules:
  0.0 92.2 jit_solution(10488883303902965343)
XLA Ops:
  0.6 3.3 %collective-permute-start = (bf16[1000,3584]{1,0:T(8,128)(2,1)}, bf16[1000,3584]{1,0:T(8,128)(2,1)}, u32[]{:S(2)}, u32[]{:S(2)}) collective-permute-start(bf16[1000,3584]{1,0:T(8,128)(2,1)} %wa.3), channel_id=1, source_target_pairs={{0,1},{1,0},{2,3},{3,2},{4,5},{5,4},{6,7},{7,6},{8,9},{9,8},{10,11... | collective-permute-start | bytes 21504008 | tf_op jit(solution)/shard_map/ppermute | solution.py:31
  4.0 1.5 %fusion = bf16[16,32,224]{2,1,0:T(8,128)(2,1)} fusion(s32[16]{0:T(128)S(1)} %get-tuple-element.33, s32[16]{0:T(128)S(1)} %get-tuple-element.34, pred[16]{0:T(512)(128)(4,1)S(1)} %compare_and_fusion, bf16[32,224]{1,0:T(8,128)(2,1)} %bitcast.16, bf16[32,224]{1,0:T(8,128)(2,1)} %bitcast.17), kind=kLoop, calls=%fused_computation.1 | loop fusion | flops 344064 | bytes 258192 | tf_op jit(solution)/shard_map/jit(_where)/select_n | solution.py:309
  5.5 6.9 %all-to-all-start = ((bf16[16,32,224]{2,1,0:T(8,128)(2,1)}), bf16[16,32,224]{2,1,0:T(8,128)(2,1)S(1)}, u32[]{:S(2)}, u32[]{:S(2)}) async-start(bf16[16,32,224]{2,1,0:T(8,128)(2,1)} %fusion), calls=%async_computation | async-start | bytes 524288 | tf_op jit(solution)/shard_map/all_to_all | solution.py:310
  12.4 0.2 collective-permute-start.1
  13.9 0.8 concatenate.30
  14.6 0.6 collective-permute-done.1
  15.2 8.8 %all-to-all-done.pieces = bf16[16,32,224]{2,1,0:T(8,128)(2,1)S(1)} async-done(((bf16[16,32,224]{2,1,0:T(8,128)(2,1)}), bf16[16,32,224]{2,1,0:T(8,128)(2,1)S(1)}, u32[]{:S(2)}, u32[]{:S(2)}) %all-to-all-start) | async-done | bytes 229408 | tf_op jit(solution)/shard_map/all_to_all | solution.py:310
  24.1 0.0 collective-permute-done.wb
  24.1 0.2 assemble.1
  24.2 3.0 %collective-permute-start.4 = (bf16[32,3712]{1,0:T(8,128)(2,1)S(1)}, bf16[32,3712]{1,0:T(8,128)(2,1)S(1)}, u32[]{:S(2)}, u32[]{:S(2)}) collective-permute-start(bf16[32,3712]{1,0:T(8,128)(2,1)S(1)} %assemble.1), channel_id=1, source_target_pairs={{0,128},{1,33},{16,144},{17,49},{32,160},{33,1},{48,176},{49,17},{... | collective-permute-start | bytes 712712 | tf_op jit(solution)/shard_map/ppermute | solution.py:44
  27.2 0.8 collective-permute-start.3
  28.0 0.0 collective-permute-start.2
  28.0 3.1 %collective-permute-done.4 = bf16[32,3712]{1,0:T(8,128)(2,1)S(1)} collective-permute-done((bf16[32,3712]{1,0:T(8,128)(2,1)S(1)}, bf16[32,3712]{1,0:T(8,128)(2,1)S(1)}, u32[]{:S(2)}, u32[]{:S(2)}) %collective-permute-start.4) | collective-permute-done | bytes 237600 | tf_op jit(solution)/shard_map/ppermute | solution.py:44
  31.1 2.6 %collective-permute-done.3 = bf16[32,3712]{1,0:T(8,128)(2,1)S(1)} collective-permute-done((bf16[32,3712]{1,0:T(8,128)(2,1)S(1)}, bf16[32,3712]{1,0:T(8,128)(2,1)S(1)}, u32[]{:S(2)}, u32[]{:S(2)}) %collective-permute-start.3) | collective-permute-done | bytes 237600 | tf_op jit(solution)/shard_map/ppermute | solution.py:44
  33.7 0.1 collective-permute-done.2
  33.8 0.1 pad_maximum_fusion.1.q0.m0
  33.9 1.2 %collective-permute-start.7 = (bf16[2,32,3712]{2,1,0:T(8,128)(2,1)S(1)}, bf16[2,32,3712]{2,1,0:T(8,128)(2,1)S(1)}, u32[]{:S(2)}, u32[]{:S(2)}) collective-permute-start(bf16[2,32,3712]{2,1,0:T(8,128)(2,1)S(1)} %pad_maximum_fusion.1.q0.m0), channel_id=1, source_target_pairs={{0,16},{1,65},{16,0},{17,81},{32,48},{33,97},{48,32},{49,113},{64,... | collective-permute-start | bytes 1425416 | tf_op jit(solution)/shard_map/ppermute | solution.py:44
  35.1 0.1 pad_maximum_fusion.q1.m1
  35.1 1.9 %collective-permute-start.9 = (bf16[2,32,3712]{2,1,0:T(8,128)(2,1)S(1)}, bf16[2,32,3712]{2,1,0:T(8,128)(2,1)S(1)}, u32[]{:S(2)}, u32[]{:S(2)}) collective-permute-start(bf16[2,32,3712]{2,1,0:T(8,128)(2,1)S(1)} %pad_maximum_fusion.q1.m1), channel_id=1, source_target_pairs={{0,48},{1,193},{16,32},{17,209},{32,16},{33,225},{48,0},{49,241},{... | collective-permute-start | bytes 1425416 | tf_op jit(solution)/shard_map/ppermute | solution.py:44
  37.0 0.9 collective-permute-start.6
  37.9 0.0 collective-permute-start.5
  37.9 3.9 %collective-permute-done.7.q2.m2 = bf16[2,32,3712]{2,1,0:T(8,128)(2,1)S(1)} collective-permute-done((bf16[2,32,3712]{2,1,0:T(8,128)(2,1)S(1)}, bf16[2,32,3712]{2,1,0:T(8,128)(2,1)S(1)}, u32[]{:S(2)}, u32[]{:S(2)}) %collective-permute-start.7) | collective-permute-done | bytes 475168 | tf_op jit(solution)/shard_map/ppermute | solution.py:44
  41.8 2.4 %collective-permute-start.8 = (bf16[2,32,3712]{2,1,0:T(8,128)(2,1)S(1)}, bf16[2,32,3712]{2,1,0:T(8,128)(2,1)S(1)}, u32[]{:S(2)}, u32[]{:S(2)}) collective-permute-start(bf16[2,32,3712]{2,1,0:T(8,128)(2,1)S(1)} %collective-permute-done.7.q2.m2), channel_id=1, source_target_pairs={{0,48},{1,193},{16,32},{17,209},{32,16},{33,225},{48,0},{49,241},{... | collective-permute-start | bytes 1425416 | tf_op jit(solution)/shard_map/ppermute | solution.py:44
  44.1 0.1 collective-permute-done.9.q3.m3
  44.2 0.0 collective-permute-start.10
  44.2 0.7 broadcast_select_fusion.1
  44.9 0.1 broadcast_select_fusion.2
  45.0 0.1 dynamic_update_slice.3.ref
  45.1 0.0 copy-start
  45.1 3.0 %copy-done = bf16[1000,3584]{1,0:T(8,128)(2,1)S(1)} copy-done((bf16[1000,3584]{1,0:T(8,128)(2,1)S(1)}, bf16[1000,3584]{1,0:T(8,128)(2,1)}, u32[]{:S(2)}) %copy-start) | copy-done | bytes 7168024
  48.1 6.8 %early.1 = (f32[2,1024,256]{2,1,0:T(8,128)S(1)}, f32[1,256]{1,0:T(1,128)S(1)}) custom-call(bf16[2,32,3712]{2,1,0:T(8,128)(2,1)S(1)} %pad_maximum_fusion.1.q0.m0, bf16[2,32,3712]{2,1,0:T(8,128)(2,1)S(1)} %pad_maximum_fusion.q1.m1, bf16[2,32,3712]{2,1,0:T(8,128)(2,1)S(1)} %collective-permute-done.7.q2.m2, ...), custom_call_target="tpu_custom_call" | custom-call | flops 3670016000 | bytes 16171008 | tf_op jit(solution)/shard_map/early/pallas_call | solution.py:236
  54.9 0.0 collective-permute-done.6.q1
  54.9 0.0 collective-permute-done.5.q0
  54.9 0.0 collective-permute-done.8.q2
  54.9 0.0 collective-permute-done.10.q3
  54.9 0.0 copy-start.1
  55.0 7.9 %late.1 = (f32[16,2,512]{2,1,0:T(2,128)S(1)}, f32[2,512]{1,0:T(2,128)S(1)}) custom-call(bf16[2,32,3712]{2,1,0:T(8,128)(2,1)S(1)} %collective-permute-done.5.q0, bf16[2,32,3712]{2,1,0:T(8,128)(2,1)S(1)} %collective-permute-done.6.q1, bf16[2,32,3712]{2,1,0:T(8,128)(2,1)S(1)} %collective-permute-done.8.q2, bf16[2,32,3712]{2,1,0:T(8,128)(2,1)} %collective-permute-done.10.q3, ...), custom_call_target="tpu_custom_call" | custom-call | flops 3670016000 | bytes 16171008 | tf_op jit(solution)/shard_map/late/pallas_call | solution.py:236
  62.9 12.9 %all_to_all.15 = f32[16,2,512]{2,1,0:T(2,128)S(1)} all-to-all(f32[16,2,512]{2,1,0:T(2,128)S(1)} %get-tuple-element.26), channel_id=1, replica_groups=mesh['x'=4,'y'=4,'z'=8,'c'=2] {'x','y'}, dimensions={0} | all-to-all | bytes 131072 | tf_op jit(solution)/shard_map/all_to_all | solution.py:344
  75.8 15.8 %all_to_all.16.parts = f32[16,4,512]{2,1,0:T(4,128)S(1)} all-to-all(f32[16,4,512]{2,1,0:T(4,128)S(1)} %broadcast_in_dim.44), channel_id=1, replica_groups=mesh['x'=4,'y'=4,'z'=8,'c'=2] {'z','c'}, dimensions={0} | all-to-all | bytes 262144 | tf_op jit(solution)/shard_map/all_to_all | solution.py:347
  91.6 0.0 copy-done.1
  91.6 0.6 losses.1
  (8 shorter events, 0.1 us)
Async XLA Ops:
  0.6 23.5 %collective-permute-start = (bf16[1000,3584]{1,0:T(8,128)(2,1)}, bf16[1000,3584]{1,0:T(8,128)(2,1)}, u32[]{:S(2)}, u32[]{:S(2)}) collective-permute-start(bf16[1000,3584]{1,0:T(8,128)(2,1)} %wa.3), channel_id=1, source_target_pairs={{0,1},{1,0},{2,3},{3,2},{4,5},{5,4},{6,7},{7,6},{8,9},{9,8},{10,11... | collective-permute-start | bytes 21504008 | tf_op jit(solution)/shard_map/ppermute | solution.py:31
  5.5 18.6 %all-to-all-start = ((bf16[16,32,224]{2,1,0:T(8,128)(2,1)}), bf16[16,32,224]{2,1,0:T(8,128)(2,1)S(1)}, u32[]{:S(2)}, u32[]{:S(2)}) async-start(bf16[16,32,224]{2,1,0:T(8,128)(2,1)} %fusion), calls=%async_computation | async-start | bytes 524288 | tf_op jit(solution)/shard_map/all_to_all | solution.py:310
  12.4 2.9 %collective-permute-start.1 = (f32[1,4]{1,0:T(1,128)}, f32[1,4]{1,0:T(1,128)S(1)}, u32[]{:S(2)}, u32[]{:S(2)}) collective-permute-start(f32[1,4]{1,0:T(1,128)} %ref.1), channel_id=1, source_target_pairs={{0,1},{1,0},{2,3},{3,2},{4,5},{5,4},{6,7},{7,6},{8,9},{9,8},{10,11... | collective-permute-start | bytes 56 | tf_op jit(solution)/shard_map/ppermute | solution.py:31
  24.2 6.8 %collective-permute-start.4 = (bf16[32,3712]{1,0:T(8,128)(2,1)S(1)}, bf16[32,3712]{1,0:T(8,128)(2,1)S(1)}, u32[]{:S(2)}, u32[]{:S(2)}) collective-permute-start(bf16[32,3712]{1,0:T(8,128)(2,1)S(1)} %assemble.1), channel_id=1, source_target_pairs={{0,128},{1,33},{16,144},{17,49},{32,160},{33,1},{48,176},{49,17},{... | collective-permute-start | bytes 712712 | tf_op jit(solution)/shard_map/ppermute | solution.py:44
  27.2 6.5 %collective-permute-start.3 = (bf16[32,3712]{1,0:T(8,128)(2,1)S(1)}, bf16[32,3712]{1,0:T(8,128)(2,1)S(1)}, u32[]{:S(2)}, u32[]{:S(2)}) collective-permute-start(bf16[32,3712]{1,0:T(8,128)(2,1)S(1)} %assemble.1), channel_id=1, source_target_pairs={{0,192},{1,49},{16,208},{17,33},{32,224},{33,17},{48,240},{49,1},{... | collective-permute-start | bytes 712712 | tf_op jit(solution)/shard_map/ppermute | solution.py:44
  28.0 5.8 %collective-permute-start.2 = (bf16[32,3712]{1,0:T(8,128)(2,1)S(1)}, bf16[32,3712]{1,0:T(8,128)(2,1)S(1)}, u32[]{:S(2)}, u32[]{:S(2)}) collective-permute-start(bf16[32,3712]{1,0:T(8,128)(2,1)S(1)} %assemble.1), channel_id=1, source_target_pairs={{0,64},{1,17},{16,80},{17,1},{32,96},{33,49},{48,112},{49,33},{64,... | collective-permute-start | bytes 712712 | tf_op jit(solution)/shard_map/ppermute | solution.py:44
  33.9 7.9 %collective-permute-start.7 = (bf16[2,32,3712]{2,1,0:T(8,128)(2,1)S(1)}, bf16[2,32,3712]{2,1,0:T(8,128)(2,1)S(1)}, u32[]{:S(2)}, u32[]{:S(2)}) collective-permute-start(bf16[2,32,3712]{2,1,0:T(8,128)(2,1)S(1)} %pad_maximum_fusion.1.q0.m0), channel_id=1, source_target_pairs={{0,16},{1,65},{16,0},{17,81},{32,48},{33,97},{48,32},{49,113},{64,... | collective-permute-start | bytes 1425416 | tf_op jit(solution)/shard_map/ppermute | solution.py:44
  35.1 9.1 %collective-permute-start.9 = (bf16[2,32,3712]{2,1,0:T(8,128)(2,1)S(1)}, bf16[2,32,3712]{2,1,0:T(8,128)(2,1)S(1)}, u32[]{:S(2)}, u32[]{:S(2)}) collective-permute-start(bf16[2,32,3712]{2,1,0:T(8,128)(2,1)S(1)} %pad_maximum_fusion.q1.m1), channel_id=1, source_target_pairs={{0,48},{1,193},{16,32},{17,209},{32,16},{33,225},{48,0},{49,241},{... | collective-permute-start | bytes 1425416 | tf_op jit(solution)/shard_map/ppermute | solution.py:44
  37.0 17.9 %collective-permute-start.6 = (bf16[2,32,3712]{2,1,0:T(8,128)(2,1)S(1)}, bf16[2,32,3712]{2,1,0:T(8,128)(2,1)S(1)}, u32[]{:S(2)}, u32[]{:S(2)}) collective-permute-start(bf16[2,32,3712]{2,1,0:T(8,128)(2,1)S(1)} %pad_maximum_fusion.1.q0.m0), channel_id=1, source_target_pairs={{0,48},{1,193},{16,32},{17,209},{32,16},{33,225},{48,0},{49,241},{... | collective-permute-start | bytes 1425416 | tf_op jit(solution)/shard_map/ppermute | solution.py:44
  37.9 17.0 %collective-permute-start.5 = (bf16[2,32,3712]{2,1,0:T(8,128)(2,1)S(1)}, bf16[2,32,3712]{2,1,0:T(8,128)(2,1)S(1)}, u32[]{:S(2)}, u32[]{:S(2)}) collective-permute-start(bf16[2,32,3712]{2,1,0:T(8,128)(2,1)S(1)} %pad_maximum_fusion.q1.m1), channel_id=1, source_target_pairs={{0,16},{1,65},{16,0},{17,81},{32,48},{33,97},{48,32},{49,113},{64,... | collective-permute-start | bytes 1425416 | tf_op jit(solution)/shard_map/ppermute | solution.py:44
  41.8 13.1 %collective-permute-start.8 = (bf16[2,32,3712]{2,1,0:T(8,128)(2,1)S(1)}, bf16[2,32,3712]{2,1,0:T(8,128)(2,1)S(1)}, u32[]{:S(2)}, u32[]{:S(2)}) collective-permute-start(bf16[2,32,3712]{2,1,0:T(8,128)(2,1)S(1)} %collective-permute-done.7.q2.m2), channel_id=1, source_target_pairs={{0,48},{1,193},{16,32},{17,209},{32,16},{33,225},{48,0},{49,241},{... | collective-permute-start | bytes 1425416 | tf_op jit(solution)/shard_map/ppermute | solution.py:44
  44.2 10.7 %collective-permute-start.10 = (bf16[2,32,3712]{2,1,0:T(8,128)(2,1)S(1)}, bf16[2,32,3712]{2,1,0:T(8,128)(2,1)}, u32[]{:S(2)}, u32[]{:S(2)}) collective-permute-start(bf16[2,32,3712]{2,1,0:T(8,128)(2,1)S(1)} %collective-permute-done.9.q3.m3), channel_id=1, source_target_pairs={{0,16},{1,65},{16,0},{17,81},{32,48},{33,97},{48,32},{49,113},{64,... | collective-permute-start | bytes 1425416 | tf_op jit(solution)/shard_map/ppermute | solution.py:44
  45.1 3.0 %copy-start = (bf16[1000,3584]{1,0:T(8,128)(2,1)S(1)}, bf16[1000,3584]{1,0:T(8,128)(2,1)}, u32[]{:S(2)}) copy-start(bf16[1000,3584]{1,0:T(8,128)(2,1)} %wa.3) | copy-start | bytes 21504004
  54.9 36.6 %copy-start.1 = (f32[1,4]{1,0:T(1,128)S(1)}, f32[1,4]{1,0:T(1,128)}, u32[]{:S(2)}) copy-start(f32[1,4]{1,0:T(1,128)} %ref.1) | copy-start | bytes 52

commit v6 on v5

--- a/solution.py
+++ b/solution.py
@@ -20,7 +20,7 @@
 VOCAB_ROWS = 1000
 TILE = 256
 MIB = 1024 * 1024
-LIMIT = 24
+EARLY_LIMIT, LATE_LIMIT = 36, 24
 
 kto_beta = 0.1
 desirable_weight = 1.0
@@ -104,7 +104,7 @@
     )
 
 
-def early_kernel(q0, q1, q2, q3, wa, wb, out, total, rows):
+def early_kernel(q0, q1, q2, q3, wa, wb, out, total, wa_out, wb_out, rows):
     step = pl.program_id(0)
 
     @pl.when(step == 0)
@@ -113,6 +113,8 @@
         total[...] = jnp.zeros_like(total)
 
     valid = step * TILE + lax.broadcasted_iota(jnp.int32, (TILE, HALF), 0) < VOCAB_ROWS
+    wa_out[...] = wa[...]
+    wb_out[...] = wb[...]
     for i, weight in enumerate((wa, wb)):
         logits = tile_logits(weight, rows)
         out[i] = logits
@@ -136,7 +138,7 @@
         partner = meta[:, 4:5].astype(jnp.float32).astype(jnp.int32)
         left = lax.broadcasted_iota(jnp.int32, (ROWS, ROWS), 0)
         right = lax.broadcasted_iota(jnp.int32, (ROWS, ROWS), 1)
-        same = (partner == right // LEN) & (left % LEN == right % LEN)
+        same = (partner == (right >> 5)) & (((left ^ right) & (LEN - 1)) == 0)
         moved = lax.dot_general(
             placed[...],
             same.astype(jnp.float32).astype(jnp.bfloat16),
@@ -231,7 +233,7 @@
     )(*arrays)
 
 
-def head_call(kernel, name, outs, arrays, in_specs, scratch, weights):
+def head_call(kernel, name, outs, arrays, in_specs, scratch, weights, limit):
     tile = pl.BlockSpec((TILE, D), lambda i: (i, 0))
     return pl.pallas_call(
         kernel,
@@ -240,7 +242,7 @@
         in_specs=[*in_specs, tile, tile],
         out_specs=[spec for _, spec in outs],
         scratch_shapes=scratch,
-        compiler_params=pltpu.CompilerParams(vmem_limit_bytes=LIMIT * MIB),
+        compiler_params=pltpu.CompilerParams(vmem_limit_bytes=limit * MIB),
         cost_estimate=pl.CostEstimate(
             flops=4 * HALF * VOCAB_ROWS * D,
             bytes_accessed=2 * (2 * VOCAB_ROWS + HALF) * D,
@@ -255,17 +257,22 @@
     tiles = pl.BlockSpec((NC, TILE, HALF), lambda i: (0, i, 0))
     line = jax.ShapeDtypeStruct((1, HALF), f32)
     held = pltpu.VMEM((HALF, D + META), jnp.bfloat16)
-    logits, total = head_call(
+    weight = jax.ShapeDtypeStruct((VOCAB_ROWS, D), jnp.bfloat16)
+    tile = pl.BlockSpec((TILE, D), lambda i: (i, 0))
+    logits, total, *weights = head_call(
         early_kernel,
         "early",
         [
             (jax.ShapeDtypeStruct((NC, TILES * TILE, HALF), f32), tiles),
             (line, whole_block(line)),
+            (weight, tile),
+            (weight, tile),
         ],
         early,
         [whole_block(a) for a in early],
         [held],
         weights,
+        EARLY_LIMIT,
     )
     outs = [
         jax.ShapeDtypeStruct((SEQS, 2, ROWS), f32),
@@ -289,6 +296,7 @@
             pltpu.VMEM((ROWS, META), f32),
         ],
         weights,
+        LATE_LIMIT,
     )
 
 

time: 92.7 us -> 92.1 us (level)
  local copies, waits for them, and re-layouts: 3.93 us -> 0.9 us
  waiting for transfers between devices: 19.3 us -> 21.7 us
  Pallas kernels: 15.5 us -> 17.6 us
  blocking collectives: 28.6 us -> 27.2 us
    unnamed x4 -> x2, local copies, waits for them, and re-layouts: 3.04 us -> 0.01 us
    ppermute x9, waiting for transfers between devices: 9.81 us -> 12.2 us  [split_xor(): return lax.ppermute(array, ('x', 'y', 'c'), split_pairs(k, first))]
    pallas_call x2, Pallas kernels: 14.7 us -> 16.8 us  [head_call(): pl.pallas_call(kernel, grid=(TILES,), out_shape=[shape for shape, _ in ou...]
    all_to_all x1, blocking collectives: 12.9 us -> 11.3 us  [on_device(): sums = jnp.sum(lax.all_to_all(sums, DP, 0, 0, tiled=True), axis=0)]
  transfers between devices with their start and end apart: 12 -> 12, of which waited for: 7 -> 7; matrix products, arithmetic and copies ran while one was open for 3% -> 4% of each run, Pallas kernels for 7% -> 10%
where the time goes in v6:
time: 92.1 us; the launch traced here: 91.6 us
  blocking collectives  27.2 us (30%)
  waiting for transfers between devices  21.7 us (24%)
  starting transfers between devices  19.7 us (21%)
  Pallas kernels  17.6 us (19%)
  other arithmetic  2.45 us (3%)
  between operations  2.08 us (2%)
    pallas_call x2, Pallas kernels, head_call(): pl.pallas_call(kernel, grid=(TILES,), out_shape=[shape for shape, _ in ou...  16.8 us
    all_to_all x1, blocking collectives, on_device(): parts = lax.all_to_all(sums, VOCAB, 0, 0, tiled=True)  15.9 us
    ppermute x9, waiting for transfers between devices, split_xor(): return lax.ppermute(array, ('x', 'y', 'c'), split_pairs(k, first))  12.2 us
    all_to_all x1, blocking collectives, on_device(): sums = jnp.sum(lax.all_to_all(sums, DP, 0, 0, tiled=True), axis=0)  11.3 us
    ppermute x9, starting transfers between devices, split_xor(): return lax.ppermute(array, ('x', 'y', 'c'), split_pairs(k, first))  9.36 us
    all_to_all x1, waiting for transfers between devices, on_device(): pieces = lax.all_to_all(copies, VOCAB, 0, 0, tiled=True)  8.85 us
    all_to_all x1, starting transfers between devices, on_device(): pieces = lax.all_to_all(copies, VOCAB, 0, 0, tiled=True)  6.86 us
    ppermute x2, starting transfers between devices, swap_cores(): return lax.ppermute(array, 'c', [(0, 1), (1, 0)])  3.51 us
  transfers between devices with their start and end apart: 12, of which 7 were waited for; matrix products, arithmetic and copies ran while one was open for 4% of the time, Pallas kernels for 10%

profile of v6, /device:TPU:1, one launch (start us, length us, event | category | flops | bytes accessed | tf_op | source)
XLA Modules:
  0.0 91.6 jit_solution(17661968769977562820)
XLA Ops:
  0.6 3.3 %collective-permute-start = (bf16[1000,3584]{1,0:T(8,128)(2,1)}, bf16[1000,3584]{1,0:T(8,128)(2,1)}, u32[]{:S(2)}, u32[]{:S(2)}) collective-permute-start(bf16[1000,3584]{1,0:T(8,128)(2,1)} %wa.1), channel_id=1, source_target_pairs={{0,1},{1,0},{2,3},{3,2},{4,5},{5,4},{6,7},{7,6},{8,9},{9,8},{10,11... | collective-permute-start | bytes 21504008 | tf_op jit(solution)/shard_map/ppermute | solution.py:31
  4.0 1.6 %fusion = bf16[16,32,224]{2,1,0:T(8,128)(2,1)} fusion(s32[16]{0:T(128)S(1)} %get-tuple-element.37, s32[16]{0:T(128)S(1)} %get-tuple-element.38, pred[16]{0:T(512)(128)(4,1)S(1)} %compare_and_fusion, bf16[32,224]{1,0:T(8,128)(2,1)} %bitcast.16, bf16[32,224]{1,0:T(8,128)(2,1)} %bitcast.17), kind=kLoop, calls=%fused_computation.1 | loop fusion | flops 344064 | bytes 258192 | tf_op jit(solution)/shard_map/jit(_where)/select_n | solution.py:317
  5.5 6.9 %all-to-all-start = ((bf16[16,32,224]{2,1,0:T(8,128)(2,1)}), bf16[16,32,224]{2,1,0:T(8,128)(2,1)S(1)}, u32[]{:S(2)}, u32[]{:S(2)}) async-start(bf16[16,32,224]{2,1,0:T(8,128)(2,1)} %fusion), calls=%async_computation | async-start | bytes 524288 | tf_op jit(solution)/shard_map/all_to_all | solution.py:318
  12.4 0.2 collective-permute-start.1
  13.9 0.8 concatenate.30
  14.6 0.6 collective-permute-done.1
  15.2 8.9 %all-to-all-done.pieces = bf16[16,32,224]{2,1,0:T(8,128)(2,1)S(1)} async-done(((bf16[16,32,224]{2,1,0:T(8,128)(2,1)}), bf16[16,32,224]{2,1,0:T(8,128)(2,1)S(1)}, u32[]{:S(2)}, u32[]{:S(2)}) %all-to-all-start) | async-done | bytes 229408 | tf_op jit(solution)/shard_map/all_to_all | solution.py:318
  24.1 0.0 collective-permute-done.wb
  24.1 0.2 assemble.1
  24.2 1.4 %collective-permute-start.2 = (bf16[32,3712]{1,0:T(8,128)(2,1)S(1)}, bf16[32,3712]{1,0:T(8,128)(2,1)S(1)}, u32[]{:S(2)}, u32[]{:S(2)}) collective-permute-start(bf16[32,3712]{1,0:T(8,128)(2,1)S(1)} %assemble.1), channel_id=1, source_target_pairs={{0,64},{1,17},{16,80},{17,1},{32,96},{33,49},{48,112},{49,33},{64,... | collective-permute-start | bytes 712712 | tf_op jit(solution)/shard_map/ppermute | solution.py:44
  25.6 1.9 %collective-permute-start.3 = (bf16[32,3712]{1,0:T(8,128)(2,1)S(1)}, bf16[32,3712]{1,0:T(8,128)(2,1)S(1)}, u32[]{:S(2)}, u32[]{:S(2)}) collective-permute-start(bf16[32,3712]{1,0:T(8,128)(2,1)S(1)} %assemble.1), channel_id=1, source_target_pairs={{0,192},{1,49},{16,208},{17,33},{32,224},{33,17},{48,240},{49,1},{... | collective-permute-start | bytes 712712 | tf_op jit(solution)/shard_map/ppermute | solution.py:44
  27.5 0.7 collective-permute-start.4
  28.3 1.3 %collective-permute-done.2 = bf16[32,3712]{1,0:T(8,128)(2,1)S(1)} collective-permute-done((bf16[32,3712]{1,0:T(8,128)(2,1)S(1)}, bf16[32,3712]{1,0:T(8,128)(2,1)S(1)}, u32[]{:S(2)}, u32[]{:S(2)}) %collective-permute-start.2) | collective-permute-done | bytes 237600 | tf_op jit(solution)/shard_map/ppermute | solution.py:44
  29.6 3.5 %collective-permute-done.3 = bf16[32,3712]{1,0:T(8,128)(2,1)S(1)} collective-permute-done((bf16[32,3712]{1,0:T(8,128)(2,1)S(1)}, bf16[32,3712]{1,0:T(8,128)(2,1)S(1)}, u32[]{:S(2)}, u32[]{:S(2)}) %collective-permute-start.3) | collective-permute-done | bytes 237600 | tf_op jit(solution)/shard_map/ppermute | solution.py:44
  33.1 1.5 %collective-permute-done.4 = bf16[32,3712]{1,0:T(8,128)(2,1)S(1)} collective-permute-done((bf16[32,3712]{1,0:T(8,128)(2,1)S(1)}, bf16[32,3712]{1,0:T(8,128)(2,1)S(1)}, u32[]{:S(2)}, u32[]{:S(2)}) %collective-permute-start.4) | collective-permute-done | bytes 237600 | tf_op jit(solution)/shard_map/ppermute | solution.py:44
  34.6 0.1 pad_maximum_fusion.q1.m1
  34.6 2.3 %collective-permute-start.9 = (bf16[2,32,3712]{2,1,0:T(8,128)(2,1)S(1)}, bf16[2,32,3712]{2,1,0:T(8,128)(2,1)S(1)}, u32[]{:S(2)}, u32[]{:S(2)}) collective-permute-start(bf16[2,32,3712]{2,1,0:T(8,128)(2,1)S(1)} %pad_maximum_fusion.q1.m1), channel_id=1, source_target_pairs={{0,48},{1,193},{16,32},{17,209},{32,16},{33,225},{48,0},{49,241},{... | collective-permute-start | bytes 1425416 | tf_op jit(solution)/shard_map/ppermute | solution.py:44
  37.0 0.1 pad_maximum_fusion.1.q0.m0
  37.0 0.1 collective-permute-start.7
  37.2 1.4 %collective-permute-start.5 = (bf16[2,32,3712]{2,1,0:T(8,128)(2,1)S(1)}, bf16[2,32,3712]{2,1,0:T(8,128)(2,1)S(1)}, u32[]{:S(2)}, u32[]{:S(2)}) collective-permute-start(bf16[2,32,3712]{2,1,0:T(8,128)(2,1)S(1)} %pad_maximum_fusion.q1.m1), channel_id=1, source_target_pairs={{0,16},{1,65},{16,0},{17,81},{32,48},{33,97},{48,32},{49,113},{64,... | collective-permute-start | bytes 1425416 | tf_op jit(solution)/shard_map/ppermute | solution.py:44
  38.6 0.4 collective-permute-start.6
  39.0 4.7 %collective-permute-done.9.q3.m3 = bf16[2,32,3712]{2,1,0:T(8,128)(2,1)S(1)} collective-permute-done((bf16[2,32,3712]{2,1,0:T(8,128)(2,1)S(1)}, bf16[2,32,3712]{2,1,0:T(8,128)(2,1)S(1)}, u32[]{:S(2)}, u32[]{:S(2)}) %collective-permute-start.9) | collective-permute-done | bytes 475168 | tf_op jit(solution)/shard_map/ppermute | solution.py:44
  43.7 0.0 collective-permute-start.10
  43.7 1.2 %collective-permute-done.7.q2.m2 = bf16[2,32,3712]{2,1,0:T(8,128)(2,1)S(1)} collective-permute-done((bf16[2,32,3712]{2,1,0:T(8,128)(2,1)S(1)}, bf16[2,32,3712]{2,1,0:T(8,128)(2,1)S(1)}, u32[]{:S(2)}, u32[]{:S(2)}) %collective-permute-start.7) | collective-permute-done | bytes 475168 | tf_op jit(solution)/shard_map/ppermute | solution.py:44
  44.9 1.1 %collective-permute-start.8 = (bf16[2,32,3712]{2,1,0:T(8,128)(2,1)S(1)}, bf16[2,32,3712]{2,1,0:T(8,128)(2,1)}, u32[]{:S(2)}, u32[]{:S(2)}) collective-permute-start(bf16[2,32,3712]{2,1,0:T(8,128)(2,1)S(1)} %collective-permute-done.7.q2.m2), channel_id=1, source_target_pairs={{0,48},{1,193},{16,32},{17,209},{32,16},{33,225},{48,0},{49,241},{... | collective-permute-start | bytes 1425416 | tf_op jit(solution)/shard_map/ppermute | solution.py:44
  46.0 0.7 broadcast_select_fusion.1
  46.6 0.1 broadcast_select_fusion.2
  46.7 0.1 dynamic_update_slice.3.ref
  46.8 9.4 %early.1 = (f32[2,1024,256]{2,1,0:T(8,128)S(1)}, f32[1,256]{1,0:T(1,128)S(1)}, bf16[1000,3584]{1,0:T(8,128)(2,1)S(1)}, bf16[1000,3584]{1,0:T(8,128)(2,1)S(1)}) custom-call(bf16[2,32,3712]{2,1,0:T(8,128)(2,1)S(1)} %pad_maximum_fusion.1.q0.m0, bf16[2,32,3712]{2,1,0:T(8,128)(2,1)S(1)} %pad_maximum_fusion.q1.m1, ...), custom_call_target="tpu_custom_call" | custom-call | flops 3670016000 | bytes 16171008 | tf_op jit(solution)/shard_map/early/pallas_call | solution.py:238
  56.3 0.0 collective-permute-done.5.q0
  56.3 0.0 collective-permute-done.6.q1
  56.3 0.0 collective-permute-done.10.q3
  56.3 0.0 collective-permute-done.8.q2
  56.3 0.0 copy-start
  56.3 7.4 %late.1 = (f32[16,2,512]{2,1,0:T(2,128)S(1)}, f32[2,512]{1,0:T(2,128)S(1)}) custom-call(bf16[2,32,3712]{2,1,0:T(8,128)(2,1)S(1)} %collective-permute-done.5.q0, bf16[2,32,3712]{2,1,0:T(8,128)(2,1)S(1)} %collective-permute-done.6.q1, bf16[2,32,3712]{2,1,0:T(8,128)(2,1)} %collective-permute-done.8.q2, bf16[2,32,3712]{2,1,0:T(8,128)(2,1)S(1)} %collective-permute-done.10.q3, ...), custom_call_target="tpu_custom_call" | custom-call | flops 3670016000 | bytes 16171008 | tf_op jit(solution)/shard_map/late/pallas_call | solution.py:238
  63.7 11.3 %all_to_all.15 = f32[16,2,512]{2,1,0:T(2,128)S(1)} all-to-all(f32[16,2,512]{2,1,0:T(2,128)S(1)} %get-tuple-element.30), channel_id=1, replica_groups=mesh['x'=4,'y'=4,'z'=8,'c'=2] {'x','y'}, dimensions={0} | all-to-all | bytes 131072 | tf_op jit(solution)/shard_map/all_to_all | solution.py:352
  75.0 15.9 %all_to_all.16.parts = f32[16,4,512]{2,1,0:T(4,128)S(1)} all-to-all(f32[16,4,512]{2,1,0:T(4,128)S(1)} %broadcast_in_dim.44), channel_id=1, replica_groups=mesh['x'=4,'y'=4,'z'=8,'c'=2] {'z','c'}, dimensions={0} | all-to-all | bytes 262144 | tf_op jit(solution)/shard_map/all_to_all | solution.py:355
  91.0 0.0 copy-done
  91.0 0.6 losses.1
  (8 shorter events, 0.1 us)
Async XLA Ops:
  0.6 23.5 %collective-permute-start = (bf16[1000,3584]{1,0:T(8,128)(2,1)}, bf16[1000,3584]{1,0:T(8,128)(2,1)}, u32[]{:S(2)}, u32[]{:S(2)}) collective-permute-start(bf16[1000,3584]{1,0:T(8,128)(2,1)} %wa.1), channel_id=1, source_target_pairs={{0,1},{1,0},{2,3},{3,2},{4,5},{5,4},{6,7},{7,6},{8,9},{9,8},{10,11... | collective-permute-start | bytes 21504008 | tf_op jit(solution)/shard_map/ppermute | solution.py:31
  5.5 18.6 %all-to-all-start = ((bf16[16,32,224]{2,1,0:T(8,128)(2,1)}), bf16[16,32,224]{2,1,0:T(8,128)(2,1)S(1)}, u32[]{:S(2)}, u32[]{:S(2)}) async-start(bf16[16,32,224]{2,1,0:T(8,128)(2,1)} %fusion), calls=%async_computation | async-start | bytes 524288 | tf_op jit(solution)/shard_map/all_to_all | solution.py:318
  12.4 2.9 %collective-permute-start.1 = (f32[1,4]{1,0:T(1,128)}, f32[1,4]{1,0:T(1,128)S(1)}, u32[]{:S(2)}, u32[]{:S(2)}) collective-permute-start(f32[1,4]{1,0:T(1,128)} %ref.1), channel_id=1, source_target_pairs={{0,1},{1,0},{2,3},{3,2},{4,5},{5,4},{6,7},{7,6},{8,9},{9,8},{10,11... | collective-permute-start | bytes 56 | tf_op jit(solution)/shard_map/ppermute | solution.py:31
  24.2 5.3 %collective-permute-start.2 = (bf16[32,3712]{1,0:T(8,128)(2,1)S(1)}, bf16[32,3712]{1,0:T(8,128)(2,1)S(1)}, u32[]{:S(2)}, u32[]{:S(2)}) collective-permute-start(bf16[32,3712]{1,0:T(8,128)(2,1)S(1)} %assemble.1), channel_id=1, source_target_pairs={{0,64},{1,17},{16,80},{17,1},{32,96},{33,49},{48,112},{49,33},{64,... | collective-permute-start | bytes 712712 | tf_op jit(solution)/shard_map/ppermute | solution.py:44
  25.6 7.5 %collective-permute-start.3 = (bf16[32,3712]{1,0:T(8,128)(2,1)S(1)}, bf16[32,3712]{1,0:T(8,128)(2,1)S(1)}, u32[]{:S(2)}, u32[]{:S(2)}) collective-permute-start(bf16[32,3712]{1,0:T(8,128)(2,1)S(1)} %assemble.1), channel_id=1, source_target_pairs={{0,192},{1,49},{16,208},{17,33},{32,224},{33,17},{48,240},{49,1},{... | collective-permute-start | bytes 712712 | tf_op jit(solution)/shard_map/ppermute | solution.py:44
  27.5 7.1 %collective-permute-start.4 = (bf16[32,3712]{1,0:T(8,128)(2,1)S(1)}, bf16[32,3712]{1,0:T(8,128)(2,1)S(1)}, u32[]{:S(2)}, u32[]{:S(2)}) collective-permute-start(bf16[32,3712]{1,0:T(8,128)(2,1)S(1)} %assemble.1), channel_id=1, source_target_pairs={{0,128},{1,33},{16,144},{17,49},{32,160},{33,1},{48,176},{49,17},{... | collective-permute-start | bytes 712712 | tf_op jit(solution)/shard_map/ppermute | solution.py:44
  34.6 9.1 %collective-permute-start.9 = (bf16[2,32,3712]{2,1,0:T(8,128)(2,1)S(1)}, bf16[2,32,3712]{2,1,0:T(8,128)(2,1)S(1)}, u32[]{:S(2)}, u32[]{:S(2)}) collective-permute-start(bf16[2,32,3712]{2,1,0:T(8,128)(2,1)S(1)} %pad_maximum_fusion.q1.m1), channel_id=1, source_target_pairs={{0,48},{1,193},{16,32},{17,209},{32,16},{33,225},{48,0},{49,241},{... | collective-permute-start | bytes 1425416 | tf_op jit(solution)/shard_map/ppermute | solution.py:44
  37.0 7.9 %collective-permute-start.7 = (bf16[2,32,3712]{2,1,0:T(8,128)(2,1)S(1)}, bf16[2,32,3712]{2,1,0:T(8,128)(2,1)S(1)}, u32[]{:S(2)}, u32[]{:S(2)}) collective-permute-start(bf16[2,32,3712]{2,1,0:T(8,128)(2,1)S(1)} %pad_maximum_fusion.1.q0.m0), channel_id=1, source_target_pairs={{0,16},{1,65},{16,0},{17,81},{32,48},{33,97},{48,32},{49,113},{64,... | collective-permute-start | bytes 1425416 | tf_op jit(solution)/shard_map/ppermute | solution.py:44
  37.2 19.1 %collective-permute-start.5 = (bf16[2,32,3712]{2,1,0:T(8,128)(2,1)S(1)}, bf16[2,32,3712]{2,1,0:T(8,128)(2,1)S(1)}, u32[]{:S(2)}, u32[]{:S(2)}) collective-permute-start(bf16[2,32,3712]{2,1,0:T(8,128)(2,1)S(1)} %pad_maximum_fusion.q1.m1), channel_id=1, source_target_pairs={{0,16},{1,65},{16,0},{17,81},{32,48},{33,97},{48,32},{49,113},{64,... | collective-permute-start | bytes 1425416 | tf_op jit(solution)/shard_map/ppermute | solution.py:44
  38.6 17.7 %collective-permute-start.6 = (bf16[2,32,3712]{2,1,0:T(8,128)(2,1)S(1)}, bf16[2,32,3712]{2,1,0:T(8,128)(2,1)S(1)}, u32[]{:S(2)}, u32[]{:S(2)}) collective-permute-start(bf16[2,32,3712]{2,1,0:T(8,128)(2,1)S(1)} %pad_maximum_fusion.1.q0.m0), channel_id=1, source_target_pairs={{0,48},{1,193},{16,32},{17,209},{32,16},{33,225},{48,0},{49,241},{... | collective-permute-start | bytes 1425416 | tf_op jit(solution)/shard_map/ppermute | solution.py:44
  43.7 12.5 %collective-permute-start.10 = (bf16[2,32,3712]{2,1,0:T(8,128)(2,1)S(1)}, bf16[2,32,3712]{2,1,0:T(8,128)(2,1)S(1)}, u32[]{:S(2)}, u32[]{:S(2)}) collective-permute-start(bf16[2,32,3712]{2,1,0:T(8,128)(2,1)S(1)} %collective-permute-done.9.q3.m3), channel_id=1, source_target_pairs={{0,16},{1,65},{16,0},{17,81},{32,48},{33,97},{48,32},{49,113},{64,... | collective-permute-start | bytes 1425416 | tf_op jit(solution)/shard_map/ppermute | solution.py:44
  44.9 11.4 %collective-permute-start.8 = (bf16[2,32,3712]{2,1,0:T(8,128)(2,1)S(1)}, bf16[2,32,3712]{2,1,0:T(8,128)(2,1)}, u32[]{:S(2)}, u32[]{:S(2)}) collective-permute-start(bf16[2,32,3712]{2,1,0:T(8,128)(2,1)S(1)} %collective-permute-done.7.q2.m2), channel_id=1, source_target_pairs={{0,48},{1,193},{16,32},{17,209},{32,16},{33,225},{48,0},{49,241},{... | collective-permute-start | bytes 1425416 | tf_op jit(solution)/shard_map/ppermute | solution.py:44
  56.3 34.7 %copy-start = (f32[1,4]{1,0:T(1,128)S(1)}, f32[1,4]{1,0:T(1,128)}, u32[]{:S(2)}) copy-start(f32[1,4]{1,0:T(1,128)} %ref.1) | copy-start | bytes 52

commit v7 on v6

--- a/solution.py
+++ b/solution.py
@@ -20,7 +20,7 @@
 VOCAB_ROWS = 1000
 TILE = 256
 MIB = 1024 * 1024
-EARLY_LIMIT, LATE_LIMIT = 36, 24
+EARLY_LIMIT, LATE_LIMIT, STAGE_LIMIT = 30, 24, 44
 
 kto_beta = 0.1
 desirable_weight = 1.0
@@ -48,6 +48,10 @@
     return jnp.bitwise_xor(a, b)
 
 
+def stage_kernel(weight, out):
+    out[...] = weight[...]
+
+
 def seq_of(far, near):
     x, y, c = (lax.axis_index(a) for a in ("x", "y", "c"))
     u = jnp.where(c == 0, bit_xor(x, near), bit_xor(x, far))
@@ -104,7 +108,7 @@
     )
 
 
-def early_kernel(q0, q1, q2, q3, wa, wb, out, total, wa_out, wb_out, rows):
+def early_kernel(q0, q1, q2, q3, wa, wb, out, total, wb_out, rows):
     step = pl.program_id(0)
 
     @pl.when(step == 0)
@@ -113,7 +117,6 @@
         total[...] = jnp.zeros_like(total)
 
     valid = step * TILE + lax.broadcasted_iota(jnp.int32, (TILE, HALF), 0) < VOCAB_ROWS
-    wa_out[...] = wa[...]
     wb_out[...] = wb[...]
     for i, weight in enumerate((wa, wb)):
         logits = tile_logits(weight, rows)
@@ -233,6 +236,19 @@
     )(*arrays)
 
 
+def stage_call(weight):
+    tile = pl.BlockSpec((TILE, D), lambda i: (i, 0))
+    return pl.pallas_call(
+        stage_kernel,
+        grid=(TILES,),
+        out_shape=jax.ShapeDtypeStruct(weight.shape, weight.dtype),
+        in_specs=[tile],
+        out_specs=tile,
+        compiler_params=pltpu.CompilerParams(vmem_limit_bytes=STAGE_LIMIT * MIB),
+        name="stage",
+    )(weight)
+
+
 def head_call(kernel, name, outs, arrays, in_specs, scratch, weights, limit):
     tile = pl.BlockSpec((TILE, D), lambda i: (i, 0))
     return pl.pallas_call(
@@ -259,13 +275,12 @@
     held = pltpu.VMEM((HALF, D + META), jnp.bfloat16)
     weight = jax.ShapeDtypeStruct((VOCAB_ROWS, D), jnp.bfloat16)
     tile = pl.BlockSpec((TILE, D), lambda i: (i, 0))
-    logits, total, *weights = head_call(
+    logits, total, other_weight = head_call(
         early_kernel,
         "early",
         [
             (jax.ShapeDtypeStruct((NC, TILES * TILE, HALF), f32), tiles),
             (line, whole_block(line)),
-            (weight, tile),
             (weight, tile),
         ],
         early,
@@ -295,7 +310,7 @@
             pltpu.VMEM((META, ROWS), f32),
             pltpu.VMEM((ROWS, META), f32),
         ],
-        weights,
+        (weights[0], other_weight),
         LATE_LIMIT,
     )
 
@@ -312,12 +327,22 @@
         [labels[0], token_mask[0], kl_pair, desirable, jnp.zeros((META - 2 * LEN - 2,), jnp.int32)]
     ).astype(f32)[None]
 
+    pair_ref = jnp.concatenate(
+        [jnp.where(first, ref_logps, ref_came), jnp.where(first, ref_came, ref_logps)], axis=1
+    )
+    mine = (z // (NZ // 2)) == c
+    ref_rows = lax.dynamic_update_slice(
+        jnp.zeros((1, ROWS), f32),
+        jnp.where(mine, pair_ref, 0.0),
+        (0, seq * LEN + (z % (NZ // 2)) * 8),
+    )
+
     shape = (NZ * NC, *hidden.shape[1:])
     core = lax.broadcasted_iota(jnp.int32, shape, 0) % NC
     copies = jnp.where(core == 0, hidden, kl_hidden)
     pieces = lax.all_to_all(copies, VOCAB, 0, 0, tiled=True)
-    pieces, other_weight, ref_came, line = lax.optimization_barrier(
-        (pieces, other_weight, ref_came, line)
+    pieces, other_weight, ref_rows, line = lax.optimization_barrier(
+        (pieces, other_weight, ref_rows, line)
     )
     (rows,) = small_call(
         assemble_kernel,
@@ -327,26 +352,22 @@
         line,
     )
 
-    one, three, two = lax.optimization_barrier([split_xor(rows, k, True) for k in (1, 3, 2)])
+    two, three, one = lax.optimization_barrier([split_xor(rows, k, True) for k in (2, 3, 1)])
     groups = (jnp.stack([rows, one]), jnp.stack([two, three]))
+    *groups, weight = lax.optimization_barrier((*groups, head_weight))
+    staged = stage_call(weight)
     over_one = [split_xor(group, 1, False) for group in groups]
     over_three = [split_xor(group, 3, False) for group in groups]
+    over_one[0], over_three[1], staged = lax.optimization_barrier(
+        (over_one[0], over_three[1], staged)
+    )
     over_two = [split_xor(over_one[0], 3, False), split_xor(over_three[1], 1, False)]
 
-    pair_ref = jnp.concatenate(
-        [jnp.where(first, ref_logps, ref_came), jnp.where(first, ref_came, ref_logps)], axis=1
-    )
-    mine = (z // (NZ // 2)) == c
-    ref_rows = lax.dynamic_update_slice(
-        jnp.zeros((1, ROWS), f32),
-        jnp.where(mine, pair_ref, 0.0),
-        (0, seq * LEN + (z % (NZ // 2)) * 8),
-    )
     sums, stat = logit_sums(
         (*groups, over_one[0], over_three[1]),
         (over_one[1], over_three[0], *over_two),
         ref_rows,
-        (head_weight, other_weight),
+        (staged, other_weight),
     )
 
     sums = jnp.sum(lax.all_to_all(sums, DP, 0, 0, tiled=True), axis=0)

time: 92.1 us -> 89.1 us (0.967)
  waiting for transfers between devices: 21.7 us -> 17.4 us
  Pallas kernels: 17.6 us -> 18.8 us
    pallas_call x0 -> x1, Pallas kernels: none -> 4.15 us  [stage_call(): pl.pallas_call(stage_kernel, grid=(TILES,), out_shape=jax.ShapeDtypeStruc...]
    ppermute x9, waiting for transfers between devices: 12.2 us -> 8.8 us  [split_xor(): return lax.ppermute(array, ('x', 'y', 'c'), split_pairs(k, first))]
    pallas_call x2, Pallas kernels: 16.8 us -> 13.9 us  [head_call(): pl.pallas_call(kernel, grid=(TILES,), out_shape=[shape for shape, _ in ou...]
  transfers between devices with their start and end apart: 12 -> 12, of which waited for: 7 -> 7; matrix products, arithmetic and copies ran while one was open for 4% -> 4% of each run, Pallas kernels for 10% -> 13%
where the time goes in v7:
time: 89.1 us; the launch traced here: 88.5 us
  blocking collectives  27.1 us (30%)
  starting transfers between devices  19.9 us (22%)
  Pallas kernels  18.8 us (21%)
  waiting for transfers between devices  17.4 us (20%)
  other arithmetic  2.46 us (3%)
  between operations  2.04 us (2%)
  local copies, waits for them, and re-layouts  0.9 us (1%)
    all_to_all x1, blocking collectives, on_device(): parts = lax.all_to_all(sums, VOCAB, 0, 0, tiled=True)  15.5 us
    pallas_call x2, Pallas kernels, head_call(): pl.pallas_call(kernel, grid=(TILES,), out_shape=[shape for shape, _ in ou...  13.9 us
    all_to_all x1, blocking collectives, on_device(): sums = jnp.sum(lax.all_to_all(sums, DP, 0, 0, tiled=True), axis=0)  11.6 us
    ppermute x9, starting transfers between devices, split_xor(): return lax.ppermute(array, ('x', 'y', 'c'), split_pairs(k, first))  9.49 us
    ppermute x9, waiting for transfers between devices, split_xor(): return lax.ppermute(array, ('x', 'y', 'c'), split_pairs(k, first))  8.8 us
    all_to_all x1, waiting for transfers between devices, on_device(): pieces = lax.all_to_all(copies, VOCAB, 0, 0, tiled=True)  8.01 us
    all_to_all x1, starting transfers between devices, on_device(): pieces = lax.all_to_all(copies, VOCAB, 0, 0, tiled=True)  6.86 us
    pallas_call x1, Pallas kernels, stage_call(): pl.pallas_call(stage_kernel, grid=(TILES,), out_shape=jax.ShapeDtypeStruc...  4.15 us
  transfers between devices with their start and end apart: 12, of which 7 were waited for; matrix products, arithmetic and copies ran while one was open for 4% of the time, Pallas kernels for 13%

profile of v7, /device:TPU:1, one launch (start us, length us, event | category | flops | bytes accessed | tf_op | source)
XLA Modules:
  0.0 88.5 jit_solution(14772241374718085213)
XLA Ops:
  0.6 3.3 %collective-permute-start = (bf16[1000,3584]{1,0:T(8,128)(2,1)}, bf16[1000,3584]{1,0:T(8,128)(2,1)}, u32[]{:S(2)}, u32[]{:S(2)}) collective-permute-start(bf16[1000,3584]{1,0:T(8,128)(2,1)} %weight), channel_id=1, source_target_pairs={{0,1},{1,0},{2,3},{3,2},{4,5},{5,4},{6,7},{7,6},{8,9},{9,8},{10,11... | collective-permute-start | bytes 21504008 | tf_op jit(solution)/shard_map/ppermute | solution.py:31
  4.0 1.6 %fusion = bf16[16,32,224]{2,1,0:T(8,128)(2,1)} fusion(s32[16]{0:T(128)S(1)} %get-tuple-element.47, s32[16]{0:T(128)S(1)} %get-tuple-element.48, pred[16]{0:T(512)(128)(4,1)S(1)} %compare_and_fusion, bf16[32,224]{1,0:T(8,128)(2,1)} %bitcast.16, bf16[32,224]{1,0:T(8,128)(2,1)} %bitcast.17), kind=kLoop, calls=%fused_computation.1 | loop fusion | flops 344064 | bytes 258192 | tf_op jit(solution)/shard_map/jit(_where)/select_n | solution.py:342
  5.5 6.9 %all-to-all-start = ((bf16[16,32,224]{2,1,0:T(8,128)(2,1)}), bf16[16,32,224]{2,1,0:T(8,128)(2,1)S(1)}, u32[]{:S(2)}, u32[]{:S(2)}) async-start(bf16[16,32,224]{2,1,0:T(8,128)(2,1)} %fusion), calls=%async_computation | async-start | bytes 524288 | tf_op jit(solution)/shard_map/all_to_all | solution.py:343
  12.4 0.2 collective-permute-start.1
  13.9 0.8 concatenate.31
  14.6 0.6 collective-permute-done.1
  15.2 0.7 broadcast_select_fusion.1
  15.9 0.1 broadcast_select_fusion.2
  16.0 0.1 dynamic_update_slice.3.ref
  16.1 8.0 %all-to-all-done.pieces = bf16[16,32,224]{2,1,0:T(8,128)(2,1)S(1)} async-done(((bf16[16,32,224]{2,1,0:T(8,128)(2,1)}), bf16[16,32,224]{2,1,0:T(8,128)(2,1)S(1)}, u32[]{:S(2)}, u32[]{:S(2)}) %all-to-all-start) | async-done | bytes 229408 | tf_op jit(solution)/shard_map/all_to_all | solution.py:343
  24.1 0.0 collective-permute-done.wb
  24.1 0.2 assemble.1
  24.2 3.0 %collective-permute-start.2 = (bf16[32,3712]{1,0:T(8,128)(2,1)S(1)}, bf16[32,3712]{1,0:T(8,128)(2,1)S(1)}, u32[]{:S(2)}, u32[]{:S(2)}) collective-permute-start(bf16[32,3712]{1,0:T(8,128)(2,1)S(1)} %assemble.1), channel_id=1, source_target_pairs={{0,128},{1,33},{16,144},{17,49},{32,160},{33,1},{48,176},{49,17},{... | collective-permute-start | bytes 712712 | tf_op jit(solution)/shard_map/ppermute | solution.py:44
  27.2 0.8 collective-permute-start.3
  28.0 0.0 collective-permute-start.4
  28.0 3.1 %collective-permute-done.2 = bf16[32,3712]{1,0:T(8,128)(2,1)S(1)} collective-permute-done((bf16[32,3712]{1,0:T(8,128)(2,1)S(1)}, bf16[32,3712]{1,0:T(8,128)(2,1)S(1)}, u32[]{:S(2)}, u32[]{:S(2)}) %collective-permute-start.2) | collective-permute-done | bytes 237600 | tf_op jit(solution)/shard_map/ppermute | solution.py:44
  31.1 2.6 %collective-permute-done.3 = bf16[32,3712]{1,0:T(8,128)(2,1)S(1)} collective-permute-done((bf16[32,3712]{1,0:T(8,128)(2,1)S(1)}, bf16[32,3712]{1,0:T(8,128)(2,1)S(1)}, u32[]{:S(2)}, u32[]{:S(2)}) %collective-permute-start.3) | collective-permute-done | bytes 237600 | tf_op jit(solution)/shard_map/ppermute | solution.py:44
  33.7 0.1 collective-permute-done.4
  33.9 0.1 pad_maximum_fusion.1.q1.m1
  33.9 0.1 pad_maximum_fusion.q0.m0
  34.0 1.2 %collective-permute-start.7 = (bf16[2,32,3712]{2,1,0:T(8,128)(2,1)S(1)}, bf16[2,32,3712]{2,1,0:T(8,128)(2,1)S(1)}, u32[]{:S(2)}, u32[]{:S(2)}) collective-permute-start(bf16[2,32,3712]{2,1,0:T(8,128)(2,1)S(1)} %pad_maximum_fusion.q0.m0), channel_id=1, source_target_pairs={{0,16},{1,65},{16,0},{17,81},{32,48},{33,97},{48,32},{49,113},{64,... | collective-permute-start | bytes 1425416 | tf_op jit(solution)/shard_map/ppermute | solution.py:44
  35.2 1.8 %collective-permute-start.8 = (bf16[2,32,3712]{2,1,0:T(8,128)(2,1)S(1)}, bf16[2,32,3712]{2,1,0:T(8,128)(2,1)S(1)}, u32[]{:S(2)}, u32[]{:S(2)}) collective-permute-start(bf16[2,32,3712]{2,1,0:T(8,128)(2,1)S(1)} %pad_maximum_fusion.1.q1.m1), channel_id=1, source_target_pairs={{0,48},{1,193},{16,32},{17,209},{32,16},{33,225},{48,0},{49,241},{... | collective-permute-start | bytes 1425416 | tf_op jit(solution)/shard_map/ppermute | solution.py:44
  37.0 0.3 collective-permute-start.5
  37.3 0.6 collective-permute-start.6
  37.9 4.1 %stage.1.wa = bf16[1000,3584]{1,0:T(8,128)(2,1)S(1)} custom-call(bf16[1000,3584]{1,0:T(8,128)(2,1)} %weight), custom_call_target="tpu_custom_call" | custom-call | tf_op jit(solution)/shard_map/stage/pallas_call | solution.py:241
  42.0 0.0 collective-permute-done.7.q2.m2
  42.0 2.1 %collective-permute-done.8.q3.m3 = bf16[2,32,3712]{2,1,0:T(8,128)(2,1)S(1)} collective-permute-done((bf16[2,32,3712]{2,1,0:T(8,128)(2,1)S(1)}, bf16[2,32,3712]{2,1,0:T(8,128)(2,1)S(1)}, u32[]{:S(2)}, u32[]{:S(2)}) %collective-permute-start.8) | collective-permute-done | bytes 475168 | tf_op jit(solution)/shard_map/ppermute | solution.py:44
  44.2 0.0 collective-permute-start.10
  44.2 1.8 %collective-permute-start.9 = (bf16[2,32,3712]{2,1,0:T(8,128)(2,1)S(1)}, bf16[2,32,3712]{2,1,0:T(8,128)(2,1)S(1)}, u32[]{:S(2)}, u32[]{:S(2)}) collective-permute-start(bf16[2,32,3712]{2,1,0:T(8,128)(2,1)S(1)} %collective-permute-done.7.q2.m2), channel_id=1, source_target_pairs={{0,48},{1,193},{16,32},{17,209},{32,16},{33,225},{48,0},{49,241},{... | collective-permute-start | bytes 1425416 | tf_op jit(solution)/shard_map/ppermute | solution.py:44
  46.0 7.5 %early.1 = (f32[2,1024,256]{2,1,0:T(8,128)S(1)}, f32[1,256]{1,0:T(1,128)S(1)}, bf16[1000,3584]{1,0:T(8,128)(2,1)S(1)}) custom-call(bf16[2,32,3712]{2,1,0:T(8,128)(2,1)S(1)} %pad_maximum_fusion.q0.m0, bf16[2,32,3712]{2,1,0:T(8,128)(2,1)S(1)} %pad_maximum_fusion.1.q1.m1, bf16[2,32,3712]{2,1,0:T(8,128)(2,1)S(1)} %collective-permute-done.7.q2.m2, ...), custom_call_target="tpu_custom_call" | custom-call | flops 3670016000 | bytes 16171008 | tf_op jit(solution)/shard_map/early/pallas_call | solution.py:254
  53.5 0.0 collective-permute-done.5.q0
  53.5 0.0 collective-permute-done.6.q1
  53.5 0.0 collective-permute-done.10.q3
  53.5 0.8 collective-permute-done.9.q2
  54.4 0.0 copy-start
  54.4 6.4 %late.1 = (f32[16,2,512]{2,1,0:T(2,128)S(1)}, f32[2,512]{1,0:T(2,128)S(1)}) custom-call(bf16[2,32,3712]{2,1,0:T(8,128)(2,1)S(1)} %collective-permute-done.5.q0, bf16[2,32,3712]{2,1,0:T(8,128)(2,1)S(1)} %collective-permute-done.6.q1, bf16[2,32,3712]{2,1,0:T(8,128)(2,1)S(1)} %collective-permute-done.9.q2, bf16[2,32,3712]{2,1,0:T(8,128)(2,1)S(1)} %collective-permute-done.10.q3, ...), custom_call_target="tpu_custom_call" | custom-call | flops 3670016000 | bytes 16171008 | tf_op jit(solution)/shard_map/late/pallas_call | solution.py:254
  60.8 11.6 %all_to_all.15 = f32[16,2,512]{2,1,0:T(2,128)S(1)} all-to-all(f32[16,2,512]{2,1,0:T(2,128)S(1)} %get-tuple-element.40), channel_id=1, replica_groups=mesh['x'=4,'y'=4,'z'=8,'c'=2] {'x','y'}, dimensions={0} | all-to-all | bytes 131072 | tf_op jit(solution)/shard_map/all_to_all | solution.py:373
  72.4 15.5 %all_to_all.16.parts = f32[16,4,512]{2,1,0:T(4,128)S(1)} all-to-all(f32[16,4,512]{2,1,0:T(4,128)S(1)} %broadcast_in_dim.44), channel_id=1, replica_groups=mesh['x'=4,'y'=4,'z'=8,'c'=2] {'z','c'}, dimensions={0} | all-to-all | bytes 262144 | tf_op jit(solution)/shard_map/all_to_all | solution.py:376
  87.9 0.0 copy-done
  87.9 0.6 losses.1
  (8 shorter events, 0.1 us)
Async XLA Ops:
  0.6 23.5 %collective-permute-start = (bf16[1000,3584]{1,0:T(8,128)(2,1)}, bf16[1000,3584]{1,0:T(8,128)(2,1)}, u32[]{:S(2)}, u32[]{:S(2)}) collective-permute-start(bf16[1000,3584]{1,0:T(8,128)(2,1)} %weight), channel_id=1, source_target_pairs={{0,1},{1,0},{2,3},{3,2},{4,5},{5,4},{6,7},{7,6},{8,9},{9,8},{10,11... | collective-permute-start | bytes 21504008 | tf_op jit(solution)/shard_map/ppermute | solution.py:31
  5.5 18.6 %all-to-all-start = ((bf16[16,32,224]{2,1,0:T(8,128)(2,1)}), bf16[16,32,224]{2,1,0:T(8,128)(2,1)S(1)}, u32[]{:S(2)}, u32[]{:S(2)}) async-start(bf16[16,32,224]{2,1,0:T(8,128)(2,1)} %fusion), calls=%async_computation | async-start | bytes 524288 | tf_op jit(solution)/shard_map/all_to_all | solution.py:343
  12.4 2.9 %collective-permute-start.1 = (f32[1,4]{1,0:T(1,128)}, f32[1,4]{1,0:T(1,128)S(1)}, u32[]{:S(2)}, u32[]{:S(2)}) collective-permute-start(f32[1,4]{1,0:T(1,128)} %ref.1), channel_id=1, source_target_pairs={{0,1},{1,0},{2,3},{3,2},{4,5},{5,4},{6,7},{7,6},{8,9},{9,8},{10,11... | collective-permute-start | bytes 56 | tf_op jit(solution)/shard_map/ppermute | solution.py:31
  24.2 6.8 %collective-permute-start.2 = (bf16[32,3712]{1,0:T(8,128)(2,1)S(1)}, bf16[32,3712]{1,0:T(8,128)(2,1)S(1)}, u32[]{:S(2)}, u32[]{:S(2)}) collective-permute-start(bf16[32,3712]{1,0:T(8,128)(2,1)S(1)} %assemble.1), channel_id=1, source_target_pairs={{0,128},{1,33},{16,144},{17,49},{32,160},{33,1},{48,176},{49,17},{... | collective-permute-start | bytes 712712 | tf_op jit(solution)/shard_map/ppermute | solution.py:44
  27.2 6.5 %collective-permute-start.3 = (bf16[32,3712]{1,0:T(8,128)(2,1)S(1)}, bf16[32,3712]{1,0:T(8,128)(2,1)S(1)}, u32[]{:S(2)}, u32[]{:S(2)}) collective-permute-start(bf16[32,3712]{1,0:T(8,128)(2,1)S(1)} %assemble.1), channel_id=1, source_target_pairs={{0,192},{1,49},{16,208},{17,33},{32,224},{33,17},{48,240},{49,1},{... | collective-permute-start | bytes 712712 | tf_op jit(solution)/shard_map/ppermute | solution.py:44
  28.0 5.8 %collective-permute-start.4 = (bf16[32,3712]{1,0:T(8,128)(2,1)S(1)}, bf16[32,3712]{1,0:T(8,128)(2,1)S(1)}, u32[]{:S(2)}, u32[]{:S(2)}) collective-permute-start(bf16[32,3712]{1,0:T(8,128)(2,1)S(1)} %assemble.1), channel_id=1, source_target_pairs={{0,64},{1,17},{16,80},{17,1},{32,96},{33,49},{48,112},{49,33},{64,... | collective-permute-start | bytes 712712 | tf_op jit(solution)/shard_map/ppermute | solution.py:44
  34.0 8.1 %collective-permute-start.7 = (bf16[2,32,3712]{2,1,0:T(8,128)(2,1)S(1)}, bf16[2,32,3712]{2,1,0:T(8,128)(2,1)S(1)}, u32[]{:S(2)}, u32[]{:S(2)}) collective-permute-start(bf16[2,32,3712]{2,1,0:T(8,128)(2,1)S(1)} %pad_maximum_fusion.q0.m0), channel_id=1, source_target_pairs={{0,16},{1,65},{16,0},{17,81},{32,48},{33,97},{48,32},{49,113},{64,... | collective-permute-start | bytes 1425416 | tf_op jit(solution)/shard_map/ppermute | solution.py:44
  35.2 9.0 %collective-permute-start.8 = (bf16[2,32,3712]{2,1,0:T(8,128)(2,1)S(1)}, bf16[2,32,3712]{2,1,0:T(8,128)(2,1)S(1)}, u32[]{:S(2)}, u32[]{:S(2)}) collective-permute-start(bf16[2,32,3712]{2,1,0:T(8,128)(2,1)S(1)} %pad_maximum_fusion.1.q1.m1), channel_id=1, source_target_pairs={{0,48},{1,193},{16,32},{17,209},{32,16},{33,225},{48,0},{49,241},{... | collective-permute-start | bytes 1425416 | tf_op jit(solution)/shard_map/ppermute | solution.py:44
  37.0 16.5 %collective-permute-start.5 = (bf16[2,32,3712]{2,1,0:T(8,128)(2,1)S(1)}, bf16[2,32,3712]{2,1,0:T(8,128)(2,1)S(1)}, u32[]{:S(2)}, u32[]{:S(2)}) collective-permute-start(bf16[2,32,3712]{2,1,0:T(8,128)(2,1)S(1)} %pad_maximum_fusion.1.q1.m1), channel_id=1, source_target_pairs={{0,16},{1,65},{16,0},{17,81},{32,48},{33,97},{48,32},{49,113},{64,... | collective-permute-start | bytes 1425416 | tf_op jit(solution)/shard_map/ppermute | solution.py:44
  37.3 16.2 %collective-permute-start.6 = (bf16[2,32,3712]{2,1,0:T(8,128)(2,1)S(1)}, bf16[2,32,3712]{2,1,0:T(8,128)(2,1)S(1)}, u32[]{:S(2)}, u32[]{:S(2)}) collective-permute-start(bf16[2,32,3712]{2,1,0:T(8,128)(2,1)S(1)} %pad_maximum_fusion.q0.m0), channel_id=1, source_target_pairs={{0,48},{1,193},{16,32},{17,209},{32,16},{33,225},{48,0},{49,241},{... | collective-permute-start | bytes 1425416 | tf_op jit(solution)/shard_map/ppermute | solution.py:44
  44.2 9.3 %collective-permute-start.10 = (bf16[2,32,3712]{2,1,0:T(8,128)(2,1)S(1)}, bf16[2,32,3712]{2,1,0:T(8,128)(2,1)S(1)}, u32[]{:S(2)}, u32[]{:S(2)}) collective-permute-start(bf16[2,32,3712]{2,1,0:T(8,128)(2,1)S(1)} %collective-permute-done.8.q3.m3), channel_id=1, source_target_pairs={{0,16},{1,65},{16,0},{17,81},{32,48},{33,97},{48,32},{49,113},{64,... | collective-permute-start | bytes 1425416 | tf_op jit(solution)/shard_map/ppermute | solution.py:44
  44.2 10.2 %collective-permute-start.9 = (bf16[2,32,3712]{2,1,0:T(8,128)(2,1)S(1)}, bf16[2,32,3712]{2,1,0:T(8,128)(2,1)S(1)}, u32[]{:S(2)}, u32[]{:S(2)}) collective-permute-start(bf16[2,32,3712]{2,1,0:T(8,128)(2,1)S(1)} %collective-permute-done.7.q2.m2), channel_id=1, source_target_pairs={{0,48},{1,193},{16,32},{17,209},{32,16},{33,225},{48,0},{49,241},{... | collective-permute-start | bytes 1425416 | tf_op jit(solution)/shard_map/ppermute | solution.py:44
  54.4 33.5 %copy-start = (f32[1,4]{1,0:T(1,128)S(1)}, f32[1,4]{1,0:T(1,128)}, u32[]{:S(2)}) copy-start(f32[1,4]{1,0:T(1,128)} %ref.1) | copy-start | bytes 52

commit v8 on v7

--- a/solution.py
+++ b/solution.py
@@ -20,7 +20,7 @@
 VOCAB_ROWS = 1000
 TILE = 256
 MIB = 1024 * 1024
-EARLY_LIMIT, LATE_LIMIT, STAGE_LIMIT = 30, 24, 44
+EARLY_LIMIT, LATE_LIMIT, STAGE_LIMIT = 30, 30, 44
 
 kto_beta = 0.1
 desirable_weight = 1.0
@@ -122,6 +122,10 @@
         logits = tile_logits(weight, rows)
         out[i] = logits
         total[...] += jnp.sum(jnp.where(valid, jnp.exp(logits), 0.0), axis=0, keepdims=True)
+
+
+LATE_TILE = 512
+LATE_TILES = -(-VOCAB_ROWS // LATE_TILE)
 
 
 def late_kernel(q0, q1, q2, q3, m0, m1, m2, m3, total, logits_in, ref, wa, wb, *refs):
@@ -154,7 +158,7 @@
         sums[2:3] = moved[3:4]
         sums[3:4] = moved[5:6]
 
-    vocab = step * TILE + lax.broadcasted_iota(jnp.int32, (TILE, HALF), 0)
+    vocab = step * LATE_TILE + lax.broadcasted_iota(jnp.int32, (LATE_TILE, HALF), 0)
     valid = vocab < VOCAB_ROWS
     for i, (weight, core) in enumerate(((wa, c), (wb, 1 - c))):
         logits = tile_logits(weight, rows)
@@ -167,7 +171,7 @@
             at = slice(0, HALF) if values is not logits else slice(HALF, ROWS)
             sums[1:2, at] += jnp.sum(picked, axis=0, keepdims=True)
 
-    @pl.when(step == TILES - 1)
+    @pl.when(step == LATE_TILES - 1)
     def _():
         turned = jnp.transpose(sums[...])
         for i, (far, near) in enumerate(PLACES):
@@ -249,11 +253,11 @@
     )(weight)
 
 
-def head_call(kernel, name, outs, arrays, in_specs, scratch, weights, limit):
-    tile = pl.BlockSpec((TILE, D), lambda i: (i, 0))
+def head_call(kernel, name, outs, arrays, in_specs, scratch, weights, limit, rows_a_tile):
+    tile = pl.BlockSpec((rows_a_tile, D), lambda i: (i, 0))
     return pl.pallas_call(
         kernel,
-        grid=(TILES,),
+        grid=(-(-VOCAB_ROWS // rows_a_tile),),
         out_shape=[shape for shape, _ in outs],
         in_specs=[*in_specs, tile, tile],
         out_specs=[spec for _, spec in outs],
@@ -288,6 +292,7 @@
         [held],
         weights,
         EARLY_LIMIT,
+        TILE,
     )
     outs = [
         jax.ShapeDtypeStruct((SEQS, 2, ROWS), f32),
@@ -301,7 +306,11 @@
         (*late, *early, total, logits, ref),
         [whole_block(a) for a in late]
         + [meta] * len(early)
-        + [whole_block(total), tiles, whole_block(ref)],
+        + [
+            whole_block(total),
+            pl.BlockSpec((NC, LATE_TILE, HALF), lambda i: (0, i, 0)),
+            whole_block(ref),
+        ],
         [
             held,
             pltpu.VMEM((ROWS, META), jnp.bfloat16),
@@ -312,6 +321,7 @@
         ],
         (weights[0], other_weight),
         LATE_LIMIT,
+        LATE_TILE,
     )
 
 
@@ -356,8 +366,11 @@
     groups = (jnp.stack([rows, one]), jnp.stack([two, three]))
     *groups, weight = lax.optimization_barrier((*groups, head_weight))
     staged = stage_call(weight)
-    over_one = [split_xor(group, 1, False) for group in groups]
-    over_three = [split_xor(group, 3, False) for group in groups]
+    over_one = [split_xor(groups[0], 1, False)]
+    over_three = [None, split_xor(groups[1], 3, False)]
+    *later, staged = lax.optimization_barrier((*groups, staged))
+    over_one.append(split_xor(later[1], 1, False))
+    over_three[0] = split_xor(later[0], 3, False)
     over_one[0], over_three[1], staged = lax.optimization_barrier(
         (over_one[0], over_three[1], staged)
     )

time: 89.1 us -> 89 us (level)
  waiting for transfers between devices: 17.4 us -> 18.5 us
    ppermute x9, waiting for transfers between devices: 8.8 us -> 9.93 us  [split_xor(): return lax.ppermute(array, ('x', 'y', 'c'), split_pairs(k, first))]
    all_to_all x1, blocking collectives: 11.6 us -> 10.7 us  [on_device(): sums = jnp.sum(lax.all_to_all(sums, DP, 0, 0, tiled=True), axis=0)]
  transfers between devices with their start and end apart: 12 -> 12, of which waited for: 7 -> 8; matrix products, arithmetic and copies ran while one was open for 4% -> 4% of each run, Pallas kernels for 13% -> 13%
where the time goes in v8:
time: 89 us; the launch traced here: 88.5 us
  blocking collectives  26.3 us (30%)
  starting transfers between devices  20 us (22%)
  waiting for transfers between devices  18.5 us (21%)
  Pallas kernels  18.3 us (21%)
  other arithmetic  2.46 us (3%)
  between operations  2.02 us (2%)
  local copies, waits for them, and re-layouts  0.9 us (1%)
    all_to_all x1, blocking collectives, on_device(): parts = lax.all_to_all(sums, VOCAB, 0, 0, tiled=True)  15.6 us
    pallas_call x2, Pallas kernels, head_call(): pl.pallas_call(kernel, grid=(-(-VOCAB_ROWS // rows_a_tile),), out_shape=[...  13.4 us
    all_to_all x1, blocking collectives, on_device(): sums = jnp.sum(lax.all_to_all(sums, DP, 0, 0, tiled=True), axis=0)  10.7 us
    ppermute x9, waiting for transfers between devices, split_xor(): return lax.ppermute(array, ('x', 'y', 'c'), split_pairs(k, first))  9.93 us
    ppermute x9, starting transfers between devices, split_xor(): return lax.ppermute(array, ('x', 'y', 'c'), split_pairs(k, first))  9.63 us
    all_to_all x1, waiting for transfers between devices, on_device(): pieces = lax.all_to_all(copies, VOCAB, 0, 0, tiled=True)  8.01 us
    all_to_all x1, starting transfers between devices, on_device(): pieces = lax.all_to_all(copies, VOCAB, 0, 0, tiled=True)  6.86 us
    pallas_call x1, Pallas kernels, stage_call(): pl.pallas_call(stage_kernel, grid=(TILES,), out_shape=jax.ShapeDtypeStruc...  4.15 us
  transfers between devices with their start and end apart: 12, of which 8 were waited for; matrix products, arithmetic and copies ran while one was open for 4% of the time, Pallas kernels for 13%

profile of v8, /device:TPU:1, one launch (start us, length us, event | category | flops | bytes accessed | tf_op | source)
XLA Modules:
  0.0 88.5 jit_solution(14069397302755367147)
XLA Ops:
  0.6 3.3 %collective-permute-start = (bf16[1000,3584]{1,0:T(8,128)(2,1)}, bf16[1000,3584]{1,0:T(8,128)(2,1)}, u32[]{:S(2)}, u32[]{:S(2)}) collective-permute-start(bf16[1000,3584]{1,0:T(8,128)(2,1)} %weight), channel_id=1, source_target_pairs={{0,1},{1,0},{2,3},{3,2},{4,5},{5,4},{6,7},{7,6},{8,9},{9,8},{10,11... | collective-permute-start | bytes 21504008 | tf_op jit(solution)/shard_map/ppermute | solution.py:31
  4.0 1.6 %fusion = bf16[16,32,224]{2,1,0:T(8,128)(2,1)} fusion(s32[16]{0:T(128)S(1)} %get-tuple-element.53, s32[16]{0:T(128)S(1)} %get-tuple-element.54, pred[16]{0:T(512)(128)(4,1)S(1)} %compare_and_fusion, bf16[32,224]{1,0:T(8,128)(2,1)} %bitcast.16, bf16[32,224]{1,0:T(8,128)(2,1)} %bitcast.17), kind=kLoop, calls=%fused_computation.1 | loop fusion | flops 344064 | bytes 258192 | tf_op jit(solution)/shard_map/jit(_where)/select_n | solution.py:352
  5.5 6.9 %all-to-all-start = ((bf16[16,32,224]{2,1,0:T(8,128)(2,1)}), bf16[16,32,224]{2,1,0:T(8,128)(2,1)S(1)}, u32[]{:S(2)}, u32[]{:S(2)}) async-start(bf16[16,32,224]{2,1,0:T(8,128)(2,1)} %fusion), calls=%async_computation | async-start | bytes 524288 | tf_op jit(solution)/shard_map/all_to_all | solution.py:353
  12.4 0.2 collective-permute-start.1
  13.9 0.8 concatenate.31
  14.6 0.6 collective-permute-done.1
  15.2 0.7 broadcast_select_fusion.1
  15.9 0.1 broadcast_select_fusion.2
  16.0 0.1 dynamic_update_slice.3.ref
  16.1 8.0 %all-to-all-done.pieces = bf16[16,32,224]{2,1,0:T(8,128)(2,1)S(1)} async-done(((bf16[16,32,224]{2,1,0:T(8,128)(2,1)}), bf16[16,32,224]{2,1,0:T(8,128)(2,1)S(1)}, u32[]{:S(2)}, u32[]{:S(2)}) %all-to-all-start) | async-done | bytes 229408 | tf_op jit(solution)/shard_map/all_to_all | solution.py:353
  24.1 0.0 collective-permute-done.wb
  24.1 0.2 assemble.1
  24.2 3.0 %collective-permute-start.2 = (bf16[32,3712]{1,0:T(8,128)(2,1)S(1)}, bf16[32,3712]{1,0:T(8,128)(2,1)S(1)}, u32[]{:S(2)}, u32[]{:S(2)}) collective-permute-start(bf16[32,3712]{1,0:T(8,128)(2,1)S(1)} %assemble.1), channel_id=1, source_target_pairs={{0,128},{1,33},{16,144},{17,49},{32,160},{33,1},{48,176},{49,17},{... | collective-permute-start | bytes 712712 | tf_op jit(solution)/shard_map/ppermute | solution.py:44
  27.2 0.8 collective-permute-start.3
  28.0 0.0 collective-permute-start.4
  28.0 3.1 %collective-permute-done.2 = bf16[32,3712]{1,0:T(8,128)(2,1)S(1)} collective-permute-done((bf16[32,3712]{1,0:T(8,128)(2,1)S(1)}, bf16[32,3712]{1,0:T(8,128)(2,1)S(1)}, u32[]{:S(2)}, u32[]{:S(2)}) %collective-permute-start.2) | collective-permute-done | bytes 237600 | tf_op jit(solution)/shard_map/ppermute | solution.py:44
  31.1 2.6 %collective-permute-done.3 = bf16[32,3712]{1,0:T(8,128)(2,1)S(1)} collective-permute-done((bf16[32,3712]{1,0:T(8,128)(2,1)S(1)}, bf16[32,3712]{1,0:T(8,128)(2,1)S(1)}, u32[]{:S(2)}, u32[]{:S(2)}) %collective-permute-start.3) | collective-permute-done | bytes 237600 | tf_op jit(solution)/shard_map/ppermute | solution.py:44
  33.7 0.1 collective-permute-done.4
  33.9 0.1 pad_maximum_fusion.1.q1.m1
  33.9 0.1 pad_maximum_fusion.q0.m0
  34.0 1.2 %collective-permute-start.7 = (bf16[2,32,3712]{2,1,0:T(8,128)(2,1)S(1)}, bf16[2,32,3712]{2,1,0:T(8,128)(2,1)S(1)}, u32[]{:S(2)}, u32[]{:S(2)}) collective-permute-start(bf16[2,32,3712]{2,1,0:T(8,128)(2,1)S(1)} %pad_maximum_fusion.q0.m0), channel_id=1, source_target_pairs={{0,16},{1,65},{16,0},{17,81},{32,48},{33,97},{48,32},{49,113},{64,... | collective-permute-start | bytes 1425416 | tf_op jit(solution)/shard_map/ppermute | solution.py:44
  35.2 1.8 %collective-permute-start.8 = (bf16[2,32,3712]{2,1,0:T(8,128)(2,1)S(1)}, bf16[2,32,3712]{2,1,0:T(8,128)(2,1)S(1)}, u32[]{:S(2)}, u32[]{:S(2)}) collective-permute-start(bf16[2,32,3712]{2,1,0:T(8,128)(2,1)S(1)} %pad_maximum_fusion.1.q1.m1), channel_id=1, source_target_pairs={{0,48},{1,193},{16,32},{17,209},{32,16},{33,225},{48,0},{49,241},{... | collective-permute-start | bytes 1425416 | tf_op jit(solution)/shard_map/ppermute | solution.py:44
  37.0 4.1 %stage.1.wa = bf16[1000,3584]{1,0:T(8,128)(2,1)S(1)} custom-call(bf16[1000,3584]{1,0:T(8,128)(2,1)} %weight), custom_call_target="tpu_custom_call" | custom-call | tf_op jit(solution)/shard_map/stage/pallas_call | solution.py:245
  41.1 0.4 collective-permute-start.5
  41.5 0.7 collective-permute-start.6
  42.2 0.0 collective-permute-done.7.q2.m2
  42.2 2.0 %collective-permute-done.8.q3.m3 = bf16[2,32,3712]{2,1,0:T(8,128)(2,1)S(1)} collective-permute-done((bf16[2,32,3712]{2,1,0:T(8,128)(2,1)S(1)}, bf16[2,32,3712]{2,1,0:T(8,128)(2,1)S(1)}, u32[]{:S(2)}, u32[]{:S(2)}) %collective-permute-start.8) | collective-permute-done | bytes 475168 | tf_op jit(solution)/shard_map/ppermute | solution.py:44
  44.2 0.0 collective-permute-start.10
  44.2 1.8 %collective-permute-start.9 = (bf16[2,32,3712]{2,1,0:T(8,128)(2,1)S(1)}, bf16[2,32,3712]{2,1,0:T(8,128)(2,1)S(1)}, u32[]{:S(2)}, u32[]{:S(2)}) collective-permute-start(bf16[2,32,3712]{2,1,0:T(8,128)(2,1)S(1)} %collective-permute-done.7.q2.m2), channel_id=1, source_target_pairs={{0,48},{1,193},{16,32},{17,209},{32,16},{33,225},{48,0},{49,241},{... | collective-permute-start | bytes 1425416 | tf_op jit(solution)/shard_map/ppermute | solution.py:44
  46.0 7.5 %early.1 = (f32[2,1024,256]{2,1,0:T(8,128)S(1)}, f32[1,256]{1,0:T(1,128)S(1)}, bf16[1000,3584]{1,0:T(8,128)(2,1)S(1)}) custom-call(bf16[2,32,3712]{2,1,0:T(8,128)(2,1)S(1)} %pad_maximum_fusion.q0.m0, bf16[2,32,3712]{2,1,0:T(8,128)(2,1)S(1)} %pad_maximum_fusion.1.q1.m1, bf16[2,32,3712]{2,1,0:T(8,128)(2,1)S(1)} %collective-permute-done.7.q2.m2, ...), custom_call_target="tpu_custom_call" | custom-call | flops 3670016000 | bytes 16171008 | tf_op jit(solution)/shard_map/early/pallas_call | solution.py:258
  53.5 0.0 collective-permute-done.5.q0
  53.5 0.0 collective-permute-done.6.q1
  53.5 0.6 collective-permute-done.10.q3
  54.1 1.5 %collective-permute-done.9.q2 = bf16[2,32,3712]{2,1,0:T(8,128)(2,1)S(1)} collective-permute-done((bf16[2,32,3712]{2,1,0:T(8,128)(2,1)S(1)}, bf16[2,32,3712]{2,1,0:T(8,128)(2,1)S(1)}, u32[]{:S(2)}, u32[]{:S(2)}) %collective-permute-start.9) | collective-permute-done | bytes 475168 | tf_op jit(solution)/shard_map/ppermute | solution.py:44
  55.6 0.0 copy-start
  55.6 5.9 %late.1 = (f32[16,2,512]{2,1,0:T(2,128)S(1)}, f32[2,512]{1,0:T(2,128)S(1)}) custom-call(bf16[2,32,3712]{2,1,0:T(8,128)(2,1)S(1)} %collective-permute-done.5.q0, bf16[2,32,3712]{2,1,0:T(8,128)(2,1)S(1)} %collective-permute-done.6.q1, bf16[2,32,3712]{2,1,0:T(8,128)(2,1)S(1)} %collective-permute-done.9.q2, bf16[2,32,3712]{2,1,0:T(8,128)(2,1)S(1)} %collective-permute-done.10.q3, ...), custom_call_target="tpu_custom_call" | custom-call | flops 3670016000 | bytes 16171008 | tf_op jit(solution)/shard_map/late/pallas_call | solution.py:258
  61.5 10.7 %all_to_all.15 = f32[16,2,512]{2,1,0:T(2,128)S(1)} all-to-all(f32[16,2,512]{2,1,0:T(2,128)S(1)} %get-tuple-element.46), channel_id=1, replica_groups=mesh['x'=4,'y'=4,'z'=8,'c'=2] {'x','y'}, dimensions={0} | all-to-all | bytes 131072 | tf_op jit(solution)/shard_map/all_to_all | solution.py:386
  72.2 15.6 %all_to_all.16.parts = f32[16,4,512]{2,1,0:T(4,128)S(1)} all-to-all(f32[16,4,512]{2,1,0:T(4,128)S(1)} %broadcast_in_dim.44), channel_id=1, replica_groups=mesh['x'=4,'y'=4,'z'=8,'c'=2] {'z','c'}, dimensions={0} | all-to-all | bytes 262144 | tf_op jit(solution)/shard_map/all_to_all | solution.py:389
  87.8 0.0 copy-done
  87.8 0.6 losses.1
  (8 shorter events, 0.1 us)
Async XLA Ops:
  0.6 23.5 %collective-permute-start = (bf16[1000,3584]{1,0:T(8,128)(2,1)}, bf16[1000,3584]{1,0:T(8,128)(2,1)}, u32[]{:S(2)}, u32[]{:S(2)}) collective-permute-start(bf16[1000,3584]{1,0:T(8,128)(2,1)} %weight), channel_id=1, source_target_pairs={{0,1},{1,0},{2,3},{3,2},{4,5},{5,4},{6,7},{7,6},{8,9},{9,8},{10,11... | collective-permute-start | bytes 21504008 | tf_op jit(solution)/shard_map/ppermute | solution.py:31
  5.5 18.6 %all-to-all-start = ((bf16[16,32,224]{2,1,0:T(8,128)(2,1)}), bf16[16,32,224]{2,1,0:T(8,128)(2,1)S(1)}, u32[]{:S(2)}, u32[]{:S(2)}) async-start(bf16[16,32,224]{2,1,0:T(8,128)(2,1)} %fusion), calls=%async_computation | async-start | bytes 524288 | tf_op jit(solution)/shard_map/all_to_all | solution.py:353
  12.4 2.9 %collective-permute-start.1 = (f32[1,4]{1,0:T(1,128)}, f32[1,4]{1,0:T(1,128)S(1)}, u32[]{:S(2)}, u32[]{:S(2)}) collective-permute-start(f32[1,4]{1,0:T(1,128)} %ref.1), channel_id=1, source_target_pairs={{0,1},{1,0},{2,3},{3,2},{4,5},{5,4},{6,7},{7,6},{8,9},{9,8},{10,11... | collective-permute-start | bytes 56 | tf_op jit(solution)/shard_map/ppermute | solution.py:31
  24.2 6.8 %collective-permute-start.2 = (bf16[32,3712]{1,0:T(8,128)(2,1)S(1)}, bf16[32,3712]{1,0:T(8,128)(2,1)S(1)}, u32[]{:S(2)}, u32[]{:S(2)}) collective-permute-start(bf16[32,3712]{1,0:T(8,128)(2,1)S(1)} %assemble.1), channel_id=1, source_target_pairs={{0,128},{1,33},{16,144},{17,49},{32,160},{33,1},{48,176},{49,17},{... | collective-permute-start | bytes 712712 | tf_op jit(solution)/shard_map/ppermute | solution.py:44
  27.2 6.5 %collective-permute-start.3 = (bf16[32,3712]{1,0:T(8,128)(2,1)S(1)}, bf16[32,3712]{1,0:T(8,128)(2,1)S(1)}, u32[]{:S(2)}, u32[]{:S(2)}) collective-permute-start(bf16[32,3712]{1,0:T(8,128)(2,1)S(1)} %assemble.1), channel_id=1, source_target_pairs={{0,192},{1,49},{16,208},{17,33},{32,224},{33,17},{48,240},{49,1},{... | collective-permute-start | bytes 712712 | tf_op jit(solution)/shard_map/ppermute | solution.py:44
  28.0 5.8 %collective-permute-start.4 = (bf16[32,3712]{1,0:T(8,128)(2,1)S(1)}, bf16[32,3712]{1,0:T(8,128)(2,1)S(1)}, u32[]{:S(2)}, u32[]{:S(2)}) collective-permute-start(bf16[32,3712]{1,0:T(8,128)(2,1)S(1)} %assemble.1), channel_id=1, source_target_pairs={{0,64},{1,17},{16,80},{17,1},{32,96},{33,49},{48,112},{49,33},{64,... | collective-permute-start | bytes 712712 | tf_op jit(solution)/shard_map/ppermute | solution.py:44
  34.0 8.2 %collective-permute-start.7 = (bf16[2,32,3712]{2,1,0:T(8,128)(2,1)S(1)}, bf16[2,32,3712]{2,1,0:T(8,128)(2,1)S(1)}, u32[]{:S(2)}, u32[]{:S(2)}) collective-permute-start(bf16[2,32,3712]{2,1,0:T(8,128)(2,1)S(1)} %pad_maximum_fusion.q0.m0), channel_id=1, source_target_pairs={{0,16},{1,65},{16,0},{17,81},{32,48},{33,97},{48,32},{49,113},{64,... | collective-permute-start | bytes 1425416 | tf_op jit(solution)/shard_map/ppermute | solution.py:44
  35.2 9.0 %collective-permute-start.8 = (bf16[2,32,3712]{2,1,0:T(8,128)(2,1)S(1)}, bf16[2,32,3712]{2,1,0:T(8,128)(2,1)S(1)}, u32[]{:S(2)}, u32[]{:S(2)}) collective-permute-start(bf16[2,32,3712]{2,1,0:T(8,128)(2,1)S(1)} %pad_maximum_fusion.1.q1.m1), channel_id=1, source_target_pairs={{0,48},{1,193},{16,32},{17,209},{32,16},{33,225},{48,0},{49,241},{... | collective-permute-start | bytes 1425416 | tf_op jit(solution)/shard_map/ppermute | solution.py:44
  41.1 12.4 %collective-permute-start.5 = (bf16[2,32,3712]{2,1,0:T(8,128)(2,1)S(1)}, bf16[2,32,3712]{2,1,0:T(8,128)(2,1)S(1)}, u32[]{:S(2)}, u32[]{:S(2)}) collective-permute-start(bf16[2,32,3712]{2,1,0:T(8,128)(2,1)S(1)} %pad_maximum_fusion.1.q1.m1), channel_id=1, source_target_pairs={{0,16},{1,65},{16,0},{17,81},{32,48},{33,97},{48,32},{49,113},{64,... | collective-permute-start | bytes 1425416 | tf_op jit(solution)/shard_map/ppermute | solution.py:44
  41.5 12.0 %collective-permute-start.6 = (bf16[2,32,3712]{2,1,0:T(8,128)(2,1)S(1)}, bf16[2,32,3712]{2,1,0:T(8,128)(2,1)S(1)}, u32[]{:S(2)}, u32[]{:S(2)}) collective-permute-start(bf16[2,32,3712]{2,1,0:T(8,128)(2,1)S(1)} %pad_maximum_fusion.q0.m0), channel_id=1, source_target_pairs={{0,48},{1,193},{16,32},{17,209},{32,16},{33,225},{48,0},{49,241},{... | collective-permute-start | bytes 1425416 | tf_op jit(solution)/shard_map/ppermute | solution.py:44
  44.2 9.9 %collective-permute-start.10 = (bf16[2,32,3712]{2,1,0:T(8,128)(2,1)S(1)}, bf16[2,32,3712]{2,1,0:T(8,128)(2,1)S(1)}, u32[]{:S(2)}, u32[]{:S(2)}) collective-permute-start(bf16[2,32,3712]{2,1,0:T(8,128)(2,1)S(1)} %collective-permute-done.8.q3.m3), channel_id=1, source_target_pairs={{0,16},{1,65},{16,0},{17,81},{32,48},{33,97},{48,32},{49,113},{64,... | collective-permute-start | bytes 1425416 | tf_op jit(solution)/shard_map/ppermute | solution.py:44
  44.2 11.4 %collective-permute-start.9 = (bf16[2,32,3712]{2,1,0:T(8,128)(2,1)S(1)}, bf16[2,32,3712]{2,1,0:T(8,128)(2,1)S(1)}, u32[]{:S(2)}, u32[]{:S(2)}) collective-permute-start(bf16[2,32,3712]{2,1,0:T(8,128)(2,1)S(1)} %collective-permute-done.7.q2.m2), channel_id=1, source_target_pairs={{0,48},{1,193},{16,32},{17,209},{32,16},{33,225},{48,0},{49,241},{... | collective-permute-start | bytes 1425416 | tf_op jit(solution)/shard_map/ppermute | solution.py:44
  55.6 32.2 %copy-start = (f32[1,4]{1,0:T(1,128)S(1)}, f32[1,4]{1,0:T(1,128)}, u32[]{:S(2)}) copy-start(f32[1,4]{1,0:T(1,128)} %ref.1) | copy-start | bytes 52

commit v9 on v8

--- a/solution.py
+++ b/solution.py
@@ -366,11 +366,8 @@
     groups = (jnp.stack([rows, one]), jnp.stack([two, three]))
     *groups, weight = lax.optimization_barrier((*groups, head_weight))
     staged = stage_call(weight)
-    over_one = [split_xor(groups[0], 1, False)]
-    over_three = [None, split_xor(groups[1], 3, False)]
-    *later, staged = lax.optimization_barrier((*groups, staged))
-    over_one.append(split_xor(later[1], 1, False))
-    over_three[0] = split_xor(later[0], 3, False)
+    over_one = [split_xor(group, 1, False) for group in groups]
+    over_three = [split_xor(group, 3, False) for group in groups]
     over_one[0], over_three[1], staged = lax.optimization_barrier(
         (over_one[0], over_three[1], staged)
     )

time: 89 us -> 88.6 us (level)
  waiting for transfers between devices: 18.5 us -> 17.4 us
    ppermute x9, waiting for transfers between devices: 9.93 us -> 8.8 us  [split_xor(): return lax.ppermute(array, ('x', 'y', 'c'), split_pairs(k, first))]
    all_to_all x1, blocking collectives: 10.7 us -> 11.6 us  [on_device(): sums = jnp.sum(lax.all_to_all(sums, DP, 0, 0, tiled=True), axis=0)]
  transfers between devices with their start and end apart: 12 -> 12, of which waited for: 8 -> 7; matrix products, arithmetic and copies ran while one was open for 4% -> 4% of each run, Pallas kernels for 13% -> 13%
where the time goes in v9:
time: 88.6 us; the launch traced here: 88 us
  blocking collectives  27.1 us (31%)
  starting transfers between devices  19.9 us (22%)
  Pallas kernels  18.3 us (21%)
  waiting for transfers between devices  17.4 us (20%)
  other arithmetic  2.46 us (3%)
  between operations  2.04 us (2%)
  local copies, waits for them, and re-layouts  0.9 us (1%)
    all_to_all x1, blocking collectives, on_device(): parts = lax.all_to_all(sums, VOCAB, 0, 0, tiled=True)  15.5 us
    pallas_call x2, Pallas kernels, head_call(): pl.pallas_call(kernel, grid=(-(-VOCAB_ROWS // rows_a_tile),), out_shape=[...  13.4 us
    all_to_all x1, blocking collectives, on_device(): sums = jnp.sum(lax.all_to_all(sums, DP, 0, 0, tiled=True), axis=0)  11.6 us
    ppermute x9, starting transfers between devices, split_xor(): return lax.ppermute(array, ('x', 'y', 'c'), split_pairs(k, first))  9.49 us
    ppermute x9, waiting for transfers between devices, split_xor(): return lax.ppermute(array, ('x', 'y', 'c'), split_pairs(k, first))  8.8 us
    all_to_all x1, waiting for transfers between devices, on_device(): pieces = lax.all_to_all(copies, VOCAB, 0, 0, tiled=True)  8.01 us
    all_to_all x1, starting transfers between devices, on_device(): pieces = lax.all_to_all(copies, VOCAB, 0, 0, tiled=True)  6.86 us
    pallas_call x1, Pallas kernels, stage_call(): pl.pallas_call(stage_kernel, grid=(TILES,), out_shape=jax.ShapeDtypeStruc...  4.15 us
  transfers between devices with their start and end apart: 12, of which 7 were waited for; matrix products, arithmetic and copies ran while one was open for 4% of the time, Pallas kernels for 13%

profile of v9, /device:TPU:1, one launch (start us, length us, event | category | flops | bytes accessed | tf_op | source)
XLA Modules:
  0.0 88.0 jit_solution(3864012423277344119)
XLA Ops:
  0.6 3.3 %collective-permute-start = (bf16[1000,3584]{1,0:T(8,128)(2,1)}, bf16[1000,3584]{1,0:T(8,128)(2,1)}, u32[]{:S(2)}, u32[]{:S(2)}) collective-permute-start(bf16[1000,3584]{1,0:T(8,128)(2,1)} %weight), channel_id=1, source_target_pairs={{0,1},{1,0},{2,3},{3,2},{4,5},{5,4},{6,7},{7,6},{8,9},{9,8},{10,11... | collective-permute-start | bytes 21504008 | tf_op jit(solution)/shard_map/ppermute | solution.py:31
  4.0 1.6 %fusion = bf16[16,32,224]{2,1,0:T(8,128)(2,1)} fusion(s32[16]{0:T(128)S(1)} %get-tuple-element.47, s32[16]{0:T(128)S(1)} %get-tuple-element.48, pred[16]{0:T(512)(128)(4,1)S(1)} %compare_and_fusion, bf16[32,224]{1,0:T(8,128)(2,1)} %bitcast.16, bf16[32,224]{1,0:T(8,128)(2,1)} %bitcast.17), kind=kLoop, calls=%fused_computation.1 | loop fusion | flops 344064 | bytes 258192 | tf_op jit(solution)/shard_map/jit(_where)/select_n | solution.py:352
  5.5 6.9 %all-to-all-start = ((bf16[16,32,224]{2,1,0:T(8,128)(2,1)}), bf16[16,32,224]{2,1,0:T(8,128)(2,1)S(1)}, u32[]{:S(2)}, u32[]{:S(2)}) async-start(bf16[16,32,224]{2,1,0:T(8,128)(2,1)} %fusion), calls=%async_computation | async-start | bytes 524288 | tf_op jit(solution)/shard_map/all_to_all | solution.py:353
  12.4 0.2 collective-permute-start.1
  13.9 0.8 concatenate.31
  14.6 0.6 collective-permute-done.1
  15.2 0.7 broadcast_select_fusion.1
  15.9 0.1 broadcast_select_fusion.2
  16.0 0.1 dynamic_update_slice.3.ref
  16.1 8.0 %all-to-all-done.pieces = bf16[16,32,224]{2,1,0:T(8,128)(2,1)S(1)} async-done(((bf16[16,32,224]{2,1,0:T(8,128)(2,1)}), bf16[16,32,224]{2,1,0:T(8,128)(2,1)S(1)}, u32[]{:S(2)}, u32[]{:S(2)}) %all-to-all-start) | async-done | bytes 229408 | tf_op jit(solution)/shard_map/all_to_all | solution.py:353
  24.1 0.0 collective-permute-done.wb
  24.1 0.2 assemble.1
  24.2 3.0 %collective-permute-start.2 = (bf16[32,3712]{1,0:T(8,128)(2,1)S(1)}, bf16[32,3712]{1,0:T(8,128)(2,1)S(1)}, u32[]{:S(2)}, u32[]{:S(2)}) collective-permute-start(bf16[32,3712]{1,0:T(8,128)(2,1)S(1)} %assemble.1), channel_id=1, source_target_pairs={{0,128},{1,33},{16,144},{17,49},{32,160},{33,1},{48,176},{49,17},{... | collective-permute-start | bytes 712712 | tf_op jit(solution)/shard_map/ppermute | solution.py:44
  27.2 0.8 collective-permute-start.3
  28.0 0.0 collective-permute-start.4
  28.0 3.1 %collective-permute-done.2 = bf16[32,3712]{1,0:T(8,128)(2,1)S(1)} collective-permute-done((bf16[32,3712]{1,0:T(8,128)(2,1)S(1)}, bf16[32,3712]{1,0:T(8,128)(2,1)S(1)}, u32[]{:S(2)}, u32[]{:S(2)}) %collective-permute-start.2) | collective-permute-done | bytes 237600 | tf_op jit(solution)/shard_map/ppermute | solution.py:44
  31.1 2.6 %collective-permute-done.3 = bf16[32,3712]{1,0:T(8,128)(2,1)S(1)} collective-permute-done((bf16[32,3712]{1,0:T(8,128)(2,1)S(1)}, bf16[32,3712]{1,0:T(8,128)(2,1)S(1)}, u32[]{:S(2)}, u32[]{:S(2)}) %collective-permute-start.3) | collective-permute-done | bytes 237600 | tf_op jit(solution)/shard_map/ppermute | solution.py:44
  33.7 0.1 collective-permute-done.4
  33.9 0.1 pad_maximum_fusion.1.q1.m1
  33.9 0.1 pad_maximum_fusion.q0.m0
  34.0 1.2 %collective-permute-start.7 = (bf16[2,32,3712]{2,1,0:T(8,128)(2,1)S(1)}, bf16[2,32,3712]{2,1,0:T(8,128)(2,1)S(1)}, u32[]{:S(2)}, u32[]{:S(2)}) collective-permute-start(bf16[2,32,3712]{2,1,0:T(8,128)(2,1)S(1)} %pad_maximum_fusion.q0.m0), channel_id=1, source_target_pairs={{0,16},{1,65},{16,0},{17,81},{32,48},{33,97},{48,32},{49,113},{64,... | collective-permute-start | bytes 1425416 | tf_op jit(solution)/shard_map/ppermute | solution.py:44
  35.2 1.8 %collective-permute-start.8 = (bf16[2,32,3712]{2,1,0:T(8,128)(2,1)S(1)}, bf16[2,32,3712]{2,1,0:T(8,128)(2,1)S(1)}, u32[]{:S(2)}, u32[]{:S(2)}) collective-permute-start(bf16[2,32,3712]{2,1,0:T(8,128)(2,1)S(1)} %pad_maximum_fusion.1.q1.m1), channel_id=1, source_target_pairs={{0,48},{1,193},{16,32},{17,209},{32,16},{33,225},{48,0},{49,241},{... | collective-permute-start | bytes 1425416 | tf_op jit(solution)/shard_map/ppermute | solution.py:44
  37.0 0.3 collective-permute-start.5
  37.3 0.6 collective-permute-start.6
  37.9 4.1 %stage.1.wa = bf16[1000,3584]{1,0:T(8,128)(2,1)S(1)} custom-call(bf16[1000,3584]{1,0:T(8,128)(2,1)} %weight), custom_call_target="tpu_custom_call" | custom-call | tf_op jit(solution)/shard_map/stage/pallas_call | solution.py:245
  42.0 0.0 collective-permute-done.7.q2.m2
  42.0 2.1 %collective-permute-done.8.q3.m3 = bf16[2,32,3712]{2,1,0:T(8,128)(2,1)S(1)} collective-permute-done((bf16[2,32,3712]{2,1,0:T(8,128)(2,1)S(1)}, bf16[2,32,3712]{2,1,0:T(8,128)(2,1)S(1)}, u32[]{:S(2)}, u32[]{:S(2)}) %collective-permute-start.8) | collective-permute-done | bytes 475168 | tf_op jit(solution)/shard_map/ppermute | solution.py:44
  44.2 0.0 collective-permute-start.10
  44.2 1.8 %collective-permute-start.9 = (bf16[2,32,3712]{2,1,0:T(8,128)(2,1)S(1)}, bf16[2,32,3712]{2,1,0:T(8,128)(2,1)S(1)}, u32[]{:S(2)}, u32[]{:S(2)}) collective-permute-start(bf16[2,32,3712]{2,1,0:T(8,128)(2,1)S(1)} %collective-permute-done.7.q2.m2), channel_id=1, source_target_pairs={{0,48},{1,193},{16,32},{17,209},{32,16},{33,225},{48,0},{49,241},{... | collective-permute-start | bytes 1425416 | tf_op jit(solution)/shard_map/ppermute | solution.py:44
  46.0 7.5 %early.1 = (f32[2,1024,256]{2,1,0:T(8,128)S(1)}, f32[1,256]{1,0:T(1,128)S(1)}, bf16[1000,3584]{1,0:T(8,128)(2,1)S(1)}) custom-call(bf16[2,32,3712]{2,1,0:T(8,128)(2,1)S(1)} %pad_maximum_fusion.q0.m0, bf16[2,32,3712]{2,1,0:T(8,128)(2,1)S(1)} %pad_maximum_fusion.1.q1.m1, bf16[2,32,3712]{2,1,0:T(8,128)(2,1)S(1)} %collective-permute-done.7.q2.m2, ...), custom_call_target="tpu_custom_call" | custom-call | flops 3670016000 | bytes 16171008 | tf_op jit(solution)/shard_map/early/pallas_call | solution.py:258
  53.5 0.0 collective-permute-done.5.q0
  53.5 0.0 collective-permute-done.6.q1
  53.5 0.0 collective-permute-done.10.q3
  53.5 0.8 collective-permute-done.9.q2
  54.4 0.0 copy-start
  54.4 5.9 %late.1 = (f32[16,2,512]{2,1,0:T(2,128)S(1)}, f32[2,512]{1,0:T(2,128)S(1)}) custom-call(bf16[2,32,3712]{2,1,0:T(8,128)(2,1)S(1)} %collective-permute-done.5.q0, bf16[2,32,3712]{2,1,0:T(8,128)(2,1)S(1)} %collective-permute-done.6.q1, bf16[2,32,3712]{2,1,0:T(8,128)(2,1)S(1)} %collective-permute-done.9.q2, bf16[2,32,3712]{2,1,0:T(8,128)(2,1)S(1)} %collective-permute-done.10.q3, ...), custom_call_target="tpu_custom_call" | custom-call | flops 3670016000 | bytes 16171008 | tf_op jit(solution)/shard_map/late/pallas_call | solution.py:258
  60.2 11.6 %all_to_all.15 = f32[16,2,512]{2,1,0:T(2,128)S(1)} all-to-all(f32[16,2,512]{2,1,0:T(2,128)S(1)} %get-tuple-element.40), channel_id=1, replica_groups=mesh['x'=4,'y'=4,'z'=8,'c'=2] {'x','y'}, dimensions={0} | all-to-all | bytes 131072 | tf_op jit(solution)/shard_map/all_to_all | solution.py:383
  71.9 15.5 %all_to_all.16.parts = f32[16,4,512]{2,1,0:T(4,128)S(1)} all-to-all(f32[16,4,512]{2,1,0:T(4,128)S(1)} %broadcast_in_dim.44), channel_id=1, replica_groups=mesh['x'=4,'y'=4,'z'=8,'c'=2] {'z','c'}, dimensions={0} | all-to-all | bytes 262144 | tf_op jit(solution)/shard_map/all_to_all | solution.py:386
  87.4 0.0 copy-done
  87.4 0.6 losses.1
  (8 shorter events, 0.1 us)
Async XLA Ops:
  0.6 23.5 %collective-permute-start = (bf16[1000,3584]{1,0:T(8,128)(2,1)}, bf16[1000,3584]{1,0:T(8,128)(2,1)}, u32[]{:S(2)}, u32[]{:S(2)}) collective-permute-start(bf16[1000,3584]{1,0:T(8,128)(2,1)} %weight), channel_id=1, source_target_pairs={{0,1},{1,0},{2,3},{3,2},{4,5},{5,4},{6,7},{7,6},{8,9},{9,8},{10,11... | collective-permute-start | bytes 21504008 | tf_op jit(solution)/shard_map/ppermute | solution.py:31
  5.5 18.6 %all-to-all-start = ((bf16[16,32,224]{2,1,0:T(8,128)(2,1)}), bf16[16,32,224]{2,1,0:T(8,128)(2,1)S(1)}, u32[]{:S(2)}, u32[]{:S(2)}) async-start(bf16[16,32,224]{2,1,0:T(8,128)(2,1)} %fusion), calls=%async_computation | async-start | bytes 524288 | tf_op jit(solution)/shard_map/all_to_all | solution.py:353
  12.4 2.9 %collective-permute-start.1 = (f32[1,4]{1,0:T(1,128)}, f32[1,4]{1,0:T(1,128)S(1)}, u32[]{:S(2)}, u32[]{:S(2)}) collective-permute-start(f32[1,4]{1,0:T(1,128)} %ref.1), channel_id=1, source_target_pairs={{0,1},{1,0},{2,3},{3,2},{4,5},{5,4},{6,7},{7,6},{8,9},{9,8},{10,11... | collective-permute-start | bytes 56 | tf_op jit(solution)/shard_map/ppermute | solution.py:31
  24.2 6.8 %collective-permute-start.2 = (bf16[32,3712]{1,0:T(8,128)(2,1)S(1)}, bf16[32,3712]{1,0:T(8,128)(2,1)S(1)}, u32[]{:S(2)}, u32[]{:S(2)}) collective-permute-start(bf16[32,3712]{1,0:T(8,128)(2,1)S(1)} %assemble.1), channel_id=1, source_target_pairs={{0,128},{1,33},{16,144},{17,49},{32,160},{33,1},{48,176},{49,17},{... | collective-permute-start | bytes 712712 | tf_op jit(solution)/shard_map/ppermute | solution.py:44
  27.2 6.5 %collective-permute-start.3 = (bf16[32,3712]{1,0:T(8,128)(2,1)S(1)}, bf16[32,3712]{1,0:T(8,128)(2,1)S(1)}, u32[]{:S(2)}, u32[]{:S(2)}) collective-permute-start(bf16[32,3712]{1,0:T(8,128)(2,1)S(1)} %assemble.1), channel_id=1, source_target_pairs={{0,192},{1,49},{16,208},{17,33},{32,224},{33,17},{48,240},{49,1},{... | collective-permute-start | bytes 712712 | tf_op jit(solution)/shard_map/ppermute | solution.py:44
  28.0 5.8 %collective-permute-start.4 = (bf16[32,3712]{1,0:T(8,128)(2,1)S(1)}, bf16[32,3712]{1,0:T(8,128)(2,1)S(1)}, u32[]{:S(2)}, u32[]{:S(2)}) collective-permute-start(bf16[32,3712]{1,0:T(8,128)(2,1)S(1)} %assemble.1), channel_id=1, source_target_pairs={{0,64},{1,17},{16,80},{17,1},{32,96},{33,49},{48,112},{49,33},{64,... | collective-permute-start | bytes 712712 | tf_op jit(solution)/shard_map/ppermute | solution.py:44
  34.0 8.1 %collective-permute-start.7 = (bf16[2,32,3712]{2,1,0:T(8,128)(2,1)S(1)}, bf16[2,32,3712]{2,1,0:T(8,128)(2,1)S(1)}, u32[]{:S(2)}, u32[]{:S(2)}) collective-permute-start(bf16[2,32,3712]{2,1,0:T(8,128)(2,1)S(1)} %pad_maximum_fusion.q0.m0), channel_id=1, source_target_pairs={{0,16},{1,65},{16,0},{17,81},{32,48},{33,97},{48,32},{49,113},{64,... | collective-permute-start | bytes 1425416 | tf_op jit(solution)/shard_map/ppermute | solution.py:44
  35.2 9.0 %collective-permute-start.8 = (bf16[2,32,3712]{2,1,0:T(8,128)(2,1)S(1)}, bf16[2,32,3712]{2,1,0:T(8,128)(2,1)S(1)}, u32[]{:S(2)}, u32[]{:S(2)}) collective-permute-start(bf16[2,32,3712]{2,1,0:T(8,128)(2,1)S(1)} %pad_maximum_fusion.1.q1.m1), channel_id=1, source_target_pairs={{0,48},{1,193},{16,32},{17,209},{32,16},{33,225},{48,0},{49,241},{... | collective-permute-start | bytes 1425416 | tf_op jit(solution)/shard_map/ppermute | solution.py:44
  37.0 16.5 %collective-permute-start.5 = (bf16[2,32,3712]{2,1,0:T(8,128)(2,1)S(1)}, bf16[2,32,3712]{2,1,0:T(8,128)(2,1)S(1)}, u32[]{:S(2)}, u32[]{:S(2)}) collective-permute-start(bf16[2,32,3712]{2,1,0:T(8,128)(2,1)S(1)} %pad_maximum_fusion.1.q1.m1), channel_id=1, source_target_pairs={{0,16},{1,65},{16,0},{17,81},{32,48},{33,97},{48,32},{49,113},{64,... | collective-permute-start | bytes 1425416 | tf_op jit(solution)/shard_map/ppermute | solution.py:44
  37.3 16.2 %collective-permute-start.6 = (bf16[2,32,3712]{2,1,0:T(8,128)(2,1)S(1)}, bf16[2,32,3712]{2,1,0:T(8,128)(2,1)S(1)}, u32[]{:S(2)}, u32[]{:S(2)}) collective-permute-start(bf16[2,32,3712]{2,1,0:T(8,128)(2,1)S(1)} %pad_maximum_fusion.q0.m0), channel_id=1, source_target_pairs={{0,48},{1,193},{16,32},{17,209},{32,16},{33,225},{48,0},{49,241},{... | collective-permute-start | bytes 1425416 | tf_op jit(solution)/shard_map/ppermute | solution.py:44
  44.2 9.3 %collective-permute-start.10 = (bf16[2,32,3712]{2,1,0:T(8,128)(2,1)S(1)}, bf16[2,32,3712]{2,1,0:T(8,128)(2,1)S(1)}, u32[]{:S(2)}, u32[]{:S(2)}) collective-permute-start(bf16[2,32,3712]{2,1,0:T(8,128)(2,1)S(1)} %collective-permute-done.8.q3.m3), channel_id=1, source_target_pairs={{0,16},{1,65},{16,0},{17,81},{32,48},{33,97},{48,32},{49,113},{64,... | collective-permute-start | bytes 1425416 | tf_op jit(solution)/shard_map/ppermute | solution.py:44
  44.2 10.2 %collective-permute-start.9 = (bf16[2,32,3712]{2,1,0:T(8,128)(2,1)S(1)}, bf16[2,32,3712]{2,1,0:T(8,128)(2,1)S(1)}, u32[]{:S(2)}, u32[]{:S(2)}) collective-permute-start(bf16[2,32,3712]{2,1,0:T(8,128)(2,1)S(1)} %collective-permute-done.7.q2.m2), channel_id=1, source_target_pairs={{0,48},{1,193},{16,32},{17,209},{32,16},{33,225},{48,0},{49,241},{... | collective-permute-start | bytes 1425416 | tf_op jit(solution)/shard_map/ppermute | solution.py:44
  54.4 33.0 %copy-start = (f32[1,4]{1,0:T(1,128)S(1)}, f32[1,4]{1,0:T(1,128)}, u32[]{:S(2)}) copy-start(f32[1,4]{1,0:T(1,128)} %ref.1) | copy-start | bytes 52
